TPU v7x, 32 devices: a whole 2x2x4 slice. The times are simulated.
32 devices in a mesh: seq: 16 (over z, y, x), head: 2 (over core).
Axes of the slice: x: 2, y: 2, z: 4, core: 2. Of those that a mesh axis runs over, the one named last changes fastest.
Arguments:
- qk: bfloat16 [2, 8192, 128], P('head', 'seq'), may hold values from -32 to 32
- values: bfloat16 [2, 8192, 128], P('head', 'seq'), may hold values from -6 to 6
- grad_out: bfloat16 [2, 8192, 128], P('head', 'seq'), may hold values from -6 to 6
- members: int32 [2, 2, 48, 256], P('head'), may hold values from 0 to 8191, as said below
- counts: int32 [2, 2, 48], P('head'), may hold values from 1 to 256, as said below
Outputs:
- d_qk: bfloat16 [2, 8192, 128], P('head', 'seq')
- d_values: bfloat16 [2, 8192, 128], P('head', 'seq')
Inputs may be any that keep to these rules, and one draw needn't show every extreme that they name: `members`: for each head and round, every token index is in exactly one valid slot; the valid slots of a group are its first counts ones and hold increasing tokens, other slots hold any token. The 3 groups c with c // 3 equal hold at most 64 valid slots whose tokens t have one value of t // 512. For each head and round the counts sum to 8192.
All inputs are finite; a program needn't handle non-finite values.
Results may differ from a plain program's by a relative error of at most 0.012.
Values may be sent and summed in bfloat16 or wider, within the bound.
No kernel may reach another device: no remote copies, remote signals or barrier semaphores. Data moves between devices by JAX's collectives and lax.ppermute only.
A program may use at most 64 MiB of HBM per device.

v0:
```python
import functools

import jax
import jax.numpy as jnp
from jax import lax
from jax.experimental import pallas as pl
from jax.experimental.pallas import tpu as pltpu
from jax.sharding import PartitionSpec as P

masked_score = -1e30
norm_eps = 1e-06
lane = 128
f32 = jnp.float32
bf16 = jnp.bfloat16


def iota(shape, axis):
    return lax.broadcasted_iota(jnp.int32, shape, axis)


def float_iota(shape, axis):
    return iota(shape, axis).astype(f32)


def dot_nn(a, b):
    return lax.dot_general(a, b, (((1,), (0,)), ((), ())), preferred_element_type=f32)


def dot_nt(a, b):
    return lax.dot_general(a, b, (((1,), (1,)), ((), ())), preferred_element_type=f32)


def dot_tn(a, b):
    return lax.dot_general(a, b, (((0,), (0,)), ((), ())), preferred_element_type=f32)


def one_hot(condition):
    return jnp.where(condition, 1.0, 0.0).astype(bf16)


def earlier(size):
    return one_hot(iota((size, size), 0) < iota((size, size), 1))


def call(kernel, out_shapes, in_specs, scratch=()):
    return pl.pallas_call(
        kernel,
        out_shape=tuple(jax.ShapeDtypeStruct(shape, dtype) for shape, dtype in out_shapes),
        in_specs=in_specs,
        out_specs=tuple(pl.BlockSpec(memory_space=pltpu.VMEM) for _ in out_shapes),
        scratch_shapes=list(scratch),
        compiler_params=pltpu.CompilerParams(vmem_limit_bytes=50 * 1024 * 1024),
    )


def vmem(count):
    return [pl.BlockSpec(memory_space=pltpu.VMEM) for _ in range(count)]


def smem():
    return pl.BlockSpec(memory_space=pltpu.SMEM)


def pack_kernel(
    rounds, devices, bound, tokens_ref, q_ref, v_ref, g_ref, send_ref, pick_ref, key_ref, value_ref
):
    per_device, _, cap = tokens_ref.shape
    token_count = q_ref.shape[0]
    start = lax.axis_index("seq") * token_count
    before = earlier(cap)
    carry = jnp.zeros((rounds * devices, 1), f32)
    for group in range(per_device):
        local = tokens_ref[group] - start
        owned = (local >= 0) & (local < token_count)
        rank = dot_nn(one_hot(owned), before) + carry
        carry = carry + jnp.sum(jnp.where(owned, 1.0, 0.0), axis=1, keepdims=True)
        key_ref[group] = jnp.where(owned, rank, -1.0)
        value_ref[group] = jnp.where(owned, local + 1, 0).astype(f32)
    column = float_iota((bound, cap), 0)
    token = float_iota((bound, token_count), 1)

    def one_device(device, carried):
        for r in range(rounds):
            row = r * devices + device
            total = jnp.zeros((bound, cap), f32)
            for group in range(per_device):
                ranks = key_ref[group, pl.ds(row, 1), :]
                values = value_ref[group, pl.ds(row, 1), :]
                total = total + jnp.where(ranks == column, values, 0.0)
            index = jnp.sum(total, axis=1, keepdims=True) - 1.0
            at = pl.multiple_of((device * rounds + r) * bound, bound)
            pick_ref[pl.ds(at, bound), :] = one_hot(index == token)
        return carried

    lax.fori_loop(0, devices, one_device, 0, unroll=2)
    rows = jnp.concatenate([q_ref[...], v_ref[...], g_ref[...]], axis=1)
    total_rows = send_ref.shape[0]
    step = total_rows // 4
    for part in range(4):
        span = pl.ds(part * step, step)
        send_ref[span, :] = dot_nn(pick_ref[span, :], rows).astype(bf16)


def index_kernel(
    rounds,
    devices,
    bound,
    token_count,
    tokens_ref,
    spread_ref,
    spread_t_ref,
    partner_ref,
    low_ref,
    table_ref,
):
    per_device, _, cap = tokens_ref.shape
    me = lax.axis_index("seq")
    buffer_rows = devices * bound
    before = earlier(cap)
    source_start = iota((devices, cap), 0) * token_count
    source_place = float_iota((devices, cap), 0) * bound + 1.0
    place_column = float_iota((buffer_rows, cap), 0)
    place_lane = float_iota((cap, buffer_rows), 1)
    for r in range(rounds):
        carry = jnp.zeros((devices, 1), f32)
        for group in range(per_device):
            tokens = tokens_ref[group, pl.ds(r * devices + me, 1), :]
            owned = (tokens >= source_start) & (tokens < source_start + token_count)
            rank = dot_nn(one_hot(owned), before) + carry
            carry = carry + jnp.sum(jnp.where(owned, 1.0, 0.0), axis=1, keepdims=True)
            place = (
                jnp.sum(jnp.where(owned, rank + source_place, 0.0), axis=0, keepdims=True) - 1.0
            )
            span = pl.ds(group * cap, cap)
            spread_t_ref[r, :, span] = one_hot(place == place_column)
            upright = jnp.transpose(jnp.broadcast_to(place, (8, cap)))[:, :1]
            spread_ref[r, span, :] = one_hot(upright == place_lane)

    high_count = devices * token_count // lane
    high_start = iota((high_count, cap), 0) * lane
    low_index = iota((lane, cap), 0)
    slot = float_iota((high_count, cap), 1)

    def split(tokens):
        high = (tokens >= high_start) & (tokens < high_start + lane)
        low = jnp.bitwise_and(tokens, lane - 1) == low_index
        return high, low

    for r in range(rounds):

        def one_device(device, total):
            for group in range(per_device):
                tokens = tokens_ref[group, pl.ds(r * devices + device, 1), :]
                high, low = split(tokens)
                group_index = (device * per_device + group).astype(f32)
                sides = jnp.concatenate(
                    [
                        jnp.where(high, group_index, 0.0).astype(bf16),
                        jnp.where(high, slot, 0.0).astype(bf16),
                    ],
                    axis=0,
                )
                total = total + dot_nt(sides, one_hot(low))
            return total

        total = lax.fori_loop(
            0, devices, one_device, jnp.zeros((2 * high_count, lane), f32), unroll=2
        )
        table_ref[r] = total.astype(bf16)

    rows_per_device = 2 * rounds * per_device * cap // lane
    halves = cap // lane
    row_column = float_iota((devices * rows_per_device, cap), 0)
    for r in range(rounds):
        other = 1 - r
        for group in range(per_device):
            tokens = tokens_ref[group, pl.ds(r * devices + me, 1), :]
            high, low = split(tokens)
            high_hot = one_hot(high)
            found = []
            for part in range(2):
                table = table_ref[other, part * high_count : (part + 1) * high_count, :]
                picked = dot_tn(table, high_hot)
                found.append(jnp.sum(jnp.where(low, picked, 0.0), axis=0, keepdims=True))
            group_index, position = found
            device = jnp.floor((group_index + 0.5) * (1.0 / per_device))
            half = jnp.floor((position + 0.5) * (1.0 / lane))
            row = (
                device * rows_per_device
                + other * per_device * halves
                + (group_index - device * per_device) * halves
                + half
            )
            span = pl.ds(group * cap, cap)
            partner_ref[r, :, span] = one_hot(row == row_column)
            low_ref[pl.ds(r * per_device + group, 1), :] = position - half * lane


def last_kernel(rounds, devices, bound, got_ref, spread_ref, out_ref):
    features = out_ref.shape[2]
    for r in range(rounds):
        rows = got_ref[:, r * bound : (r + 1) * bound, :features].reshape(devices * bound, features)
        out_ref[r] = dot_nn(spread_ref[r], rows).astype(bf16)


def inverse_norm(rows):
    wide = rows.astype(f32)
    return lax.rsqrt(jnp.sum(wide * wide, axis=1, keepdims=True) + norm_eps)


def unit_rows(rows):
    return (rows.astype(f32) * inverse_norm(rows)).astype(bf16)


def forward(unit_before, unit_now, queries, value_before, value_now, cot, fill_before, fill_now):
    cap = queries.shape[0]
    key = iota((cap, cap), 0)
    score_before = jnp.where(key < fill_before, dot_nt(unit_before, queries), masked_score)
    allowed = (key < fill_now) & (key != iota((cap, cap), 1))
    score_now = jnp.where(allowed, dot_nt(unit_now, queries), masked_score)
    highest = jnp.maximum(
        jnp.max(score_before, axis=0, keepdims=True), jnp.max(score_now, axis=0, keepdims=True)
    )
    exp_before = jnp.exp(score_before - highest)
    exp_now = jnp.exp(score_now - highest)
    total = jnp.sum(exp_before, axis=0, keepdims=True) + jnp.sum(exp_now, axis=0, keepdims=True)
    inverse = 1.0 / total
    prob_before = exp_before * inverse
    prob_now = exp_now * inverse
    inner_before = dot_nt(value_before, cot)
    inner_now = dot_nt(value_now, cot)
    dots = jnp.sum(prob_before * inner_before, axis=0, keepdims=True) + jnp.sum(
        prob_now * inner_now, axis=0, keepdims=True
    )
    probs = (prob_before.astype(bf16), prob_now.astype(bf16))
    inners = (inner_before.astype(bf16), inner_now.astype(bf16))
    return highest + jnp.log(total), dots, probs, inners


def forward_inner_kernel(
    rounds, devices, bound, counts_ref, got_ref, spread_ref, rows_ref, prob_ref, inner_ref, sums_ref
):
    cap = prob_ref.shape[3]
    per_device = spread_ref.shape[1] // cap
    size = rows_ref.shape[3] // 3
    first = lax.axis_index("seq") * per_device
    for r in range(rounds):
        received = got_ref[:, r * bound : (r + 1) * bound, :].reshape(devices * bound, 3 * size)
        unpacked = dot_nn(spread_ref[r], received).astype(bf16)
        units = []
        for group in range(per_device):
            rows = unpacked[group * cap : (group + 1) * cap]
            rows_ref[r, group] = rows
            units.append(unit_rows(rows[:, :size]))
        for group in range(1, per_device):
            rows = unpacked[group * cap : (group + 1) * cap]
            behind = unpacked[(group - 1) * cap : group * cap]
            log_total, dots, probs, inners = forward(
                units[group - 1],
                units[group],
                rows[:, :size],
                behind[:, size : 2 * size],
                rows[:, size : 2 * size],
                rows[:, 2 * size :],
                counts_ref[r, first + group - 1],
                counts_ref[r, first + group],
            )
            for side in range(2):
                prob_ref[r, group - 1, side * cap : (side + 1) * cap, :] = probs[side]
                inner_ref[r, group - 1, side * cap : (side + 1) * cap, :] = inners[side]
            sums_ref[pl.ds(r * per_device + group, 1), :] = log_total
            sums_ref[pl.ds((rounds + r) * per_device + group, 1), :] = dots


def forward_first_kernel(
    rounds,
    devices,
    counts_ref,
    rows_ref,
    behind_ref,
    inner_sums_ref,
    prob_ref,
    inner_ref,
    sums_ref,
    send_ref,
):
    cap = prob_ref.shape[2]
    per_device = rows_ref.shape[1]
    size = rows_ref.shape[3] // 3
    groups = counts_ref.shape[1]
    first = lax.axis_index("seq") * per_device
    before = lax.rem(first + groups - 1, groups)
    sums_ref[...] = inner_sums_ref[...]
    for r in range(rounds):
        rows = rows_ref[r, 0]
        behind = behind_ref[r]
        log_total, dots, probs, inners = forward(
            unit_rows(behind[:, :size]),
            unit_rows(rows[:, :size]),
            rows[:, :size],
            behind[:, size:],
            rows[:, size : 2 * size],
            rows[:, 2 * size :],
            counts_ref[r, before],
            counts_ref[r, first],
        )
        for side in range(2):
            prob_ref[r, side * cap : (side + 1) * cap, :] = probs[side]
            inner_ref[r, side * cap : (side + 1) * cap, :] = inners[side]
        sums_ref[pl.ds(r * per_device, 1), :] = log_total
        sums_ref[pl.ds((rounds + r) * per_device, 1), :] = dots
    halves = cap // lane
    for row in range(2 * rounds * per_device):
        for half in range(halves):
            part = sums_ref[row : row + 1, half * lane : (half + 1) * lane]
            send_ref[:, row * halves + half : row * halves + half + 1, :] = jnp.broadcast_to(
                part[None], (devices, 1, lane)
            )


def backward(unit_before, unit_now, queries, cot, probs, inners, weight, mixture):
    cap = queries.shape[0]
    units = (unit_before, unit_now)
    query_grad = jnp.zeros((cap, queries.shape[1]), f32)
    unit_grads = []
    value_grads = []
    for side in range(2):
        weighted = probs[side].astype(f32) * weight
        score_grad = (weighted * (inners[side].astype(f32) - mixture)).astype(bf16)
        unit_grads.append(dot_nn(score_grad, queries))
        value_grads.append(dot_nn(weighted.astype(bf16), cot))
        query_grad = query_grad + dot_tn(score_grad, units[side])
    return query_grad, unit_grads, value_grads


def key_grad(rows, unit_grad):
    wide = rows.astype(f32)
    inverse = inverse_norm(rows)
    along = jnp.sum(wide * unit_grad, axis=1, keepdims=True)
    return inverse * unit_grad - wide * (inverse * inverse * inverse * along)


def three_parts(values):
    high = values.astype(bf16)
    rest = values - high.astype(f32)
    middle = rest.astype(bf16)
    return high, middle, (rest - middle.astype(f32)).astype(bf16)


def backward_first_kernel(
    rounds,
    counts_ref,
    everyone_ref,
    partner_ref,
    low_ref,
    sums_ref,
    rows_ref,
    behind_ref,
    prob_ref,
    inner_ref,
    edge_ref,
    query_ref,
    part_ref,
    scale_ref,
):
    cap = prob_ref.shape[2]
    per_device = rows_ref.shape[1]
    size = rows_ref.shape[3] // 3
    first = lax.axis_index("seq") * per_device
    table_rows = everyone_ref.shape[0]
    apart = rounds * per_device * cap // lane
    table = everyone_ref[...]
    both = jnp.concatenate([table, pltpu.roll(table, table_rows - apart, 0)], axis=1)
    upright = jnp.concatenate(three_parts(jnp.transpose(both)), axis=0)
    low_column = float_iota((lane, cap), 0)
    slot = iota((1, cap), 1)
    for r in range(rounds):
        picked = dot_nn(upright, partner_ref[r])
        picked = picked[: 2 * lane] + (picked[2 * lane : 4 * lane] + picked[4 * lane :])
        for group in range(per_device):
            at = r * per_device + group
            here = low_ref[at : at + 1, :] == low_column
            span = slice(group * cap, (group + 1) * cap)
            other_log = jnp.sum(jnp.where(here, picked[:lane, span], 0.0), axis=0, keepdims=True)
            other_dot = jnp.sum(jnp.where(here, picked[lane:, span], 0.0), axis=0, keepdims=True)
            own_log = sums_ref[at : at + 1, :]
            own_dot = sums_ref[rounds * per_device + at : rounds * per_device + at + 1, :]
            weight = 1.0 / (1.0 + jnp.exp(other_log - own_log))
            other_weight = 1.0 / (1.0 + jnp.exp(own_log - other_log))
            mixture = weight * own_dot + other_weight * other_dot
            valid = slot < counts_ref[r, first + group]
            scale_ref[at : at + 1, :] = jnp.where(valid, weight, 0.0)
            scale_ref[rounds * per_device + at : rounds * per_device + at + 1, :] = jnp.where(
                valid, mixture, 0.0
            )
    for r in range(rounds):
        rows = rows_ref[r, 0]
        at = r * per_device
        query_grad, unit_grads, value_grads = backward(
            unit_rows(behind_ref[r][:, :size]),
            unit_rows(rows[:, :size]),
            rows[:, :size],
            rows[:, 2 * size :],
            (prob_ref[r, :cap, :], prob_ref[r, cap:, :]),
            (inner_ref[r, :cap, :], inner_ref[r, cap:, :]),
            scale_ref[at : at + 1, :],
            scale_ref[rounds * per_device + at : rounds * per_device + at + 1, :],
        )
        edge_ref[r] = jnp.concatenate([unit_grads[0], value_grads[0]], axis=1).astype(bf16)
        query_ref[r] = query_grad
        part_ref[r] = jnp.concatenate([unit_grads[1], value_grads[1]], axis=1)


def backward_inner_kernel(
    rounds,
    rows_ref,
    prob_ref,
    inner_ref,
    scale_ref,
    query_ref,
    part_ref,
    done_ref,
    last_query_ref,
    last_part_ref,
):
    cap = prob_ref.shape[3]
    per_device = rows_ref.shape[1]
    size = rows_ref.shape[3] // 3
    for r in range(rounds):
        query_grad = query_ref[r]
        part = part_ref[r]
        for group in range(1, per_device):
            rows = rows_ref[r, group]
            behind = rows_ref[r, group - 1][:, :size]
            at = r * per_device + group
            next_query, unit_grads, value_grads = backward(
                unit_rows(behind),
                unit_rows(rows[:, :size]),
                rows[:, :size],
                rows[:, 2 * size :],
                (prob_ref[r, group - 1, :cap, :], prob_ref[r, group - 1, cap:, :]),
                (inner_ref[r, group - 1, :cap, :], inner_ref[r, group - 1, cap:, :]),
                scale_ref[at : at + 1, :],
                scale_ref[rounds * per_device + at : rounds * per_device + at + 1, :],
            )
            done = jnp.concatenate(
                [
                    query_grad + key_grad(behind, part[:, :size] + unit_grads[0]),
                    part[:, size:] + value_grads[0],
                ],
                axis=1,
            )
            done_ref[r, (group - 1) * cap : group * cap, :] = done.astype(bf16)
            query_grad = next_query
            part = jnp.concatenate([unit_grads[1], value_grads[1]], axis=1)
        last_query_ref[r] = query_grad
        last_part_ref[r] = part


def return_kernel(
    rounds,
    devices,
    bound,
    rows_ref,
    done_ref,
    query_ref,
    part_ref,
    edge_ref,
    spread_t_ref,
    send_ref,
):
    size = query_ref.shape[2]
    for r in range(rounds):
        total = part_ref[r] + edge_ref[r].astype(f32)
        last = jnp.concatenate(
            [query_ref[r] + key_grad(rows_ref[r, rows_ref.shape[1] - 1][:, :size], total[:, :size]), total[:, size:]],
            axis=1,
        ).astype(bf16)
        grads = jnp.concatenate([done_ref[r], last], axis=0)
        packed = dot_nn(spread_t_ref[r], grads).astype(bf16)
        send_ref[:, r * bound : (r + 1) * bound, :] = packed.reshape(devices, bound, 2 * size)


def home_kernel(pick_ref, got_ref, qk_ref, value_ref):
    size = qk_ref.shape[1]
    total = dot_tn(pick_ref[...], got_ref[...])
    qk_ref[...] = total[:, :size].astype(bf16)
    value_ref[...] = total[:, size:].astype(bf16)


def exchange(array):
    return lax.all_to_all(array, "seq", split_axis=0, concat_axis=0, tiled=True)


def shifted(array, by):
    devices = lax.axis_size("seq")
    return lax.ppermute(array, "seq", [(i, (i + by) % devices) for i in range(devices)])


def head_backward(qk, values, cot, members, counts):
    devices = lax.axis_size("seq")
    token_count, size = qk.shape
    rounds, groups, cap = members.shape
    per_device = groups // devices
    slots = per_device * cap
    bound = 2 * token_count // devices
    span = rounds * bound
    sum_rows = 2 * rounds * per_device
    table_rows = devices * sum_rows * cap // lane
    filled = jnp.arange(cap, dtype=jnp.int32) < counts[..., None]
    tokens = jnp.transpose(
        jnp.where(filled, members, -1).reshape(rounds * devices, per_device, cap), (1, 0, 2)
    )
    send, pick = call(
        functools.partial(pack_kernel, rounds, devices, bound),
        [((devices * span, 3 * size), bf16), ((devices * span, token_count), bf16)],
        vmem(4),
        [pltpu.VMEM((per_device, rounds * devices, cap), f32)] * 2,
    )(tokens, qk, values, cot)
    got = exchange(send).reshape(devices, span, 3 * size)
    spread, spread_t, partner, low = call(
        functools.partial(index_kernel, rounds, devices, bound, token_count),
        [
            ((rounds, slots, devices * bound), bf16),
            ((rounds, devices * bound, slots), bf16),
            ((rounds, table_rows, slots), bf16),
            ((rounds * per_device, cap), f32),
        ],
        vmem(1),
        [pltpu.VMEM((rounds, 2 * devices * token_count // lane, lane), bf16)],
    )(tokens)
    (last,) = call(
        functools.partial(last_kernel, rounds, devices, bound),
        [((rounds, cap, 2 * size), bf16)],
        vmem(2),
    )(got, spread[:, slots - cap :])
    behind = shifted(last, 1)
    rows, prob, inner, inner_sums = call(
        functools.partial(forward_inner_kernel, rounds, devices, bound),
        [
            ((rounds, per_device, cap, 3 * size), bf16),
            ((rounds, per_device - 1, 2 * cap, cap), bf16),
            ((rounds, per_device - 1, 2 * cap, cap), bf16),
            ((sum_rows, cap), f32),
        ],
        [smem()] + vmem(2),
    )(counts, got, spread)
    first_prob, first_inner, sums, sums_send = call(
        functools.partial(forward_first_kernel, rounds, devices),
        [
            ((rounds, 2 * cap, cap), bf16),
            ((rounds, 2 * cap, cap), bf16),
            ((sum_rows, cap), f32),
            ((devices, sum_rows * cap // lane, lane), f32),
        ],
        [smem()] + vmem(3),
    )(counts, rows, behind, inner_sums)
    everyone = exchange(sums_send.reshape(table_rows, lane))
    edge, query, part, scale = call(
        functools.partial(backward_first_kernel, rounds),
        [
            ((rounds, cap, 2 * size), bf16),
            ((rounds, cap, size), f32),
            ((rounds, cap, 2 * size), f32),
            ((sum_rows, cap), f32),
        ],
        [smem()] + vmem(8),
    )(counts, everyone, partner, low, sums, rows, behind, first_prob, first_inner)
    edge_in = shifted(edge, -1)
    done, last_query, last_part = call(
        functools.partial(backward_inner_kernel, rounds),
        [
            ((rounds, slots - cap, 2 * size), bf16),
            ((rounds, cap, size), f32),
            ((rounds, cap, 2 * size), f32),
        ],
        vmem(6),
    )(rows, prob, inner, scale, query, part)
    (grads_send,) = call(
        functools.partial(return_kernel, rounds, devices, bound),
        [((devices, span, 2 * size), bf16)],
        vmem(6),
    )(rows, done, last_query, last_part, edge_in, spread_t)
    home = exchange(grads_send.reshape(devices * span, 2 * size))
    return call(
        home_kernel, [((token_count, size), bf16), ((token_count, size), bf16)], vmem(2)
    )(pick, home)


def on_device(qk, values, grad_out, members, counts):
    grad_qk, grad_v = head_backward(qk[0], values[0], grad_out[0], members[0], counts[0])
    return (grad_qk[None], grad_v[None])


def solution(mesh):
    in_specs = (
        P("head", "seq", None),
        P("head", "seq", None),
        P("head", "seq", None),
        P("head", None, None, None),
        P("head", None, None),
    )
    out_specs = (P("head", "seq", None), P("head", "seq", None))
    return jax.shard_map(
        on_device, mesh=mesh, in_specs=in_specs, out_specs=out_specs, check_vma=False
    )
```

profile of v0, /device:TPU:0, one launch (start us, length us, event | category | flops | bytes accessed | tf_op | source)
XLA Modules:
  0.0 120.6 jit_solution(434996900740684228)
XLA Ops:
  0.6 0.8 lt.17
  1.4 0.1 copy.8
  1.5 0.9 squeeze.15
  2.4 0.1 fusion.tokens_ref
  2.5 0.0 copy-start.7
  2.5 0.9 copy-done.7
  3.4 0.0 copy-start.8
  3.4 0.9 copy-done.8
  4.3 0.0 copy-start.9
  4.3 0.9 copy-done.9
  5.2 4.3 %shard_map.68 = (bf16[2048,384]{1,0:T(8,128)(2,1)}, bf16[2048,512]{1,0:T(8,128)(2,1)}) custom-call(s32[3,32,256]{2,1,0:T(8,128)S(1)} %fusion.tokens_ref, bf16[512,128]{1,0:T(8,128)(2,1)S(1)} %bitcast.15, bf16[512,128]{1,0:T(8,128)(2,1)S(1)} %bitcast.16, bf16[512,128]{1,0:T(8,128)(2,1)S(1)} %bitcast.17), custom_call_target="tpu_custom_call" | custom-call | tf_op jit(solution)/shard_map/pallas_call | solution.py:514
  9.5 8.3 %all-to-all-start = ((bf16[16,128,384]{2,1,0:T(8,128)(2,1)}), bf16[16,128,384]{2,1,0:T(8,128)(2,1)S(1)}, u32[]{:S(2)}, u32[]{:S(2)}) async-start(bf16[16,128,384]{2,1,0:T(8,128)(2,1)} %bitcast.5), calls=%async_computation | async-start | bytes 3145728 | tf_op jit(solution)/shard_map/all_to_all | solution.py:492
  17.8 9.5 %shard_map.69 = (bf16[2,768,1024]{2,1,0:T(8,128)(2,1)}, bf16[2,1024,768]{2,1,0:T(8,128)(2,1)}, bf16[2,384,768]{2,1,0:T(8,128)(2,1)S(1)}, f32[6,256]{1,0:T(8,128)S(1)}) custom-call(s32[3,32,256]{2,1,0:T(8,128)S(1)} %fusion.tokens_ref), custom_call_target="tpu_custom_call" | custom-call | tf_op jit(solution)/shard_map/pallas_call | solution.py:521
  27.3 0.0 copy-start.4
  27.3 1.0 copy-done.4
  28.4 1.3 %slice.3.spread_ref = bf16[2,256,1024]{2,1,0:T(8,128)(2,1)S(1)} slice(bf16[2,768,1024]{2,1,0:T(8,128)(2,1)} %get-tuple-element.27.spread_ref), slice={[0:2], [512:768], [0:1024]} | slice | bytes 2097152 | tf_op jit(solution)/shard_map/slice | solution.py:536
  29.7 0.0 copy-start.10
  29.7 22.3 %all-to-all-done.got_ref = bf16[16,128,384]{2,1,0:T(8,128)(2,1)S(1)} async-done(((bf16[16,128,384]{2,1,0:T(8,128)(2,1)}), bf16[16,128,384]{2,1,0:T(8,128)(2,1)S(1)}, u32[]{:S(2)}, u32[]{:S(2)}) %all-to-all-start) | async-done | bytes 1572896 | tf_op jit(solution)/shard_map/all_to_all | solution.py:492
  52.0 0.0 copy-start.2
  52.0 0.4 shard_map.71
  52.5 1.0 collective-permute-start
  53.4 0.0 copy-done.2
  53.4 0.0 copy-done.10
  53.4 5.3 %shard_map.70 = (bf16[2,3,256,384]{3,2,1,0:T(8,128)(2,1)S(1)}, bf16[2,2,512,256]{3,2,1,0:T(8,128)(2,1)S(1)}, bf16[2,2,512,256]{3,2,1,0:T(8,128)(2,1)S(1)}, f32[12,256]{1,0:T(8,128)S(1)}) custom-call(s32[2,48]{1,0:T(2,128)S(1)} %bitcast.18, bf16[16,128,384]{2,1,0:T(8,128)(2,1)} %copy-done.2, bf16[2,768,1024]{2,1,0:T(8,128)(2,1)} %get-tuple-element.27.spread_ref), custom_call_target="tpu_custom_call" | custom-call | tf_op jit(solution)/shard_map/pallas_call | solution.py:538
  58.8 0.0 copy-start.6
  58.8 1.0 copy-done.6
  59.7 0.0 copy-start
  59.7 0.0 copy-start.5
  59.7 3.9 %collective-permute-done.behind_ref = bf16[2,256,256]{2,1,0:T(8,128)(2,1)S(1)} collective-permute-done((bf16[2,256,256]{2,1,0:T(8,128)(2,1)S(1)}, bf16[2,256,256]{2,1,0:T(8,128)(2,1)S(1)}, u32[]{:S(2)}, u32[]{:S(2)}) %collective-permute-start) | collective-permute-done | bytes 262176 | tf_op jit(solution)/shard_map/ppermute | solution.py:497
  63.6 1.5 %shard_map.72 = (bf16[2,512,256]{2,1,0:T(8,128)(2,1)S(1)}, bf16[2,512,256]{2,1,0:T(8,128)(2,1)S(1)}, f32[12,256]{1,0:T(8,128)S(1)}, f32[16,24,128]{2,1,0:T(8,128)S(1)}) custom-call(s32[2,48]{1,0:T(2,128)S(1)} %bitcast.19, bf16[2,3,256,384]{3,2,1,0:T(8,128)(2,1)S(1)} %get-tuple-element.28.rows_ref, bf16[2,256,256]{2,1,0:T(8,128)(2,1)S(1)} %collective-permute-done.behind_ref, ...), custom_call_target="tpu_custom_call" | custom-call | tf_op jit(solution)/shard_map/pallas_call | solution.py:548
  65.1 12.2 %all_to_all.25 = f32[16,24,128]{2,1,0:T(8,128)S(1)} all-to-all(f32[16,24,128]{2,1,0:T(8,128)S(1)} %get-tuple-element.32), channel_id=1, replica_groups=mesh['seq'=16,'head'=2] {'seq'}, dimensions={0} | all-to-all | bytes 393216 | tf_op jit(solution)/shard_map/all_to_all | solution.py:492
  77.3 0.0 copy-done
  77.3 0.0 copy-done.5
  77.3 3.2 %shard_map.73 = (bf16[2,256,256]{2,1,0:T(8,128)(2,1)S(1)}, f32[2,256,128]{2,1,0:T(8,128)S(1)}, f32[2,256,256]{2,1,0:T(8,128)S(1)}, f32[12,256]{1,0:T(8,128)S(1)}) custom-call(s32[2,48]{1,0:T(2,128)S(1)} %bitcast.20, f32[384,128]{1,0:T(8,128)S(1)} %bitcast.14, bf16[2,384,768]{2,1,0:T(8,128)(2,1)S(1)} %copy-done.5, f32[6,256]{1,0:T(8,128)S(1)} %get-tuple-element.34.low_ref, ...), custom_call_target="tpu_custom_call" | custom-call | tf_op jit(solution)/shard_map/pallas_call | solution.py:559
  80.5 2.0 %collective-permute-start.1 = (bf16[2,256,256]{2,1,0:T(8,128)(2,1)S(1)}, bf16[2,256,256]{2,1,0:T(8,128)(2,1)S(1)}, u32[]{:S(2)}, u32[]{:S(2)}) collective-permute-start(bf16[2,256,256]{2,1,0:T(8,128)(2,1)S(1)} %get-tuple-element.44), channel_id=1, source_target_pairs={{0,30},{2,0},{4,2},{6,4},{8,6},{10,8},{12,10},{14,12},{16,14},{18,... | collective-permute-start | bytes 786440 | tf_op jit(solution)/shard_map/ppermute | solution.py:497
  82.4 0.0 copy-start.1
  82.4 2.9 %shard_map.74 = (bf16[2,512,256]{2,1,0:T(8,128)(2,1)S(1)}, f32[2,256,128]{2,1,0:T(8,128)S(1)}, f32[2,256,256]{2,1,0:T(8,128)S(1)}) custom-call(bf16[2,3,256,384]{3,2,1,0:T(8,128)(2,1)} %copy-done, bf16[2,2,512,256]{3,2,1,0:T(8,128)(2,1)S(1)} %get-tuple-element.29.prob_ref, bf16[2,2,512,256]{3,2,1,0:T(8,128)(2,1)} %copy-done.6, ...), custom_call_target="tpu_custom_call" | custom-call | tf_op jit(solution)/shard_map/pallas_call | solution.py:570
  85.4 1.7 %collective-permute-done.1.edge_ref = bf16[2,256,256]{2,1,0:T(8,128)(2,1)S(1)} collective-permute-done((bf16[2,256,256]{2,1,0:T(8,128)(2,1)S(1)}, bf16[2,256,256]{2,1,0:T(8,128)(2,1)S(1)}, u32[]{:S(2)}, u32[]{:S(2)}) %collective-permute-start.1) | collective-permute-done | bytes 262176 | tf_op jit(solution)/shard_map/ppermute | solution.py:497
  87.1 0.0 copy-done.1
  87.1 2.9 %shard_map.75 = bf16[16,128,256]{2,1,0:T(8,128)(2,1)S(1)} custom-call(bf16[2,3,256,384]{3,2,1,0:T(8,128)(2,1)S(1)} %copy-done.1, bf16[2,512,256]{2,1,0:T(8,128)(2,1)S(1)} %get-tuple-element.41.done_ref, f32[2,256,128]{2,1,0:T(8,128)S(1)} %get-tuple-element.42.query_ref, f32[2,256,256]{2,1,0:T(8,128)S(1)} %get-tuple-element.43.part_ref, ...), custom_call_target="tpu_custom_call" | custom-call | tf_op jit(solution)/shard_map/pallas_call | solution.py:579
  90.0 0.0 copy-start.3
  90.0 29.1 %all_to_all.26 = bf16[16,128,256]{2,1,0:T(8,128)(2,1)S(1)} all-to-all(bf16[16,128,256]{2,1,0:T(8,128)(2,1)S(1)} %shard_map.75), channel_id=1, replica_groups=mesh['seq'=16,'head'=2] {'seq'}, dimensions={0} | all-to-all | bytes 2097152 | tf_op jit(solution)/shard_map/all_to_all | solution.py:492
  119.1 0.0 copy-done.3
  119.1 1.5 %shard_map.76 = (bf16[512,128]{1,0:T(8,128)(2,1)}, bf16[512,128]{1,0:T(8,128)(2,1)}) custom-call(bf16[2048,512]{1,0:T(8,128)(2,1)S(1)} %copy-done.3, bf16[2048,256]{1,0:T(8,128)(2,1)S(1)} %bitcast.13), custom_call_target="tpu_custom_call" | custom-call | tf_op jit(solution)/shard_map/pallas_call | solution.py:585
Async XLA Ops:
  2.5 0.9 copy-start.7
  3.4 0.9 copy-start.8
  4.3 0.9 copy-start.9
  9.5 42.5 %all-to-all-start = ((bf16[16,128,384]{2,1,0:T(8,128)(2,1)}), bf16[16,128,384]{2,1,0:T(8,128)(2,1)S(1)}, u32[]{:S(2)}, u32[]{:S(2)}) async-start(bf16[16,128,384]{2,1,0:T(8,128)(2,1)} %bitcast.5), calls=%async_computation | async-start | bytes 3145728 | tf_op jit(solution)/shard_map/all_to_all | solution.py:492
  27.3 1.0 copy-start.4
  29.7 23.8 %copy-start.10 = (s32[1,2,48]{2,1,0:T(2,128)S(1)}, s32[1,2,48]{2,1,0:T(2,128)}, u32[]{:S(2)}) copy-start(s32[1,2,48]{2,1,0:T(2,128)} %param.9) | copy-start | bytes 1156
  52.0 1.4 %copy-start.2 = (bf16[16,128,384]{2,1,0:T(8,128)(2,1)}, bf16[16,128,384]{2,1,0:T(8,128)(2,1)S(1)}, u32[]{:S(2)}) copy-start(bf16[16,128,384]{2,1,0:T(8,128)(2,1)S(1)} %all-to-all-done.got_ref) | copy-start | bytes 4718596
  52.5 11.1 %collective-permute-start = (bf16[2,256,256]{2,1,0:T(8,128)(2,1)S(1)}, bf16[2,256,256]{2,1,0:T(8,128)(2,1)S(1)}, u32[]{:S(2)}, u32[]{:S(2)}) collective-permute-start(bf16[2,256,256]{2,1,0:T(8,128)(2,1)S(1)} %shard_map.71), channel_id=1, source_target_pairs={{0,2},{2,4},{4,6},{6,8},{8,10},{10,12},{12,14},{14,16},{16,18},{18... | collective-permute-start | bytes 786440 | tf_op jit(solution)/shard_map/ppermute | solution.py:497
  58.8 1.0 copy-start.6
  59.7 17.5 %copy-start = (bf16[2,3,256,384]{3,2,1,0:T(8,128)(2,1)}, bf16[2,3,256,384]{3,2,1,0:T(8,128)(2,1)S(1)}, u32[]{:S(2)}) copy-start(bf16[2,3,256,384]{3,2,1,0:T(8,128)(2,1)S(1)} %get-tuple-element.28.rows_ref) | copy-start | bytes 3538948
  59.7 17.5 %copy-start.5 = (bf16[2,384,768]{2,1,0:T(8,128)(2,1)S(1)}, bf16[2,384,768]{2,1,0:T(8,128)(2,1)}, u32[]{:S(2)}) copy-start(bf16[2,384,768]{2,1,0:T(8,128)(2,1)} %copy-done.4) | copy-start | bytes 3538948
  80.5 6.6 %collective-permute-start.1 = (bf16[2,256,256]{2,1,0:T(8,128)(2,1)S(1)}, bf16[2,256,256]{2,1,0:T(8,128)(2,1)S(1)}, u32[]{:S(2)}, u32[]{:S(2)}) collective-permute-start(bf16[2,256,256]{2,1,0:T(8,128)(2,1)S(1)} %get-tuple-element.44), channel_id=1, source_target_pairs={{0,30},{2,0},{4,2},{6,4},{8,6},{10,8},{12,10},{14,12},{16,14},{18,... | collective-permute-start | bytes 786440 | tf_op jit(solution)/shard_map/ppermute | solution.py:497
  82.4 4.7 %copy-start.1 = (bf16[2,3,256,384]{3,2,1,0:T(8,128)(2,1)S(1)}, bf16[2,3,256,384]{3,2,1,0:T(8,128)(2,1)}, u32[]{:S(2)}) copy-start(bf16[2,3,256,384]{3,2,1,0:T(8,128)(2,1)} %copy-done) | copy-start | bytes 3538948
  90.0 29.1 %copy-start.3 = (bf16[2048,512]{1,0:T(8,128)(2,1)S(1)}, bf16[2048,512]{1,0:T(8,128)(2,1)}, u32[]{:S(2)}) copy-start(bf16[2048,512]{1,0:T(8,128)(2,1)} %get-tuple-element.25.pick_ref) | copy-start | bytes 6291460
where the time goes:
time: 121 us
  blocking collectives  41.3 us (34%)
  Pallas kernels  31.5 us (26%)
  waiting for transfers between devices  27.9 us (23%)
  starting transfers between devices  11.2 us (9%)
  local copies, waits for them, and re-layouts  7.8 us (6%)
    all_to_all x2, blocking collectives, exchange(): return lax.all_to_all(array, 'seq', split_axis=0, concat_axis=0, tiled=True)  41.3 us
    all_to_all x1, waiting for transfers between devices, exchange(): return lax.all_to_all(array, 'seq', split_axis=0, concat_axis=0, tiled=True)  22.3 us
    pallas_call x1, Pallas kernels, head_backward(): call(functools.partial(index_kernel, rounds, devices, bound, token_count)...  9.51 us
    all_to_all x1, starting transfers between devices, exchange(): return lax.all_to_all(array, 'seq', split_axis=0, concat_axis=0, tiled=True)  8.32 us
    ppermute x2, waiting for transfers between devices, shifted(): lax.ppermute(array, 'seq', [(i, (i + by) % devices) for i in range(device...  5.57 us
    pallas_call x1, Pallas kernels, head_backward(): call(functools.partial(forward_inner_kernel, rounds, devices, bound), [((...  5.31 us
    unnamed x22, local copies, waits for them, and re-layouts  4.72 us
    pallas_call x1, Pallas kernels, head_backward(): call(functools.partial(pack_kernel, rounds, devices, bound), [((devices *...  4.29 us
  transfers between devices with their start and end apart: 3, of which 3 were waited for; matrix products, arithmetic and copies ran while one was open for 1% of the time, Pallas kernels for 15%

commit v1 on v0

v1 whole, which is shorter than its diff:
```python
import functools
import math

import jax
import jax.numpy as jnp
from jax import lax
from jax.experimental import pallas as pl
from jax.experimental.pallas import tpu as pltpu
from jax.sharding import PartitionSpec as P

masked_score = -1e30
norm_eps = 1e-06
lane = 128
f32 = jnp.float32
bf16 = jnp.bfloat16


def iota(shape, axis):
    return lax.broadcasted_iota(jnp.int32, shape, axis)


def float_iota(shape, axis):
    return iota(shape, axis).astype(f32)


def dot_nn(a, b):
    return lax.dot_general(a, b, (((1,), (0,)), ((), ())), preferred_element_type=f32)


def dot_nt(a, b):
    return lax.dot_general(a, b, (((1,), (1,)), ((), ())), preferred_element_type=f32)


def dot_tn(a, b):
    return lax.dot_general(a, b, (((0,), (0,)), ((), ())), preferred_element_type=f32)


def one_hot(condition):
    return jnp.where(condition, 1.0, 0.0).astype(bf16)


def block_of(device, devices):
    if devices % 4:
        return device
    depth = devices // 4
    level, column = device // 4, device % 4
    turn = column ^ (column >> 1)
    step = level + (turn % 2) * (depth - 1 - 2 * level)
    return turn * depth + step


def device_of(block, devices):
    if devices % 4:
        return block
    depth = devices // 4
    turn, step = block // depth, block % depth
    level = step + (turn % 2) * (depth - 1 - 2 * step)
    return level * 4 + (turn ^ (turn >> 1))


def earlier(size):
    return one_hot(iota((size, size), 0) < iota((size, size), 1))


def call(kernel, out_shapes, operands, scratch=(), scalars=0, remote=0, semaphores=0, far=(), direct=()):
    count = len(operands)
    held = sum(array.size * array.dtype.itemsize for array in operands[scalars : count - remote])
    for shape, dtype in list(out_shapes) + list(scratch):
        held += math.prod(shape) * jnp.dtype(dtype).itemsize
    spaces = (
        [pltpu.SMEM] * scalars + [pltpu.VMEM] * (count - scalars - remote) + [pltpu.HBM] * remote
    )
    operands = [
        pltpu.with_memory_space_constraint(array, space) if space is pltpu.HBM else array
        for array, space in zip(operands, spaces)
    ]
    return pl.pallas_call(
        kernel,
        out_shape=tuple(
            pltpu.HBM(shape, dtype) if at in far else jax.ShapeDtypeStruct(shape, dtype)
            for at, (shape, dtype) in enumerate(out_shapes)
        ),
        in_specs=[pl.BlockSpec(memory_space=space) for space in spaces],
        out_specs=tuple(
            pl.BlockSpec(memory_space=pltpu.HBM if at in direct else pltpu.VMEM)
            for at in range(len(out_shapes))
        ),
        scratch_shapes=[pltpu.VMEM(shape, dtype) for shape, dtype in scratch]
        + [pltpu.SemaphoreType.DMA((semaphores,))] * min(semaphores, 1),
        compiler_params=pltpu.CompilerParams(vmem_limit_bytes=held + 12 * 1024 * 1024),
    )(*operands)


def slot_tokens(members_ref, counts_ref, devices, group):
    rounds, groups = counts_ref.shape
    per_device = groups // devices
    rows = pl.ds(group, rounds * devices, stride=per_device)
    parts = [members_ref[half, rows, :] for half in range(members_ref.shape[0])]
    listed = jnp.concatenate(parts, axis=1)
    diagonal = iota((devices, groups), 1) == iota((devices, groups), 0) * per_device + group
    limits = [
        jnp.sum(
            jnp.where(diagonal, counts_ref[r : r + 1, :].astype(f32), 0.0), axis=1, keepdims=True
        )
        for r in range(rounds)
    ]
    limit = jnp.concatenate(limits, axis=0)
    return jnp.where(float_iota(listed.shape, 1) < limit, listed, -1)


def rank_slots(rounds, devices, token_count, tokens_ref, key_ref, value_ref):
    per_device, _, cap = key_ref.shape
    start = lax.axis_index("seq") * token_count
    before = earlier(cap)
    carry = jnp.zeros((rounds * devices, 1), f32)
    for group in range(per_device):
        local = tokens_ref[group] - start
        owned = (local >= 0) & (local < token_count)
        rank = dot_nn(one_hot(owned), before) + carry
        carry = carry + jnp.sum(jnp.where(owned, 1.0, 0.0), axis=1, keepdims=True)
        key_ref[group] = jnp.where(owned, rank, -1.0)
        value_ref[group] = jnp.where(owned, local + 1, 0).astype(f32)


def pick_rows(rounds, devices, bound, block, token_count, key_ref, value_ref):
    per_device, _, cap = key_ref.shape
    column = float_iota((bound, cap), 0)
    token = float_iota((bound, token_count), 1)
    picks = []
    for r in range(rounds):
        row = r * devices + block
        total = jnp.zeros((bound, cap), f32)
        for group in range(per_device):
            ranks = key_ref[group, pl.ds(row, 1), :]
            values = value_ref[group, pl.ds(row, 1), :]
            total = total + jnp.where(ranks == column, values, 0.0)
        index = jnp.sum(total, axis=1, keepdims=True) - 1.0
        picks.append(one_hot(index == token))
    return jnp.concatenate(picks, axis=0)


def pack_kernel(
    rounds,
    devices,
    bound,
    counts_hbm,
    members_hbm,
    q_hbm,
    v_hbm,
    g_hbm,
    send_hbm,
    tokens_ref,
    packed_ref,
    key_ref,
    value_ref,
    counts_ref,
    members_ref,
    rows_ref,
    sems,
):
    token_count, size = q_hbm.shape
    halves = members_ref.shape[0]
    copies = [pltpu.make_async_copy(counts_hbm, counts_ref, sems.at[halves + 3])]
    for half in range(halves):
        source = members_hbm.at[:, pl.ds(half * lane, lane)]
        copies.append(pltpu.make_async_copy(source, members_ref.at[half], sems.at[half]))
    for at, source in enumerate((q_hbm, v_hbm, g_hbm)):
        target = rows_ref.at[:, pl.ds(at * size, size)]
        copies.append(pltpu.make_async_copy(source, target, sems.at[halves + at]))
    for copy in copies:
        copy.start()
    for copy in copies[: halves + 1]:
        copy.wait()
    for group in range(tokens_ref.shape[0]):
        tokens_ref[group] = slot_tokens(members_ref, counts_ref, devices, group)
    rank_slots(rounds, devices, token_count, tokens_ref, key_ref, value_ref)
    parts = 4
    step = devices // parts
    sends = []
    for part in range(parts):
        picks = [
            pick_rows(
                rounds, devices, bound, block_of(device, devices), token_count, key_ref, value_ref
            )
            for device in range(part * step, (part + 1) * step)
        ]
        if part == 0:
            for copy in copies[halves + 1 :]:
                copy.wait()
        span = pl.ds(part * step * rounds * bound, step * rounds * bound)
        packed_ref[span, :] = dot_nn(jnp.concatenate(picks, axis=0), rows_ref[...]).astype(bf16)
        copy = pltpu.make_async_copy(
            packed_ref.at[span, :], send_hbm.at[span, :], sems.at[halves + 4 + part]
        )
        copy.start()
        sends.append(copy)
    for copy in sends:
        copy.wait()


def index_kernel(
    rounds,
    devices,
    bound,
    token_count,
    tokens_ref,
    place_ref,
    spread_t_ref,
    partner_ref,
    low_ref,
    home_ref,
    table_ref,
    pick_ref,
    key_ref,
    value_ref,
):
    per_device, _, cap = tokens_ref.shape
    me = block_of(lax.axis_index("seq"), devices)
    after = lax.rem(me + 1, devices)
    buffer_rows = devices * bound
    before = earlier(cap)
    source_start = iota((devices, cap), 0) * token_count
    source_place = float_iota((devices, cap), 0) * bound + 1.0
    place_column = float_iota((buffer_rows, cap), 0)
    for r in range(rounds):
        carry = jnp.zeros((devices, 1), f32)
        for group in range(per_device):
            tokens = tokens_ref[group, pl.ds(r * devices + me, 1), :]
            owned = (tokens >= source_start) & (tokens < source_start + token_count)
            rank = dot_nn(one_hot(owned), before) + carry
            carry = carry + jnp.sum(jnp.where(owned, 1.0, 0.0), axis=1, keepdims=True)
            place = (
                jnp.sum(jnp.where(owned, rank + source_place, 0.0), axis=0, keepdims=True) - 1.0
            )
            span = pl.ds(group * cap, cap)
            spread_t_ref[r, :, span] = one_hot(place == place_column)
            place_ref[pl.ds(r * per_device + group, 1), :] = place

    high_count = devices * token_count // lane
    high_start = iota((high_count, cap), 0) * lane
    low_index = iota((lane, cap), 0)
    slot = float_iota((high_count, cap), 1)

    def split(tokens):
        high = (tokens >= high_start) & (tokens < high_start + lane)
        low = jnp.bitwise_and(tokens, lane - 1) == low_index
        return high, low

    for r in range(rounds):

        def one_block(block, total):
            device = device_of(block, devices)
            for group in range(per_device):
                tokens = tokens_ref[group, pl.ds(r * devices + block, 1), :]
                high, low = split(tokens)
                group_index = (device * per_device + group).astype(f32)
                sides = jnp.concatenate(
                    [
                        jnp.where(high, group_index, 0.0).astype(bf16),
                        jnp.where(high, slot, 0.0).astype(bf16),
                    ],
                    axis=0,
                )
                total = total + dot_nt(sides, one_hot(low))
            return total

        total = lax.fori_loop(
            0, devices, one_block, jnp.zeros((2 * high_count, lane), f32), unroll=2
        )
        table_ref[r] = total.astype(bf16)

    halves = cap // lane
    kept = table_kept(per_device * halves)
    row_column = float_iota((devices * kept, cap), 0)
    for r in range(rounds):
        other = 1 - r
        for group in range(per_device + 1):
            if group < per_device:
                tokens = tokens_ref[group, pl.ds(r * devices + me, 1), :]
            else:
                tokens = tokens_ref[0, pl.ds(r * devices + after, 1), :]
            high, low = split(tokens)
            high_hot = one_hot(high)
            found = []
            for part in range(2):
                table = table_ref[other, part * high_count : (part + 1) * high_count, :]
                picked = dot_tn(table, high_hot)
                found.append(jnp.sum(jnp.where(low, picked, 0.0), axis=0, keepdims=True))
            group_index, position = found
            device = jnp.floor((group_index + 0.5) * (1.0 / per_device))
            half = jnp.floor((position + 0.5) * (1.0 / lane))
            row = device * kept + (group_index - device * per_device) * halves + half
            span = pl.ds(group * cap, cap)
            partner_ref[r, :, span] = one_hot(row == row_column)
            low_ref[pl.ds(r * (per_device + 1) + group, 1), :] = position - half * lane

    rank_slots(rounds, devices, token_count, tokens_ref, key_ref, value_ref)

    def pick_device(device, carried):
        at = pl.multiple_of(device * rounds * bound, rounds * bound)
        pick_ref[pl.ds(at, rounds * bound), :] = pick_rows(
            rounds, devices, bound, block_of(device, devices), token_count, key_ref, value_ref
        )
        return carried

    lax.fori_loop(0, devices, pick_device, 0, unroll=2)
    home_ref[...] = jnp.transpose(pick_ref[...])


def table_kept(count):
    return (count + 7) // 8 * 8


def unpack(got_ref, place_ref, r, group, rounds):
    devices, span, width = got_ref.shape
    bound = span // rounds
    cap = place_ref.shape[1]
    row = r * (place_ref.shape[0] // rounds) + group
    received = got_ref[:, r * bound : (r + 1) * bound, :].reshape(devices * bound, width)
    spread = one_hot(place_ref[row : row + 1, :] == float_iota((devices * bound, cap), 0))
    return dot_tn(spread, received).astype(bf16)


def ends_kernel(
    rounds, got_ref, place_ref, last_ref, first_ref, last_cot_ref, first_value_ref
):
    size = got_ref.shape[2] // 3
    per_device = place_ref.shape[0] // rounds
    for r in range(rounds):
        rows = unpack(got_ref, place_ref, r, per_device - 1, rounds)
        last_ref[r] = rows[:, : 2 * size]
        last_cot_ref[r] = rows[:, 2 * size :]
        rows = unpack(got_ref, place_ref, r, 0, rounds)
        first_ref[r, :, :size] = rows[:, :size]
        first_ref[r, :, size:] = rows[:, 2 * size :]
        first_value_ref[r] = rows[:, size : 2 * size]


def inverse_norm(rows):
    wide = rows.astype(f32)
    return lax.rsqrt(jnp.sum(wide * wide, axis=1, keepdims=True) + norm_eps)


def unit_rows(rows):
    return (rows.astype(f32) * inverse_norm(rows)).astype(bf16)


def scored(unit, queries, fill, own):
    cap = queries.shape[0]
    key = iota((cap, cap), 0)
    allowed = key < fill
    if own:
        allowed = allowed & (key != iota((cap, cap), 1))
    return jnp.where(allowed, dot_nt(unit, queries), masked_score)


def normalised(scores, inners):
    highest = jnp.maximum(
        jnp.max(scores[0], axis=0, keepdims=True), jnp.max(scores[1], axis=0, keepdims=True)
    )
    exps = [jnp.exp(score - highest) for score in scores]
    total = jnp.sum(exps[0], axis=0, keepdims=True) + jnp.sum(exps[1], axis=0, keepdims=True)
    inverse = 1.0 / total
    probs = [part * inverse for part in exps]
    dots = jnp.sum(probs[0] * inners[0], axis=0, keepdims=True) + jnp.sum(
        probs[1] * inners[1], axis=0, keepdims=True
    )
    return highest + jnp.log(total), dots, [prob.astype(bf16) for prob in probs]


def forward_inner_kernel(
    rounds,
    devices,
    counts_ref,
    got_ref,
    place_ref,
    last_ref,
    first_ref,
    last_cot_ref,
    first_value_ref,
    rows_ref,
    units_ref,
    prob_ref,
    inner_ref,
    first_score_ref,
    first_inner_ref,
    sums_ref,
):
    cap = prob_ref.shape[3]
    per_device = rows_ref.shape[1]
    size = rows_ref.shape[3] // 3
    base = block_of(lax.axis_index("seq"), devices) * per_device
    for r in range(rounds):
        rows_ref[r, 0, :, :size] = first_ref[r, :, :size]
        rows_ref[r, 0, :, size : 2 * size] = first_value_ref[r]
        rows_ref[r, 0, :, 2 * size :] = first_ref[r, :, size:]
        for group in range(1, per_device - 1):
            rows_ref[r, group] = unpack(got_ref, place_ref, r, group, rounds)
        rows_ref[r, per_device - 1, :, : 2 * size] = last_ref[r]
        rows_ref[r, per_device - 1, :, 2 * size :] = last_cot_ref[r]
        units = [unit_rows(rows_ref[r, group, :, :size]) for group in range(per_device)]
        for group in range(per_device):
            units_ref[r, group] = units[group]
        for group in range(per_device):
            queries = rows_ref[r, group, :, :size]
            cot = rows_ref[r, group, :, 2 * size :]
            values = rows_ref[r, group, :, size : 2 * size]
            score_now = scored(units[group], queries, counts_ref[r, base + group], True)
            inner_now = dot_nt(values, cot)
            if group == 0:
                first_score_ref[r] = score_now
                first_inner_ref[r] = inner_now
                continue
            values = rows_ref[r, group - 1, :, size : 2 * size]
            inner_before = dot_nt(values, cot)
            score_before = scored(
                units[group - 1], queries, counts_ref[r, base + group - 1], False
            )
            inners = [inner_before, inner_now]
            log_total, dots, probs = normalised([score_before, score_now], inners)
            for side in range(2):
                span = slice(side * cap, (side + 1) * cap)
                prob_ref[r, group - 1, span, :] = probs[side]
                inner_ref[r, group - 1, span, :] = inners[side].astype(bf16)
            row = r * per_device + group
            sums_ref[row : row + 1, :] = log_total
            row = (rounds + r) * per_device + group
            sums_ref[row : row + 1, :] = dots


def forward_first_kernel(
    rounds,
    devices,
    counts_ref,
    rows_ref,
    units_ref,
    behind_ref,
    ahead_ref,
    score_ref,
    inner_now_ref,
    inner_sums_ref,
    unit_ref,
    prob_ref,
    inner_ref,
    ahead_score_ref,
    ahead_inner_ref,
    sums_ref,
    send_ref,
):
    cap = prob_ref.shape[2]
    per_device = rows_ref.shape[1]
    size = rows_ref.shape[3] // 3
    groups = counts_ref.shape[1]
    base = block_of(lax.axis_index("seq"), devices) * per_device
    before = lax.rem(base + groups - 1, groups)
    sums_ref[...] = inner_sums_ref[...]
    last = per_device - 1
    for r in range(rounds):
        behind_unit = unit_rows(behind_ref[r, :, :size])
        unit_ref[r] = behind_unit
        queries = rows_ref[r, 0, :, :size]
        cot = rows_ref[r, 0, :, 2 * size :]
        score_before = scored(behind_unit, queries, counts_ref[r, before], False)
        inners = [dot_nt(behind_ref[r, :, size:], cot), inner_now_ref[r]]
        log_total, dots, probs = normalised([score_before, score_ref[r]], inners)
        for side in range(2):
            span = slice(side * cap, (side + 1) * cap)
            prob_ref[r, span, :] = probs[side]
            inner_ref[r, span, :] = inners[side].astype(bf16)
        row = r * per_device
        sums_ref[row : row + 1, :] = log_total
        row = (rounds + r) * per_device
        sums_ref[row : row + 1, :] = dots
        ahead_score_ref[r] = scored(
            units_ref[r, last], ahead_ref[r, :, :size], counts_ref[r, base + last], False
        )
        values = rows_ref[r, last, :, size : 2 * size]
        ahead_inner_ref[r] = dot_nt(values, ahead_ref[r, :, size:]).astype(bf16)
    halves = cap // lane
    count = per_device * halves
    for r in range(rounds):
        for kind in range(2):
            for group in range(per_device):
                row = (kind * rounds + r) * per_device + group
                for half in range(halves):
                    part = sums_ref[row : row + 1, half * lane : (half + 1) * lane]
                    at = (2 * r + kind) * count + group * halves + half
                    send_ref[:, at : at + 1, :] = jnp.broadcast_to(part[None], (devices, 1, lane))


def key_grad(rows, unit_grad):
    wide = rows.astype(f32)
    inverse = inverse_norm(rows)
    along = jnp.sum(wide * unit_grad, axis=1, keepdims=True)
    return inverse * unit_grad - wide * (inverse * inverse * inverse * along)


def three_parts(values):
    high = values.astype(bf16)
    rest = values - high.astype(f32)
    middle = rest.astype(bf16)
    return high, middle, (rest - middle.astype(f32)).astype(bf16)


def backward_kernel(
    rounds,
    devices,
    bound,
    counts_ref,
    everyone_ref,
    partner_ref,
    low_ref,
    sums_ref,
    rows_ref,
    ahead_ref,
    units_ref,
    behind_unit_ref,
    first_prob_ref,
    first_inner_ref,
    prob_ref,
    inner_ref,
    ahead_score_ref,
    ahead_inner_ref,
    spread_t_ref,
    send_ref,
    grads_ref,
):
    cap = rows_ref.shape[2]
    per_device = rows_ref.shape[1]
    size = rows_ref.shape[3] // 3
    groups = counts_ref.shape[1]
    me = block_of(lax.axis_index("seq"), devices)
    ahead_device = device_of(lax.rem(me + 1, devices), devices)
    halves = cap // lane
    count = per_device * halves
    kept = table_kept(count)
    low_column = float_iota((lane, cap), 0)
    slot = iota((1, cap), 1)

    def sums_of_all(r, kind):
        start = (2 * r + kind) * count
        held = min(start, everyone_ref.shape[1] - kept)
        rows = everyone_ref[:, held : held + kept, :]
        if start > held:
            rows = jnp.concatenate(
                [rows[:, start - held :], jnp.zeros((devices, start - held, lane), f32)], axis=1
            )
        return jnp.transpose(rows.reshape(devices * kept, lane))

    def ahead_sums(r, kind):
        start = (2 * r + kind) * count
        rows = [everyone_ref[ahead_device, start + h : start + h + 1, :] for h in range(halves)]
        return jnp.concatenate(rows, axis=1)

    for r in range(rounds):
        logs = three_parts(sums_of_all(1 - r, 0))
        dots = three_parts(sums_of_all(1 - r, 1))
        upright = jnp.concatenate(logs + dots[:2], axis=0)
        picked = dot_nn(upright, partner_ref[r])
        picked_log = picked[:lane] + (picked[lane : 2 * lane] + picked[2 * lane : 3 * lane])
        picked_dot = picked[3 * lane : 4 * lane] + picked[4 * lane :]
        scales = []
        for group in range(per_device + 1):
            at = r * (per_device + 1) + group
            here = low_ref[at : at + 1, :] == low_column
            span = slice(group * cap, (group + 1) * cap)
            other_log = jnp.sum(jnp.where(here, picked_log[:, span], 0.0), axis=0, keepdims=True)
            other_dot = jnp.sum(jnp.where(here, picked_dot[:, span], 0.0), axis=0, keepdims=True)
            if group < per_device:
                row = r * per_device + group
                own_log = sums_ref[row : row + 1, :]
                own_dot = sums_ref[rounds * per_device + row : rounds * per_device + row + 1, :]
            else:
                own_log = ahead_sums(r, 0)
                own_dot = ahead_sums(r, 1)
                ahead_log = own_log
            weight = 1.0 / (1.0 + jnp.exp(other_log - own_log))
            other_weight = 1.0 / (1.0 + jnp.exp(own_log - other_log))
            mixture = weight * own_dot + other_weight * other_dot
            valid = slot < counts_ref[r, lax.rem(me * per_device + group, groups)]
            scales.append((jnp.where(valid, weight, 0.0), jnp.where(valid, mixture, 0.0)))

        def score_grads(prob, inner, scale):
            weighted = prob.astype(f32) * scale[0]
            score_grad = (weighted * (inner.astype(f32) - scale[1])).astype(bf16)
            return weighted.astype(bf16), score_grad

        query_grad = None
        unit_grad = None
        value_grad = None
        for group in range(per_device + 1):
            if group < per_device:
                queries = rows_ref[r, group][:, :size]
                cot = rows_ref[r, group][:, 2 * size :]
            else:
                queries = ahead_ref[r][:, :size]
                cot = ahead_ref[r][:, size:]
            if group == 0:
                probs = [first_prob_ref[r, :cap, :], first_prob_ref[r, cap:, :]]
                inners = [first_inner_ref[r, :cap, :], first_inner_ref[r, cap:, :]]
            elif group < per_device:
                probs = [prob_ref[r, group - 1, :cap, :], prob_ref[r, group - 1, cap:, :]]
                inners = [inner_ref[r, group - 1, :cap, :], inner_ref[r, group - 1, cap:, :]]
            else:
                probs = [jnp.exp(ahead_score_ref[r] - ahead_log)]
                inners = [ahead_inner_ref[r]]
            weighted, score_grad = score_grads(probs[0], inners[0], scales[group])
            if group > 0:
                unit_grad = unit_grad + dot_nn(score_grad, queries)
                value_grad = value_grad + dot_nn(weighted, cot)
                key_part = key_grad(rows_ref[r, group - 1][:, :size], unit_grad)
                span = slice((group - 1) * cap, group * cap)
                grads_ref[span, :size] = (query_grad + key_part).astype(bf16)
                grads_ref[span, size:] = value_grad.astype(bf16)
            if group < per_device:
                unit_before = behind_unit_ref[r] if group == 0 else units_ref[r, group - 1]
                query_grad = dot_tn(score_grad, unit_before)
                weighted, score_grad = score_grads(probs[1], inners[1], scales[group])
                query_grad = query_grad + dot_tn(score_grad, units_ref[r, group])
                unit_grad = dot_nn(score_grad, queries)
                value_grad = dot_nn(weighted, cot)
        packed = dot_nn(spread_t_ref[r], grads_ref[...]).astype(bf16)
        send_ref[:, r * bound : (r + 1) * bound, :] = packed.reshape(devices, bound, 2 * size)


def home_kernel(home_ref, got_ref, qk_ref, value_ref):
    size = qk_ref.shape[1]
    total = dot_nn(home_ref[...], got_ref[...])
    qk_ref[...] = total[:, :size].astype(bf16)
    value_ref[...] = total[:, size:].astype(bf16)


def exchange(array):
    return lax.all_to_all(array, "seq", split_axis=0, concat_axis=0, tiled=True)


def shifted(array, by):
    devices = lax.axis_size("seq")
    order = [device_of(block, devices) for block in range(devices)]
    return lax.ppermute(array, "seq", [(order[i], order[(i + by) % devices]) for i in range(devices)])


def head_backward(qk, values, cot, members, counts):
    devices = lax.axis_size("seq")
    token_count, size = qk.shape
    rounds, groups, cap = members.shape
    per_device = groups // devices
    slots = per_device * cap
    bound = 2 * token_count // devices
    span = rounds * bound
    buffer_rows = devices * bound
    sum_rows = 2 * rounds * per_device
    listed = members.reshape(rounds * groups, cap)
    keys = [((per_device, rounds * devices, cap), f32)] * 2
    pick = ((devices * span, token_count), bf16)
    send, tokens = call(
        functools.partial(pack_kernel, rounds, devices, bound),
        [((devices * span, 3 * size), bf16), (keys[0][0], jnp.int32)],
        [counts, listed, qk, values, cot],
        [((devices * span, 3 * size), bf16)]
        + keys
        + [
            (counts.shape, jnp.int32),
            ((cap // lane, rounds * groups, lane), jnp.int32),
            ((token_count, 3 * size), bf16),
        ],
        remote=5,
        semaphores=cap // lane + 8,
        far=(0,),
        direct=(0,),
    )
    got = exchange(send).reshape(devices, span, 3 * size)
    place, spread_t, partner, low, home_pick = call(
        functools.partial(index_kernel, rounds, devices, bound, token_count),
        [
            ((rounds * per_device, cap), f32),
            ((rounds, buffer_rows, slots), bf16),
            ((rounds, devices * table_kept(slots // lane), slots + cap), bf16),
            ((rounds * (per_device + 1), cap), f32),
            ((token_count, devices * span), bf16),
        ],
        [tokens],
        [((rounds, 2 * devices * token_count // lane, lane), bf16), pick] + keys,
        far=(1, 2, 4),
    )
    last, first, last_cot, first_value = call(
        functools.partial(ends_kernel, rounds),
        [((rounds, cap, 2 * size), bf16)] * 2 + [((rounds, cap, size), bf16)] * 2,
        [got, place],
    )
    behind = shifted(last, 1)
    ahead = shifted(first, -1)
    square = (rounds, cap, cap)
    rows, units, prob, inner, first_score, first_inner_now, inner_sums = call(
        functools.partial(forward_inner_kernel, rounds, devices),
        [
            ((rounds, per_device, cap, 3 * size), bf16),
            ((rounds, per_device, cap, size), bf16),
            ((rounds, per_device - 1, 2 * cap, cap), bf16),
            ((rounds, per_device - 1, 2 * cap, cap), bf16),
            (square, f32),
            (square, f32),
            ((sum_rows, cap), f32),
        ],
        [counts, got, place, last, first, last_cot, first_value],
        scalars=1,
    )
    behind_unit, first_prob, first_inner, ahead_score, ahead_inner, sums, sums_send = call(
        functools.partial(forward_first_kernel, rounds, devices),
        [
            ((rounds, cap, size), bf16),
            ((rounds, 2 * cap, cap), bf16),
            ((rounds, 2 * cap, cap), bf16),
            (square, f32),
            (square, bf16),
            ((sum_rows, cap), f32),
            ((devices, sum_rows * cap // lane, lane), f32),
        ],
        [counts, rows, units, behind, ahead, first_score, first_inner_now, inner_sums],
        scalars=1,
    )
    everyone = exchange(sums_send)
    (grads_send,) = call(
        functools.partial(backward_kernel, rounds, devices, bound),
        [((devices, span, 2 * size), bf16)],
        [
            counts,
            everyone,
            partner,
            low,
            sums,
            rows,
            ahead,
            units,
            behind_unit,
            first_prob,
            first_inner,
            prob,
            inner,
            ahead_score,
            ahead_inner,
            spread_t,
        ],
        [((slots, 2 * size), bf16)],
        scalars=1,
    )
    home = exchange(grads_send.reshape(devices * span, 2 * size))
    return call(
        home_kernel,
        [((token_count, size), bf16), ((token_count, size), bf16)],
        [home_pick, home],
    )


def on_device(qk, values, grad_out, members, counts):
    grad_qk, grad_v = head_backward(qk[0], values[0], grad_out[0], members[0], counts[0])
    return (grad_qk[None], grad_v[None])


def solution(mesh):
    in_specs = (
        P("head", "seq", None),
        P("head", "seq", None),
        P("head", "seq", None),
        P("head", None, None, None),
        P("head", None, None),
    )
    out_specs = (P("head", "seq", None), P("head", "seq", None))
    return jax.shard_map(
        on_device, mesh=mesh, in_specs=in_specs, out_specs=out_specs, check_vma=False
    )
```

time: 121 us -> 106 us (0.88)
  local copies, waits for them, and re-layouts: 7.8 us -> 0.02 us
  Pallas kernels: 31.5 us -> 26 us
  blocking collectives: 41.3 us -> 38.4 us
  starting transfers between devices: 11.2 us -> 13.2 us
    pallas_call x9 -> x7, Pallas kernels: 31.5 us -> 26 us  [call(): pl.pallas_call(kernel, out_shape=tuple((pltpu.HBM(shape, dtype) if at in...]
    unnamed x22 -> x8, local copies, waits for them, and re-layouts: 4.72 us -> 0.02 us
    all_to_all x2, blocking collectives: 41.3 us -> 38.4 us  [exchange(): return lax.all_to_all(array, 'seq', split_axis=0, concat_axis=0, tiled=True)]
    ppermute x2, starting transfers between devices: 2.92 us -> 4.89 us  [shifted(): lax.ppermute(array, 'seq', [(order[i], order[(i + by) % devices]) for i i...]
    ppermute x2, waiting for transfers between devices: 5.57 us -> 3.71 us  [shifted(): lax.ppermute(array, 'seq', [(order[i], order[(i + by) % devices]) for i i...]
    slice x1 -> x0, local copies, waits for them, and re-layouts: 1.29 us -> none  [head_backward(): spread[:, slots - cap:]]
  transfers between devices with their start and end apart: 3 -> 3, of which waited for: 3 -> 3; matrix products, arithmetic and copies ran while one was open for 1% -> 0% of each run, Pallas kernels for 15% -> 13%
where the time goes in v1:
time: 106 us; the launch traced here: 105 us
  blocking collectives  38.4 us (36%)
  waiting for transfers between devices  27.1 us (26%)
  Pallas kernels  26 us (25%)
  starting transfers between devices  13.2 us (12%)
    all_to_all x2, blocking collectives, exchange(): return lax.all_to_all(array, 'seq', split_axis=0, concat_axis=0, tiled=True)  38.4 us
    pallas_call x7, Pallas kernels, call(): pl.pallas_call(kernel, out_shape=tuple((pltpu.HBM(shape, dtype) if at in...  26 us
    all_to_all x1, waiting for transfers between devices, exchange(): return lax.all_to_all(array, 'seq', split_axis=0, concat_axis=0, tiled=True)  23.4 us
    all_to_all x1, starting transfers between devices, exchange(): return lax.all_to_all(array, 'seq', split_axis=0, concat_axis=0, tiled=True)  8.32 us
    ppermute x2, starting transfers between devices, shifted(): lax.ppermute(array, 'seq', [(order[i], order[(i + by) % devices]) for i i...  4.89 us
    ppermute x2, waiting for transfers between devices, shifted(): lax.ppermute(array, 'seq', [(order[i], order[(i + by) % devices]) for i i...  3.71 us
  transfers between devices with their start and end apart: 3, of which 3 were waited for; matrix products, arithmetic and copies ran while one was open for 0% of the time, Pallas kernels for 13%

profile of v1, /device:TPU:0, one launch (start us, length us, event | category | flops | bytes accessed | tf_op | source)
XLA Modules:
  0.0 105.3 jit_solution(1771285134899178302)
XLA Ops:
  0.6 3.6 %shard_map.68 = (bf16[2048,384]{1,0:T(8,128)(2,1)}, s32[3,32,256]{2,1,0:T(8,128)S(1)}) custom-call(s32[2,48]{1,0:T(2,128)} %bitcast.10, s32[96,256]{1,0:T(8,128)} %bitcast.18, bf16[512,128]{1,0:T(8,128)(2,1)} %bitcast.15, bf16[512,128]{1,0:T(8,128)(2,1)} %bitcast.16, bf16[512,128]{1,0:T(8,128)(2,1)} %bitcast.17), custom_call_target="tpu_custom_call" | custom-call | tf_op jit(solution)/shard_map/pallas_call | solution.py:77
  4.2 8.3 %all-to-all-start = ((bf16[16,128,384]{2,1,0:T(8,128)(2,1)}), bf16[16,128,384]{2,1,0:T(8,128)(2,1)S(1)}, u32[]{:S(2)}, u32[]{:S(2)}) async-start(bf16[16,128,384]{2,1,0:T(8,128)(2,1)} %bitcast.14), calls=%async_computation | async-start | bytes 3145728 | tf_op jit(solution)/shard_map/all_to_all | solution.py:634
  12.5 0.0 copy-start.3
  12.5 10.8 %shard_map.69 = (f32[6,256]{1,0:T(8,128)S(1)}, bf16[2,1024,768]{2,1,0:T(8,128)(2,1)}, bf16[2,128,1024]{2,1,0:T(8,128)(2,1)}, f32[8,256]{1,0:T(8,128)S(1)}, bf16[512,2048]{1,0:T(8,128)(2,1)}) custom-call(s32[3,32,256]{2,1,0:T(8,128)S(1)} %get-tuple-element.29.tokens_ref), custom_call_target="tpu_custom_call" | custom-call | tf_op jit(solution)/shard_map/pallas_call | solution.py:77
  23.4 23.4 %all-to-all-done.got_ref = bf16[16,128,384]{2,1,0:T(8,128)(2,1)S(1)} async-done(((bf16[16,128,384]{2,1,0:T(8,128)(2,1)}), bf16[16,128,384]{2,1,0:T(8,128)(2,1)S(1)}, u32[]{:S(2)}, u32[]{:S(2)}) %all-to-all-start) | async-done | bytes 1572896 | tf_op jit(solution)/shard_map/all_to_all | solution.py:634
  46.7 1.4 %shard_map.70 = (bf16[2,256,256]{2,1,0:T(8,128)(2,1)S(1)}, bf16[2,256,256]{2,1,0:T(8,128)(2,1)S(1)}, bf16[2,256,128]{2,1,0:T(8,128)(2,1)S(1)}, bf16[2,256,128]{2,1,0:T(8,128)(2,1)S(1)}) custom-call(bf16[16,128,384]{2,1,0:T(8,128)(2,1)S(1)} %all-to-all-done.got_ref, f32[6,256]{1,0:T(8,128)S(1)} %get-tuple-element.32.place_ref), custom_call_target="tpu_custom_call" | custom-call | tf_op jit(solution)/shard_map/pallas_call | solution.py:77
  48.1 2.7 %collective-permute-start.1 = (bf16[2,256,256]{2,1,0:T(8,128)(2,1)S(1)}, bf16[2,256,256]{2,1,0:T(8,128)(2,1)S(1)}, u32[]{:S(2)}, u32[]{:S(2)}) collective-permute-start(bf16[2,256,256]{2,1,0:T(8,128)(2,1)S(1)} %get-tuple-element.34.first_ref), channel_id=1, source_target_pairs={{0,4},{8,0},{16,8},{24,16},{26,24},{18,26},{10,18},{2,10},{6,2},{1... | collective-permute-start | bytes 786440 | tf_op jit(solution)/shard_map/ppermute | solution.py:640
  50.8 2.2 %collective-permute-start = (bf16[2,256,256]{2,1,0:T(8,128)(2,1)S(1)}, bf16[2,256,256]{2,1,0:T(8,128)(2,1)S(1)}, u32[]{:S(2)}, u32[]{:S(2)}) collective-permute-start(bf16[2,256,256]{2,1,0:T(8,128)(2,1)S(1)} %get-tuple-element.33.last_ref), channel_id=1, source_target_pairs={{0,8},{8,16},{16,24},{24,26},{26,18},{18,10},{10,2},{2,6},{6,14},{... | collective-permute-start | bytes 786440 | tf_op jit(solution)/shard_map/ppermute | solution.py:640
  53.0 0.0 copy-done.3
  53.0 0.0 copy-start.2
  53.0 3.1 %shard_map.71 = (bf16[2,3,256,384]{3,2,1,0:T(8,128)(2,1)S(1)}, bf16[2,3,256,128]{3,2,1,0:T(8,128)(2,1)S(1)}, bf16[2,2,512,256]{3,2,1,0:T(8,128)(2,1)S(1)}, bf16[...) custom-call(s32[2,48]{1,0:T(2,128)S(1)} %bitcast.11, ...), custom_call_target="tpu_custom_call" | custom-call | tf_op jit(solution)/shard_map/pallas_call | solution.py:77
  56.1 1.2 %collective-permute-done.1.ahead_ref = bf16[2,256,256]{2,1,0:T(8,128)(2,1)S(1)} collective-permute-done((bf16[2,256,256]{2,1,0:T(8,128)(2,1)S(1)}, bf16[2,256,256]{2,1,0:T(8,128)(2,1)S(1)}, u32[]{:S(2)}, u32[]{:S(2)}) %collective-permute-start.1) | collective-permute-done | bytes 262176 | tf_op jit(solution)/shard_map/ppermute | solution.py:640
  57.3 2.5 %collective-permute-done.behind_ref = bf16[2,256,256]{2,1,0:T(8,128)(2,1)S(1)} collective-permute-done((bf16[2,256,256]{2,1,0:T(8,128)(2,1)S(1)}, bf16[2,256,256]{2,1,0:T(8,128)(2,1)S(1)}, u32[]{:S(2)}, u32[]{:S(2)}) %collective-permute-start) | collective-permute-done | bytes 262176 | tf_op jit(solution)/shard_map/ppermute | solution.py:640
  59.8 0.0 copy-start
  59.8 1.5 %shard_map.72 = (bf16[2,256,128]{2,1,0:T(8,128)(2,1)S(1)}, bf16[2,512,256]{2,1,0:T(8,128)(2,1)S(1)}, bf16[2,512,256]{2,1,0:T(8,128)(2,1)S(1)}, f32[2,256,256]{2,...) custom-call(s32[2,48]{1,0:T(2,128)S(1)} %bitcast.12, ...), custom_call_target="tpu_custom_call" | custom-call | tf_op jit(solution)/shard_map/pallas_call | solution.py:77
  61.3 12.2 %all_to_all.22.everyone_ref = f32[16,24,128]{2,1,0:T(8,128)S(1)} all-to-all(f32[16,24,128]{2,1,0:T(8,128)S(1)} %get-tuple-element.42), channel_id=1, replica_groups=mesh['seq'=16,'head'=2] {'seq'}, dimensions={0} | all-to-all | bytes 393216 | tf_op jit(solution)/shard_map/all_to_all | solution.py:634
  73.5 0.0 copy-done.2
  73.5 0.0 copy-done
  73.5 4.3 %shard_map.73 = bf16[16,128,256]{2,1,0:T(8,128)(2,1)S(1)} custom-call(s32[2,48]{1,0:T(2,128)S(1)} %bitcast.13, f32[16,24,128]{2,1,0:T(8,128)S(1)} %all_to_all.22.everyone_ref, bf16[2,128,1024]{2,1,0:T(8,128)(2,1)S(1)} %copy-done.2, f32[8,256]{1,0:T(8,128)S(1)} %get-tuple-element.44.low_ref, f32[12,256]{1,0:T(8,128)S(1)} %get-tuple-element.45.sums_ref, ...), custom_call_target="tpu_custom_call" | custom-call | tf_op jit(solution)/shard_map/pallas_call | solution.py:77
  77.8 0.0 copy-start.1
  77.8 26.2 %all_to_all.23 = bf16[16,128,256]{2,1,0:T(8,128)(2,1)S(1)} all-to-all(bf16[16,128,256]{2,1,0:T(8,128)(2,1)S(1)} %shard_map.73), channel_id=1, replica_groups=mesh['seq'=16,'head'=2] {'seq'}, dimensions={0} | all-to-all | bytes 2097152 | tf_op jit(solution)/shard_map/all_to_all | solution.py:634
  103.9 0.0 copy-done.1
  103.9 1.4 %shard_map.74 = (bf16[512,128]{1,0:T(8,128)(2,1)}, bf16[512,128]{1,0:T(8,128)(2,1)}) custom-call(bf16[512,2048]{1,0:T(8,128)(2,1)S(1)} %copy-done.1, bf16[2048,256]{1,0:T(8,128)(2,1)S(1)} %bitcast.9), custom_call_target="tpu_custom_call" | custom-call | tf_op jit(solution)/shard_map/pallas_call | solution.py:77
Async XLA Ops:
  4.2 42.5 %all-to-all-start = ((bf16[16,128,384]{2,1,0:T(8,128)(2,1)}), bf16[16,128,384]{2,1,0:T(8,128)(2,1)S(1)}, u32[]{:S(2)}, u32[]{:S(2)}) async-start(bf16[16,128,384]{2,1,0:T(8,128)(2,1)} %bitcast.14), calls=%async_computation | async-start | bytes 3145728 | tf_op jit(solution)/shard_map/all_to_all | solution.py:634
  12.5 40.4 %copy-start.3 = (s32[1,2,48]{2,1,0:T(2,128)S(1)}, s32[1,2,48]{2,1,0:T(2,128)}, u32[]{:S(2)}) copy-start(s32[1,2,48]{2,1,0:T(2,128)} %param.9) | copy-start | bytes 1156
  48.1 9.2 %collective-permute-start.1 = (bf16[2,256,256]{2,1,0:T(8,128)(2,1)S(1)}, bf16[2,256,256]{2,1,0:T(8,128)(2,1)S(1)}, u32[]{:S(2)}, u32[]{:S(2)}) collective-permute-start(bf16[2,256,256]{2,1,0:T(8,128)(2,1)S(1)} %get-tuple-element.34.first_ref), channel_id=1, source_target_pairs={{0,4},{8,0},{16,8},{24,16},{26,24},{18,26},{10,18},{2,10},{6,2},{1... | collective-permute-start | bytes 786440 | tf_op jit(solution)/shard_map/ppermute | solution.py:640
  50.8 9.0 %collective-permute-start = (bf16[2,256,256]{2,1,0:T(8,128)(2,1)S(1)}, bf16[2,256,256]{2,1,0:T(8,128)(2,1)S(1)}, u32[]{:S(2)}, u32[]{:S(2)}) collective-permute-start(bf16[2,256,256]{2,1,0:T(8,128)(2,1)S(1)} %get-tuple-element.33.last_ref), channel_id=1, source_target_pairs={{0,8},{8,16},{16,24},{24,26},{26,18},{18,10},{10,2},{2,6},{6,14},{... | collective-permute-start | bytes 786440 | tf_op jit(solution)/shard_map/ppermute | solution.py:640
  53.0 20.5 %copy-start.2 = (bf16[2,128,1024]{2,1,0:T(8,128)(2,1)S(1)}, bf16[2,128,1024]{2,1,0:T(8,128)(2,1)}, u32[]{:S(2)}) copy-start(bf16[2,128,1024]{2,1,0:T(8,128)(2,1)} %get-tuple-element.43.partner_ref) | copy-start | bytes 1572868
  59.8 13.7 %copy-start = (bf16[2,1024,768]{2,1,0:T(8,128)(2,1)S(1)}, bf16[2,1024,768]{2,1,0:T(8,128)(2,1)}, u32[]{:S(2)}) copy-start(bf16[2,1024,768]{2,1,0:T(8,128)(2,1)} %get-tuple-element.53.spread_t_ref) | copy-start | bytes 9437188
  77.8 26.2 %copy-start.1 = (bf16[512,2048]{1,0:T(8,128)(2,1)S(1)}, bf16[512,2048]{1,0:T(8,128)(2,1)}, u32[]{:S(2)}) copy-start(bf16[512,2048]{1,0:T(8,128)(2,1)} %get-tuple-element.30.home_ref) | copy-start | bytes 6291460

commit v2 on v1

--- a/solution.py
+++ b/solution.py
@@ -37,6 +37,12 @@
 
 def one_hot(condition):
     return jnp.where(condition, 1.0, 0.0).astype(bf16)
+
+
+def short_hot(index, shape, axis):
+    place = iota(shape, axis).astype(jnp.int16)
+    short = jnp.broadcast_to(index.astype(jnp.int32), shape).astype(jnp.int16)
+    return jnp.where(short == place, jnp.ones(shape, bf16), jnp.zeros(shape, bf16))
 
 
 def block_of(device, devices):
@@ -125,7 +131,6 @@
 def pick_rows(rounds, devices, bound, block, token_count, key_ref, value_ref):
     per_device, _, cap = key_ref.shape
     column = float_iota((bound, cap), 0)
-    token = float_iota((bound, token_count), 1)
     picks = []
     for r in range(rounds):
         row = r * devices + block
@@ -135,7 +140,7 @@
             values = value_ref[group, pl.ds(row, 1), :]
             total = total + jnp.where(ranks == column, values, 0.0)
         index = jnp.sum(total, axis=1, keepdims=True) - 1.0
-        picks.append(one_hot(index == token))
+        picks.append(short_hot(index, (bound, token_count), 1))
     return jnp.concatenate(picks, axis=0)
 
 
@@ -311,29 +316,34 @@
     return (count + 7) // 8 * 8
 
 
-def unpack(got_ref, place_ref, r, group, rounds):
+def spread_of(place_ref, r, group, rounds, buffer_rows):
+    row = r * (place_ref.shape[0] // rounds) + group
+    cap = place_ref.shape[1]
+    return short_hot(place_ref[row : row + 1, :], (buffer_rows, cap), 0)
+
+
+def received_rows(got_ref, r, rounds):
     devices, span, width = got_ref.shape
     bound = span // rounds
-    cap = place_ref.shape[1]
-    row = r * (place_ref.shape[0] // rounds) + group
-    received = got_ref[:, r * bound : (r + 1) * bound, :].reshape(devices * bound, width)
-    spread = one_hot(place_ref[row : row + 1, :] == float_iota((devices * bound, cap), 0))
-    return dot_tn(spread, received).astype(bf16)
-
-
-def ends_kernel(
-    rounds, got_ref, place_ref, last_ref, first_ref, last_cot_ref, first_value_ref
-):
+    return got_ref[:, r * bound : (r + 1) * bound, :].reshape(devices * bound, width)
+
+
+def last_kernel(rounds, got_ref, place_ref, last_ref):
     size = got_ref.shape[2] // 3
     per_device = place_ref.shape[0] // rounds
     for r in range(rounds):
-        rows = unpack(got_ref, place_ref, r, per_device - 1, rounds)
-        last_ref[r] = rows[:, : 2 * size]
-        last_cot_ref[r] = rows[:, 2 * size :]
-        rows = unpack(got_ref, place_ref, r, 0, rounds)
-        first_ref[r, :, :size] = rows[:, :size]
-        first_ref[r, :, size:] = rows[:, 2 * size :]
-        first_value_ref[r] = rows[:, size : 2 * size]
+        received = received_rows(got_ref, r, rounds)
+        spread = spread_of(place_ref, r, per_device - 1, rounds, received.shape[0])
+        last_ref[r] = dot_tn(spread, received[:, : 2 * size]).astype(bf16)
+
+
+def first_kernel(rounds, got_ref, place_ref, first_ref):
+    size = got_ref.shape[2] // 3
+    for r in range(rounds):
+        received = received_rows(got_ref, r, rounds)
+        spread = spread_of(place_ref, r, 0, rounds, received.shape[0])
+        wanted = jnp.concatenate([received[:, :size], received[:, 2 * size :]], axis=1)
+        first_ref[r] = dot_tn(spread, wanted).astype(bf16)
 
 
 def inverse_norm(rows):
@@ -376,8 +386,6 @@
     place_ref,
     last_ref,
     first_ref,
-    last_cot_ref,
-    first_value_ref,
     rows_ref,
     units_ref,
     prob_ref,
@@ -391,13 +399,20 @@
     size = rows_ref.shape[3] // 3
     base = block_of(lax.axis_index("seq"), devices) * per_device
     for r in range(rounds):
-        rows_ref[r, 0, :, :size] = first_ref[r, :, :size]
-        rows_ref[r, 0, :, size : 2 * size] = first_value_ref[r]
-        rows_ref[r, 0, :, 2 * size :] = first_ref[r, :, size:]
-        for group in range(1, per_device - 1):
-            rows_ref[r, group] = unpack(got_ref, place_ref, r, group, rounds)
-        rows_ref[r, per_device - 1, :, : 2 * size] = last_ref[r]
-        rows_ref[r, per_device - 1, :, 2 * size :] = last_cot_ref[r]
+        received = received_rows(got_ref, r, rounds)
+        for group in range(per_device):
+            spread = spread_of(place_ref, r, group, rounds, received.shape[0])
+            if group == 0:
+                values = dot_tn(spread, received[:, size : 2 * size]).astype(bf16)
+                rows_ref[r, group, :, :size] = first_ref[r, :, :size]
+                rows_ref[r, group, :, size : 2 * size] = values
+                rows_ref[r, group, :, 2 * size :] = first_ref[r, :, size:]
+            elif group < per_device - 1:
+                rows_ref[r, group] = dot_tn(spread, received).astype(bf16)
+            else:
+                rows_ref[r, group, :, : 2 * size] = last_ref[r]
+                cots = dot_tn(spread, received[:, 2 * size :]).astype(bf16)
+                rows_ref[r, group, :, 2 * size :] = cots
         units = [unit_rows(rows_ref[r, group, :, :size]) for group in range(per_device)]
         for group in range(per_device):
             units_ref[r, group] = units[group]
@@ -433,19 +448,16 @@
     devices,
     counts_ref,
     rows_ref,
-    units_ref,
     behind_ref,
-    ahead_ref,
     score_ref,
     inner_now_ref,
     inner_sums_ref,
     unit_ref,
     prob_ref,
     inner_ref,
-    ahead_score_ref,
-    ahead_inner_ref,
     sums_ref,
     send_ref,
+    block_ref,
 ):
     cap = prob_ref.shape[2]
     per_device = rows_ref.shape[1]
@@ -454,7 +466,6 @@
     base = block_of(lax.axis_index("seq"), devices) * per_device
     before = lax.rem(base + groups - 1, groups)
     sums_ref[...] = inner_sums_ref[...]
-    last = per_device - 1
     for r in range(rounds):
         behind_unit = unit_rows(behind_ref[r, :, :size])
         unit_ref[r] = behind_unit
@@ -471,11 +482,6 @@
         sums_ref[row : row + 1, :] = log_total
         row = (rounds + r) * per_device
         sums_ref[row : row + 1, :] = dots
-        ahead_score_ref[r] = scored(
-            units_ref[r, last], ahead_ref[r, :, :size], counts_ref[r, base + last], False
-        )
-        values = rows_ref[r, last, :, size : 2 * size]
-        ahead_inner_ref[r] = dot_nt(values, ahead_ref[r, :, size:]).astype(bf16)
     halves = cap // lane
     count = per_device * halves
     for r in range(rounds):
@@ -483,9 +489,13 @@
             for group in range(per_device):
                 row = (kind * rounds + r) * per_device + group
                 for half in range(halves):
-                    part = sums_ref[row : row + 1, half * lane : (half + 1) * lane]
                     at = (2 * r + kind) * count + group * halves + half
-                    send_ref[:, at : at + 1, :] = jnp.broadcast_to(part[None], (devices, 1, lane))
+                    block_ref[at : at + 1, :] = sums_ref[
+                        row : row + 1, half * lane : (half + 1) * lane
+                    ]
+    block = block_ref[...]
+    for device in range(devices):
+        send_ref[device] = block
 
 
 def key_grad(rows, unit_grad):
@@ -519,8 +529,6 @@
     first_inner_ref,
     prob_ref,
     inner_ref,
-    ahead_score_ref,
-    ahead_inner_ref,
     spread_t_ref,
     send_ref,
     grads_ref,
@@ -602,8 +610,10 @@
                 probs = [prob_ref[r, group - 1, :cap, :], prob_ref[r, group - 1, cap:, :]]
                 inners = [inner_ref[r, group - 1, :cap, :], inner_ref[r, group - 1, cap:, :]]
             else:
-                probs = [jnp.exp(ahead_score_ref[r] - ahead_log)]
-                inners = [ahead_inner_ref[r]]
+                fill = counts_ref[r, me * per_device + per_device - 1]
+                score = scored(units_ref[r, per_device - 1], queries, fill, False)
+                probs = [jnp.exp(score - ahead_log)]
+                inners = [dot_nt(rows_ref[r, per_device - 1][:, size : 2 * size], cot)]
             weighted, score_grad = score_grads(probs[0], inners[0], scales[group])
             if group > 0:
                 unit_grad = unit_grad + dot_nn(score_grad, queries)
@@ -683,12 +693,13 @@
         [((rounds, 2 * devices * token_count // lane, lane), bf16), pick] + keys,
         far=(1, 2, 4),
     )
-    last, first, last_cot, first_value = call(
-        functools.partial(ends_kernel, rounds),
-        [((rounds, cap, 2 * size), bf16)] * 2 + [((rounds, cap, size), bf16)] * 2,
-        [got, place],
+    (last,) = call(
+        functools.partial(last_kernel, rounds), [((rounds, cap, 2 * size), bf16)], [got, place]
     )
     behind = shifted(last, 1)
+    (first,) = call(
+        functools.partial(first_kernel, rounds), [((rounds, cap, 2 * size), bf16)], [got, place]
+    )
     ahead = shifted(first, -1)
     square = (rounds, cap, cap)
     rows, units, prob, inner, first_score, first_inner_now, inner_sums = call(
@@ -702,23 +713,23 @@
             (square, f32),
             ((sum_rows, cap), f32),
         ],
-        [counts, got, place, last, first, last_cot, first_value],
+        [counts, got, place, last, first],
         scalars=1,
     )
-    behind_unit, first_prob, first_inner, ahead_score, ahead_inner, sums, sums_send = call(
+    behind_unit, first_prob, first_inner, sums, sums_send = call(
         functools.partial(forward_first_kernel, rounds, devices),
         [
             ((rounds, cap, size), bf16),
             ((rounds, 2 * cap, cap), bf16),
             ((rounds, 2 * cap, cap), bf16),
-            (square, f32),
-            (square, bf16),
             ((sum_rows, cap), f32),
             ((devices, sum_rows * cap // lane, lane), f32),
         ],
-        [counts, rows, units, behind, ahead, first_score, first_inner_now, inner_sums],
+        [counts, rows, behind, first_score, first_inner_now, inner_sums],
+        [((sum_rows * cap // lane, lane), f32)],
         scalars=1,
     )
+    sums_send, ahead = lax.optimization_barrier((sums_send, ahead))
     everyone = exchange(sums_send)
     (grads_send,) = call(
         functools.partial(backward_kernel, rounds, devices, bound),
@@ -737,8 +748,6 @@
             first_inner,
             prob,
             inner,
-            ahead_score,
-            ahead_inner,
             spread_t,
         ],
         [((slots, 2 * size), bf16)],

time: 106 us -> 104 us (0.981)
  waiting for transfers between devices: 27.1 us -> 25 us
    ppermute x2, waiting for transfers between devices: 3.71 us -> 1.64 us  [shifted(): lax.ppermute(array, 'seq', [(order[i], order[(i + by) % devices]) for i i...]
    pallas_call x7 -> x8, Pallas kernels: 26 us -> 26.3 us  [call(): pl.pallas_call(kernel, out_shape=tuple((pltpu.HBM(shape, dtype) if at in...]
  transfers between devices with their start and end apart: 3 -> 3, of which waited for: 3 -> 2; matrix products, arithmetic and copies ran while one was open for 0% -> 0% of each run, Pallas kernels for 13% -> 15%
where the time goes in v2:
time: 104 us
  blocking collectives  38.8 us (37%)
  Pallas kernels  26.3 us (25%)
  waiting for transfers between devices  25 us (24%)
  starting transfers between devices  13.2 us (13%)
    all_to_all x2, blocking collectives, exchange(): return lax.all_to_all(array, 'seq', split_axis=0, concat_axis=0, tiled=True)  38.8 us
    pallas_call x8, Pallas kernels, call(): pl.pallas_call(kernel, out_shape=tuple((pltpu.HBM(shape, dtype) if at in...  26.3 us
    all_to_all x1, waiting for transfers between devices, exchange(): return lax.all_to_all(array, 'seq', split_axis=0, concat_axis=0, tiled=True)  23.3 us
    all_to_all x1, starting transfers between devices, exchange(): return lax.all_to_all(array, 'seq', split_axis=0, concat_axis=0, tiled=True)  8.33 us
    ppermute x2, starting transfers between devices, shifted(): lax.ppermute(array, 'seq', [(order[i], order[(i + by) % devices]) for i i...  4.88 us
  transfers between devices with their start and end apart: 3, of which 2 were waited for; matrix products, arithmetic and copies ran while one was open for 0% of the time, Pallas kernels for 15%

profile of v2, /device:TPU:0, one launch (start us, length us, event | category | flops | bytes accessed | tf_op | source)
XLA Modules:
  0.0 104.0 jit_solution(12233256757917577250)
XLA Ops:
  0.6 3.5 %shard_map.68 = (bf16[2048,384]{1,0:T(8,128)(2,1)}, s32[3,32,256]{2,1,0:T(8,128)S(1)}) custom-call(s32[2,48]{1,0:T(2,128)} %bitcast.10, s32[96,256]{1,0:T(8,128)} %bitcast.18, bf16[512,128]{1,0:T(8,128)(2,1)} %bitcast.15, bf16[512,128]{1,0:T(8,128)(2,1)} %bitcast.16, bf16[512,128]{1,0:T(8,128)(2,1)} %bitcast.17), custom_call_target="tpu_custom_call" | custom-call | tf_op jit(solution)/shard_map/pallas_call | solution.py:83
  4.1 8.3 %all-to-all-start = ((bf16[16,128,384]{2,1,0:T(8,128)(2,1)}), bf16[16,128,384]{2,1,0:T(8,128)(2,1)S(1)}, u32[]{:S(2)}, u32[]{:S(2)}) async-start(bf16[16,128,384]{2,1,0:T(8,128)(2,1)} %bitcast.14), calls=%async_computation | async-start | bytes 3145728 | tf_op jit(solution)/shard_map/all_to_all | solution.py:644
  12.5 10.9 %shard_map.69 = (f32[6,256]{1,0:T(8,128)S(1)}, bf16[2,1024,768]{2,1,0:T(8,128)(2,1)}, bf16[2,128,1024]{2,1,0:T(8,128)(2,1)}, f32[8,256]{1,0:T(8,128)S(1)}, bf16[512,2048]{1,0:T(8,128)(2,1)}) custom-call(s32[3,32,256]{2,1,0:T(8,128)S(1)} %get-tuple-element.25.tokens_ref), custom_call_target="tpu_custom_call" | custom-call | tf_op jit(solution)/shard_map/pallas_call | solution.py:83
  23.3 23.3 %all-to-all-done.got_ref = bf16[16,128,384]{2,1,0:T(8,128)(2,1)S(1)} async-done(((bf16[16,128,384]{2,1,0:T(8,128)(2,1)}), bf16[16,128,384]{2,1,0:T(8,128)(2,1)S(1)}, u32[]{:S(2)}, u32[]{:S(2)}) %all-to-all-start) | async-done | bytes 1572896 | tf_op jit(solution)/shard_map/all_to_all | solution.py:644
  46.7 0.0 copy-start.3
  46.7 0.5 shard_map.70.last_ref
  47.2 4.8 %collective-permute-start = (bf16[2,256,256]{2,1,0:T(8,128)(2,1)S(1)}, bf16[2,256,256]{2,1,0:T(8,128)(2,1)S(1)}, u32[]{:S(2)}, u32[]{:S(2)}) collective-permute-start(bf16[2,256,256]{2,1,0:T(8,128)(2,1)S(1)} %shard_map.70.last_ref), channel_id=1, source_target_pairs={{0,8},{8,16},{16,24},{24,26},{26,18},{18,10},{10,2},{2,6},{6,14},{... | collective-permute-start | bytes 786440 | tf_op jit(solution)/shard_map/ppermute | solution.py:650
  52.0 0.5 shard_map.71.first_ref
  52.5 0.1 collective-permute-start.1
  52.5 0.0 copy-done.3
  52.6 0.0 copy-start
  52.6 3.4 %shard_map.72 = (bf16[2,3,256,384]{3,2,1,0:T(8,128)(2,1)S(1)}, bf16[2,3,256,128]{3,2,1,0:T(8,128)(2,1)S(1)}, bf16[2,2,512,256]{3,2,1,0:T(8,128)(2,1)S(1)}, bf16[...) custom-call(s32[2,48]{1,0:T(2,128)S(1)} %bitcast.11, ...), custom_call_target="tpu_custom_call" | custom-call | tf_op jit(solution)/shard_map/pallas_call | solution.py:83
  55.9 0.0 copy-start.2
  55.9 0.0 collective-permute-done.behind_ref
  56.0 1.3 %shard_map.73 = (bf16[2,256,128]{2,1,0:T(8,128)(2,1)S(1)}, bf16[2,512,256]{2,1,0:T(8,128)(2,1)S(1)}, bf16[2,512,256]{2,1,0:T(8,128)(2,1)S(1)}, f32[12,256]{1,0:T(8,128)S(1)}, f32[16,24,128]{2,1,0:T(8,128)S(1)}) custom-call(s32[2,48]{1,0:T(2,128)S(1)} %bitcast.12, bf16[2,3,256,384]{3,2,1,0:T(8,128)(2,1)S(1)} %get-tuple-element.29.rows_ref, ...), custom_call_target="tpu_custom_call" | custom-call | tf_op jit(solution)/shard_map/pallas_call | solution.py:83
  57.3 1.6 %collective-permute-done.1.ahead_ref = bf16[2,256,256]{2,1,0:T(8,128)(2,1)S(1)} collective-permute-done((bf16[2,256,256]{2,1,0:T(8,128)(2,1)S(1)}, bf16[2,256,256]{2,1,0:T(8,128)(2,1)S(1)}, u32[]{:S(2)}, u32[]{:S(2)}) %collective-permute-start.1) | collective-permute-done | bytes 262176 | tf_op jit(solution)/shard_map/ppermute | solution.py:650
  58.9 12.4 %all_to_all.22.everyone_ref = f32[16,24,128]{2,1,0:T(8,128)S(1)} all-to-all(f32[16,24,128]{2,1,0:T(8,128)S(1)} %get-tuple-element.34), channel_id=1, replica_groups=mesh['seq'=16,'head'=2] {'seq'}, dimensions={0} | all-to-all | bytes 393216 | tf_op jit(solution)/shard_map/all_to_all | solution.py:644
  71.3 0.0 copy-done
  71.3 0.0 copy-done.2
  71.3 4.9 %shard_map.74 = bf16[16,128,256]{2,1,0:T(8,128)(2,1)S(1)} custom-call(s32[2,48]{1,0:T(2,128)S(1)} %bitcast.13, f32[16,24,128]{2,1,0:T(8,128)S(1)} %all_to_all.22.everyone_ref, bf16[2,128,1024]{2,1,0:T(8,128)(2,1)S(1)} %copy-done.2, f32[8,256]{1,0:T(8,128)S(1)} %get-tuple-element.36.low_ref, f32[12,256]{1,0:T(8,128)S(1)} %get-tuple-element.37.sums_ref, ...), custom_call_target="tpu_custom_call" | custom-call | tf_op jit(solution)/shard_map/pallas_call | solution.py:83
  76.2 0.0 copy-start.1
  76.2 26.4 %all_to_all.23 = bf16[16,128,256]{2,1,0:T(8,128)(2,1)S(1)} all-to-all(bf16[16,128,256]{2,1,0:T(8,128)(2,1)S(1)} %shard_map.74), channel_id=1, replica_groups=mesh['seq'=16,'head'=2] {'seq'}, dimensions={0} | all-to-all | bytes 2097152 | tf_op jit(solution)/shard_map/all_to_all | solution.py:644
  102.6 0.0 copy-done.1
  102.6 1.4 %shard_map.75 = (bf16[512,128]{1,0:T(8,128)(2,1)}, bf16[512,128]{1,0:T(8,128)(2,1)}) custom-call(bf16[512,2048]{1,0:T(8,128)(2,1)S(1)} %copy-done.1, bf16[2048,256]{1,0:T(8,128)(2,1)S(1)} %bitcast.9), custom_call_target="tpu_custom_call" | custom-call | tf_op jit(solution)/shard_map/pallas_call | solution.py:83
Async XLA Ops:
  4.1 42.5 %all-to-all-start = ((bf16[16,128,384]{2,1,0:T(8,128)(2,1)}), bf16[16,128,384]{2,1,0:T(8,128)(2,1)S(1)}, u32[]{:S(2)}, u32[]{:S(2)}) async-start(bf16[16,128,384]{2,1,0:T(8,128)(2,1)} %bitcast.14), calls=%async_computation | async-start | bytes 3145728 | tf_op jit(solution)/shard_map/all_to_all | solution.py:644
  46.7 5.9 %copy-start.3 = (s32[1,2,48]{2,1,0:T(2,128)S(1)}, s32[1,2,48]{2,1,0:T(2,128)}, u32[]{:S(2)}) copy-start(s32[1,2,48]{2,1,0:T(2,128)} %param.9) | copy-start | bytes 1156
  47.2 8.8 %collective-permute-start = (bf16[2,256,256]{2,1,0:T(8,128)(2,1)S(1)}, bf16[2,256,256]{2,1,0:T(8,128)(2,1)S(1)}, u32[]{:S(2)}, u32[]{:S(2)}) collective-permute-start(bf16[2,256,256]{2,1,0:T(8,128)(2,1)S(1)} %shard_map.70.last_ref), channel_id=1, source_target_pairs={{0,8},{8,16},{16,24},{24,26},{26,18},{18,10},{10,2},{2,6},{6,14},{... | collective-permute-start | bytes 786440 | tf_op jit(solution)/shard_map/ppermute | solution.py:650
  52.5 6.4 %collective-permute-start.1 = (bf16[2,256,256]{2,1,0:T(8,128)(2,1)S(1)}, bf16[2,256,256]{2,1,0:T(8,128)(2,1)S(1)}, u32[]{:S(2)}, u32[]{:S(2)}) collective-permute-start(bf16[2,256,256]{2,1,0:T(8,128)(2,1)S(1)} %shard_map.71.first_ref), channel_id=1, source_target_pairs={{0,4},{8,0},{16,8},{24,16},{26,24},{18,26},{10,18},{2,10},{6,2},{1... | collective-permute-start | bytes 786440 | tf_op jit(solution)/shard_map/ppermute | solution.py:650
  52.6 18.7 %copy-start = (bf16[2,1024,768]{2,1,0:T(8,128)(2,1)S(1)}, bf16[2,1024,768]{2,1,0:T(8,128)(2,1)}, u32[]{:S(2)}) copy-start(bf16[2,1024,768]{2,1,0:T(8,128)(2,1)} %get-tuple-element.45.spread_t_ref) | copy-start | bytes 9437188
  55.9 15.4 %copy-start.2 = (bf16[2,128,1024]{2,1,0:T(8,128)(2,1)S(1)}, bf16[2,128,1024]{2,1,0:T(8,128)(2,1)}, u32[]{:S(2)}) copy-start(bf16[2,128,1024]{2,1,0:T(8,128)(2,1)} %get-tuple-element.35.partner_ref) | copy-start | bytes 1572868
  76.2 26.4 %copy-start.1 = (bf16[512,2048]{1,0:T(8,128)(2,1)S(1)}, bf16[512,2048]{1,0:T(8,128)(2,1)}, u32[]{:S(2)}) copy-start(bf16[512,2048]{1,0:T(8,128)(2,1)} %get-tuple-element.26.home_ref) | copy-start | bytes 6291460

commit v3 on v2

--- a/solution.py
+++ b/solution.py
@@ -68,14 +68,12 @@
     return one_hot(iota((size, size), 0) < iota((size, size), 1))
 
 
-def call(kernel, out_shapes, operands, scratch=(), scalars=0, remote=0, semaphores=0, far=(), direct=()):
+def call(kernel, out_shapes, operands, scratch=(), remote=0, semaphores=0, far=(), direct=()):
     count = len(operands)
-    held = sum(array.size * array.dtype.itemsize for array in operands[scalars : count - remote])
+    held = sum(array.size * array.dtype.itemsize for array in operands[: count - remote])
     for shape, dtype in list(out_shapes) + list(scratch):
         held += math.prod(shape) * jnp.dtype(dtype).itemsize
-    spaces = (
-        [pltpu.SMEM] * scalars + [pltpu.VMEM] * (count - scalars - remote) + [pltpu.HBM] * remote
-    )
+    spaces = [pltpu.VMEM] * (count - remote) + [pltpu.HBM] * remote
     operands = [
         pltpu.with_memory_space_constraint(array, space) if space is pltpu.HBM else array
         for array, space in zip(operands, spaces)
@@ -210,6 +208,7 @@
     token_count,
     tokens_ref,
     place_ref,
+    fill_ref,
     spread_t_ref,
     partner_ref,
     low_ref,
@@ -240,6 +239,16 @@
             span = pl.ds(group * cap, cap)
             spread_t_ref[r, :, span] = one_hot(place == place_column)
             place_ref[pl.ds(r * per_device + group, 1), :] = place
+
+    behind = lax.rem(me + devices - 1, devices)
+    for r in range(rounds):
+        for at in range(per_device + 2):
+            block = behind if at == 0 else after if at > per_device else me
+            group = (at - 1) % per_device
+            tokens = tokens_ref[group, pl.ds(r * devices + block, 1), :]
+            fill = jnp.sum(jnp.where(tokens >= 0, 1.0, 0.0), axis=1, keepdims=True)
+            row = r * (per_device + 2) + at
+            fill_ref[row : row + 1, :] = jnp.broadcast_to(fill, (1, cap))
 
     high_count = devices * token_count // lane
     high_start = iota((high_count, cap), 0) * lane
@@ -328,19 +337,13 @@
     return got_ref[:, r * bound : (r + 1) * bound, :].reshape(devices * bound, width)
 
 
-def last_kernel(rounds, got_ref, place_ref, last_ref):
+def ends_kernel(rounds, got_ref, place_ref, last_ref, first_ref):
     size = got_ref.shape[2] // 3
     per_device = place_ref.shape[0] // rounds
     for r in range(rounds):
         received = received_rows(got_ref, r, rounds)
         spread = spread_of(place_ref, r, per_device - 1, rounds, received.shape[0])
         last_ref[r] = dot_tn(spread, received[:, : 2 * size]).astype(bf16)
-
-
-def first_kernel(rounds, got_ref, place_ref, first_ref):
-    size = got_ref.shape[2] // 3
-    for r in range(rounds):
-        received = received_rows(got_ref, r, rounds)
         spread = spread_of(place_ref, r, 0, rounds, received.shape[0])
         wanted = jnp.concatenate([received[:, :size], received[:, 2 * size :]], axis=1)
         first_ref[r] = dot_tn(spread, wanted).astype(bf16)
@@ -355,12 +358,17 @@
     return (rows.astype(f32) * inverse_norm(rows)).astype(bf16)
 
 
+def fill_row(fill_ref, r, at, rounds):
+    row = r * (fill_ref.shape[0] // rounds) + at
+    return fill_ref[row : row + 1, :]
+
+
 def scored(unit, queries, fill, own):
     cap = queries.shape[0]
-    key = iota((cap, cap), 0)
+    key = float_iota((cap, cap), 0)
     allowed = key < fill
     if own:
-        allowed = allowed & (key != iota((cap, cap), 1))
+        allowed = allowed & (key != float_iota((cap, cap), 1))
     return jnp.where(allowed, dot_nt(unit, queries), masked_score)
 
 
@@ -380,8 +388,7 @@
 
 def forward_inner_kernel(
     rounds,
-    devices,
-    counts_ref,
+    fill_ref,
     got_ref,
     place_ref,
     last_ref,
@@ -397,7 +404,6 @@
     cap = prob_ref.shape[3]
     per_device = rows_ref.shape[1]
     size = rows_ref.shape[3] // 3
-    base = block_of(lax.axis_index("seq"), devices) * per_device
     for r in range(rounds):
         received = received_rows(got_ref, r, rounds)
         for group in range(per_device):
@@ -420,7 +426,9 @@
             queries = rows_ref[r, group, :, :size]
             cot = rows_ref[r, group, :, 2 * size :]
             values = rows_ref[r, group, :, size : 2 * size]
-            score_now = scored(units[group], queries, counts_ref[r, base + group], True)
+            score_now = scored(
+                units[group], queries, fill_row(fill_ref, r, group + 1, rounds), True
+            )
             inner_now = dot_nt(values, cot)
             if group == 0:
                 first_score_ref[r] = score_now
@@ -429,7 +437,7 @@
             values = rows_ref[r, group - 1, :, size : 2 * size]
             inner_before = dot_nt(values, cot)
             score_before = scored(
-                units[group - 1], queries, counts_ref[r, base + group - 1], False
+                units[group - 1], queries, fill_row(fill_ref, r, group, rounds), False
             )
             inners = [inner_before, inner_now]
             log_total, dots, probs = normalised([score_before, score_now], inners)
@@ -446,7 +454,7 @@
 def forward_first_kernel(
     rounds,
     devices,
-    counts_ref,
+    fill_ref,
     rows_ref,
     behind_ref,
     score_ref,
@@ -462,16 +470,13 @@
     cap = prob_ref.shape[2]
     per_device = rows_ref.shape[1]
     size = rows_ref.shape[3] // 3
-    groups = counts_ref.shape[1]
-    base = block_of(lax.axis_index("seq"), devices) * per_device
-    before = lax.rem(base + groups - 1, groups)
     sums_ref[...] = inner_sums_ref[...]
     for r in range(rounds):
         behind_unit = unit_rows(behind_ref[r, :, :size])
         unit_ref[r] = behind_unit
         queries = rows_ref[r, 0, :, :size]
         cot = rows_ref[r, 0, :, 2 * size :]
-        score_before = scored(behind_unit, queries, counts_ref[r, before], False)
+        score_before = scored(behind_unit, queries, fill_row(fill_ref, r, 0, rounds), False)
         inners = [dot_nt(behind_ref[r, :, size:], cot), inner_now_ref[r]]
         log_total, dots, probs = normalised([score_before, score_ref[r]], inners)
         for side in range(2):
@@ -516,7 +521,7 @@
     rounds,
     devices,
     bound,
-    counts_ref,
+    fill_ref,
     everyone_ref,
     partner_ref,
     low_ref,
@@ -536,14 +541,13 @@
     cap = rows_ref.shape[2]
     per_device = rows_ref.shape[1]
     size = rows_ref.shape[3] // 3
-    groups = counts_ref.shape[1]
     me = block_of(lax.axis_index("seq"), devices)
     ahead_device = device_of(lax.rem(me + 1, devices), devices)
     halves = cap // lane
     count = per_device * halves
     kept = table_kept(count)
     low_column = float_iota((lane, cap), 0)
-    slot = iota((1, cap), 1)
+    slot = float_iota((1, cap), 1)
 
     def sums_of_all(r, kind):
         start = (2 * r + kind) * count
@@ -585,7 +589,7 @@
             weight = 1.0 / (1.0 + jnp.exp(other_log - own_log))
             other_weight = 1.0 / (1.0 + jnp.exp(own_log - other_log))
             mixture = weight * own_dot + other_weight * other_dot
-            valid = slot < counts_ref[r, lax.rem(me * per_device + group, groups)]
+            valid = slot < fill_row(fill_ref, r, group + 1, rounds)
             scales.append((jnp.where(valid, weight, 0.0), jnp.where(valid, mixture, 0.0)))
 
         def score_grads(prob, inner, scale):
@@ -610,7 +614,7 @@
                 probs = [prob_ref[r, group - 1, :cap, :], prob_ref[r, group - 1, cap:, :]]
                 inners = [inner_ref[r, group - 1, :cap, :], inner_ref[r, group - 1, cap:, :]]
             else:
-                fill = counts_ref[r, me * per_device + per_device - 1]
+                fill = fill_row(fill_ref, r, per_device, rounds)
                 score = scored(units_ref[r, per_device - 1], queries, fill, False)
                 probs = [jnp.exp(score - ahead_log)]
                 inners = [dot_nt(rows_ref[r, per_device - 1][:, size : 2 * size], cot)]
@@ -680,10 +684,11 @@
         direct=(0,),
     )
     got = exchange(send).reshape(devices, span, 3 * size)
-    place, spread_t, partner, low, home_pick = call(
+    place, fill, spread_t, partner, low, home_pick = call(
         functools.partial(index_kernel, rounds, devices, bound, token_count),
         [
             ((rounds * per_device, cap), f32),
+            ((rounds * (per_device + 2), cap), f32),
             ((rounds, buffer_rows, slots), bf16),
             ((rounds, devices * table_kept(slots // lane), slots + cap), bf16),
             ((rounds * (per_device + 1), cap), f32),
@@ -691,19 +696,18 @@
         ],
         [tokens],
         [((rounds, 2 * devices * token_count // lane, lane), bf16), pick] + keys,
-        far=(1, 2, 4),
-    )
-    (last,) = call(
-        functools.partial(last_kernel, rounds), [((rounds, cap, 2 * size), bf16)], [got, place]
+        far=(2, 3, 5),
+    )
+    last, first = call(
+        functools.partial(ends_kernel, rounds),
+        [((rounds, cap, 2 * size), bf16)] * 2,
+        [got, place],
     )
     behind = shifted(last, 1)
-    (first,) = call(
-        functools.partial(first_kernel, rounds), [((rounds, cap, 2 * size), bf16)], [got, place]
-    )
     ahead = shifted(first, -1)
     square = (rounds, cap, cap)
     rows, units, prob, inner, first_score, first_inner_now, inner_sums = call(
-        functools.partial(forward_inner_kernel, rounds, devices),
+        functools.partial(forward_inner_kernel, rounds),
         [
             ((rounds, per_device, cap, 3 * size), bf16),
             ((rounds, per_device, cap, size), bf16),
@@ -713,8 +717,7 @@
             (square, f32),
             ((sum_rows, cap), f32),
         ],
-        [counts, got, place, last, first],
-        scalars=1,
+        [fill, got, place, last, first],
     )
     behind_unit, first_prob, first_inner, sums, sums_send = call(
         functools.partial(forward_first_kernel, rounds, devices),
@@ -725,9 +728,8 @@
             ((sum_rows, cap), f32),
             ((devices, sum_rows * cap // lane, lane), f32),
         ],
-        [counts, rows, behind, first_score, first_inner_now, inner_sums],
+        [fill, rows, behind, first_score, first_inner_now, inner_sums],
         [((sum_rows * cap // lane, lane), f32)],
-        scalars=1,
     )
     sums_send, ahead = lax.optimization_barrier((sums_send, ahead))
     everyone = exchange(sums_send)
@@ -735,7 +737,7 @@
         functools.partial(backward_kernel, rounds, devices, bound),
         [((devices, span, 2 * size), bf16)],
         [
-            counts,
+            fill,
             everyone,
             partner,
             low,
@@ -751,7 +753,6 @@
             spread_t,
         ],
         [((slots, 2 * size), bf16)],
-        scalars=1,
     )
     home = exchange(grads_send.reshape(devices * span, 2 * size))
     return call(

time: 104 us -> 103 us (level)
  Pallas kernels: 26.3 us -> 24.2 us
  waiting for transfers between devices: 25 us -> 26.1 us
    pallas_call x8 -> x7, Pallas kernels: 26.3 us -> 24.2 us  [call(): pl.pallas_call(kernel, out_shape=tuple((pltpu.HBM(shape, dtype) if at in...]
    ppermute x2, waiting for transfers between devices: 1.64 us -> 2.76 us  [shifted(): lax.ppermute(array, 'seq', [(order[i], order[(i + by) % devices]) for i i...]
  transfers between devices with their start and end apart: 3 -> 3, of which waited for: 2 -> 3; matrix products, arithmetic and copies ran while one was open for 0% -> 0% of each run, Pallas kernels for 15% -> 14%
where the time goes in v3:
time: 103 us
  blocking collectives  38.8 us (38%)
  waiting for transfers between devices  26.1 us (25%)
  Pallas kernels  24.2 us (23%)
  starting transfers between devices  13.2 us (13%)
    all_to_all x2, blocking collectives, exchange(): return lax.all_to_all(array, 'seq', split_axis=0, concat_axis=0, tiled=True)  38.8 us
    pallas_call x7, Pallas kernels, call(): pl.pallas_call(kernel, out_shape=tuple((pltpu.HBM(shape, dtype) if at in...  24.2 us
    all_to_all x1, waiting for transfers between devices, exchange(): return lax.all_to_all(array, 'seq', split_axis=0, concat_axis=0, tiled=True)  23.3 us
    all_to_all x1, starting transfers between devices, exchange(): return lax.all_to_all(array, 'seq', split_axis=0, concat_axis=0, tiled=True)  8.32 us
    ppermute x2, starting transfers between devices, shifted(): lax.ppermute(array, 'seq', [(order[i], order[(i + by) % devices]) for i i...  4.83 us
    ppermute x2, waiting for transfers between devices, shifted(): lax.ppermute(array, 'seq', [(order[i], order[(i + by) % devices]) for i i...  2.76 us
  transfers between devices with their start and end apart: 3, of which 3 were waited for; matrix products, arithmetic and copies ran while one was open for 0% of the time, Pallas kernels for 14%

profile of v3, /device:TPU:0, one launch (start us, length us, event | category | flops | bytes accessed | tf_op | source)
XLA Modules:
  0.0 103.0 jit_solution(5020490490546927861)
XLA Ops:
  0.6 3.5 %shard_map.68 = (bf16[2048,384]{1,0:T(8,128)(2,1)}, s32[3,32,256]{2,1,0:T(8,128)S(1)}) custom-call(s32[2,48]{1,0:T(2,128)} %bitcast.15, s32[96,256]{1,0:T(8,128)} %bitcast.14, bf16[512,128]{1,0:T(8,128)(2,1)} %bitcast.11, bf16[512,128]{1,0:T(8,128)(2,1)} %bitcast.12, bf16[512,128]{1,0:T(8,128)(2,1)} %bitcast.13), custom_call_target="tpu_custom_call" | custom-call | tf_op jit(solution)/shard_map/pallas_call | solution.py:81
  4.1 8.3 %all-to-all-start = ((bf16[16,128,384]{2,1,0:T(8,128)(2,1)}), bf16[16,128,384]{2,1,0:T(8,128)(2,1)S(1)}, u32[]{:S(2)}, u32[]{:S(2)}) async-start(bf16[16,128,384]{2,1,0:T(8,128)(2,1)} %bitcast.10), calls=%async_computation | async-start | bytes 3145728 | tf_op jit(solution)/shard_map/all_to_all | solution.py:648
  12.5 10.9 %shard_map.69 = (f32[6,256]{1,0:T(8,128)S(1)}, f32[10,256]{1,0:T(8,128)S(1)}, bf16[2,1024,768]{2,1,0:T(8,128)(2,1)}, bf16[2,128,1024]{2,1,0:T(8,128)(2,1)}, f32[...) custom-call(s32[3,32,256]{2,1,0:T(8,128)S(1)} %get-tuple-element.28.tokens_ref), custom_call_target="tpu_custom_call" | custom-call | tf_op jit(solution)/shard_map/pallas_call | solution.py:81
  23.4 23.3 %all-to-all-done.got_ref = bf16[16,128,384]{2,1,0:T(8,128)(2,1)S(1)} async-done(((bf16[16,128,384]{2,1,0:T(8,128)(2,1)}), bf16[16,128,384]{2,1,0:T(8,128)(2,1)S(1)}, u32[]{:S(2)}, u32[]{:S(2)}) %all-to-all-start) | async-done | bytes 1572896 | tf_op jit(solution)/shard_map/all_to_all | solution.py:648
  46.7 0.8 shard_map.70
  47.4 4.8 %collective-permute-start = (bf16[2,256,256]{2,1,0:T(8,128)(2,1)S(1)}, bf16[2,256,256]{2,1,0:T(8,128)(2,1)S(1)}, u32[]{:S(2)}, u32[]{:S(2)}) collective-permute-start(bf16[2,256,256]{2,1,0:T(8,128)(2,1)S(1)} %get-tuple-element.33.last_ref), channel_id=1, source_target_pairs={{0,8},{8,16},{16,24},{24,26},{26,18},{18,10},{10,2},{2,6},{6,14},{... | collective-permute-start | bytes 786440 | tf_op jit(solution)/shard_map/ppermute | solution.py:654
  52.3 0.0 collective-permute-start.1
  52.3 0.0 copy-start
  52.3 2.8 %shard_map.71 = (bf16[2,3,256,384]{3,2,1,0:T(8,128)(2,1)S(1)}, bf16[2,3,256,128]{3,2,1,0:T(8,128)(2,1)S(1)}, bf16[2,2,512,256]{3,2,1,0:T(8,128)(2,1)S(1)}, bf16[...) custom-call(f32[10,256]{1,0:T(8,128)S(1)} %get-tuple-element.30.fill, ...), custom_call_target="tpu_custom_call" | custom-call | tf_op jit(solution)/shard_map/pallas_call | solution.py:81
  55.1 0.0 copy-start.2
  55.1 1.0 %collective-permute-done.behind_ref = bf16[2,256,256]{2,1,0:T(8,128)(2,1)S(1)} collective-permute-done((bf16[2,256,256]{2,1,0:T(8,128)(2,1)S(1)}, bf16[2,256,256]{2,1,0:T(8,128)(2,1)S(1)}, u32[]{:S(2)}, u32[]{:S(2)}) %collective-permute-start) | collective-permute-done | bytes 262176 | tf_op jit(solution)/shard_map/ppermute | solution.py:654
  56.1 0.8 shard_map.72
  56.9 1.7 %collective-permute-done.1.ahead_ref = bf16[2,256,256]{2,1,0:T(8,128)(2,1)S(1)} collective-permute-done((bf16[2,256,256]{2,1,0:T(8,128)(2,1)S(1)}, bf16[2,256,256]{2,1,0:T(8,128)(2,1)S(1)}, u32[]{:S(2)}, u32[]{:S(2)}) %collective-permute-start.1) | collective-permute-done | bytes 262176 | tf_op jit(solution)/shard_map/ppermute | solution.py:654
  58.6 12.4 %all_to_all.22.everyone_ref = f32[16,24,128]{2,1,0:T(8,128)S(1)} all-to-all(f32[16,24,128]{2,1,0:T(8,128)S(1)} %get-tuple-element.40), channel_id=1, replica_groups=mesh['seq'=16,'head'=2] {'seq'}, dimensions={0} | all-to-all | bytes 393216 | tf_op jit(solution)/shard_map/all_to_all | solution.py:648
  71.0 0.0 copy-done
  71.0 0.0 copy-done.2
  71.0 4.1 %shard_map.73 = bf16[16,128,256]{2,1,0:T(8,128)(2,1)S(1)} custom-call(f32[10,256]{1,0:T(8,128)S(1)} %get-tuple-element.30.fill_ref, f32[16,24,128]{2,1,0:T(8,128)S(1)} %all_to_all.22.everyone_ref, bf16[2,128,1024]{2,1,0:T(8,128)(2,1)S(1)} %copy-done.2, f32[8,256]{1,0:T(8,128)S(1)} %get-tuple-element.42.low_ref, f32[12,256]{1,0:T(8,128)S(1)} %get-tuple-element.43.sums_ref, ...), custom_call_target="tpu_custom_call" | custom-call | tf_op jit(solution)/shard_map/pallas_call | solution.py:81
  75.1 0.0 copy-start.1
  75.1 26.4 %all_to_all.23 = bf16[16,128,256]{2,1,0:T(8,128)(2,1)S(1)} all-to-all(bf16[16,128,256]{2,1,0:T(8,128)(2,1)S(1)} %shard_map.73), channel_id=1, replica_groups=mesh['seq'=16,'head'=2] {'seq'}, dimensions={0} | all-to-all | bytes 2097152 | tf_op jit(solution)/shard_map/all_to_all | solution.py:648
  101.5 0.0 copy-done.1
  101.5 1.4 %shard_map.74 = (bf16[512,128]{1,0:T(8,128)(2,1)}, bf16[512,128]{1,0:T(8,128)(2,1)}) custom-call(bf16[512,2048]{1,0:T(8,128)(2,1)S(1)} %copy-done.1, bf16[2048,256]{1,0:T(8,128)(2,1)S(1)} %bitcast.9), custom_call_target="tpu_custom_call" | custom-call | tf_op jit(solution)/shard_map/pallas_call | solution.py:81
Async XLA Ops:
  4.1 42.5 %all-to-all-start = ((bf16[16,128,384]{2,1,0:T(8,128)(2,1)}), bf16[16,128,384]{2,1,0:T(8,128)(2,1)S(1)}, u32[]{:S(2)}, u32[]{:S(2)}) async-start(bf16[16,128,384]{2,1,0:T(8,128)(2,1)} %bitcast.10), calls=%async_computation | async-start | bytes 3145728 | tf_op jit(solution)/shard_map/all_to_all | solution.py:648
  47.4 8.7 %collective-permute-start = (bf16[2,256,256]{2,1,0:T(8,128)(2,1)S(1)}, bf16[2,256,256]{2,1,0:T(8,128)(2,1)S(1)}, u32[]{:S(2)}, u32[]{:S(2)}) collective-permute-start(bf16[2,256,256]{2,1,0:T(8,128)(2,1)S(1)} %get-tuple-element.33.last_ref), channel_id=1, source_target_pairs={{0,8},{8,16},{16,24},{24,26},{26,18},{18,10},{10,2},{2,6},{6,14},{... | collective-permute-start | bytes 786440 | tf_op jit(solution)/shard_map/ppermute | solution.py:654
  52.3 6.4 %collective-permute-start.1 = (bf16[2,256,256]{2,1,0:T(8,128)(2,1)S(1)}, bf16[2,256,256]{2,1,0:T(8,128)(2,1)S(1)}, u32[]{:S(2)}, u32[]{:S(2)}) collective-permute-start(bf16[2,256,256]{2,1,0:T(8,128)(2,1)S(1)} %get-tuple-element.34.first_ref), channel_id=1, source_target_pairs={{0,4},{8,0},{16,8},{24,16},{26,24},{18,26},{10,18},{2,10},{6,2},{1... | collective-permute-start | bytes 786440 | tf_op jit(solution)/shard_map/ppermute | solution.py:654
  52.3 18.8 %copy-start = (bf16[2,1024,768]{2,1,0:T(8,128)(2,1)S(1)}, bf16[2,1024,768]{2,1,0:T(8,128)(2,1)}, u32[]{:S(2)}) copy-start(bf16[2,1024,768]{2,1,0:T(8,128)(2,1)} %get-tuple-element.51.spread_t_ref) | copy-start | bytes 9437188
  55.1 15.9 %copy-start.2 = (bf16[2,128,1024]{2,1,0:T(8,128)(2,1)S(1)}, bf16[2,128,1024]{2,1,0:T(8,128)(2,1)}, u32[]{:S(2)}) copy-start(bf16[2,128,1024]{2,1,0:T(8,128)(2,1)} %get-tuple-element.41.partner_ref) | copy-start | bytes 1572868
  75.1 26.4 %copy-start.1 = (bf16[512,2048]{1,0:T(8,128)(2,1)S(1)}, bf16[512,2048]{1,0:T(8,128)(2,1)}, u32[]{:S(2)}) copy-start(bf16[512,2048]{1,0:T(8,128)(2,1)} %get-tuple-element.29.home_ref) | copy-start | bytes 6291460

commit v4 on v3

--- a/solution.py
+++ b/solution.py
@@ -564,7 +564,7 @@
         rows = [everyone_ref[ahead_device, start + h : start + h + 1, :] for h in range(halves)]
         return jnp.concatenate(rows, axis=1)
 
-    for r in range(rounds):
+    def scales_of(r):
         logs = three_parts(sums_of_all(1 - r, 0))
         dots = three_parts(sums_of_all(1 - r, 1))
         upright = jnp.concatenate(logs + dots[:2], axis=0)
@@ -585,28 +585,28 @@
             else:
                 own_log = ahead_sums(r, 0)
                 own_dot = ahead_sums(r, 1)
-                ahead_log = own_log
             weight = 1.0 / (1.0 + jnp.exp(other_log - own_log))
             other_weight = 1.0 / (1.0 + jnp.exp(own_log - other_log))
             mixture = weight * own_dot + other_weight * other_dot
             valid = slot < fill_row(fill_ref, r, group + 1, rounds)
             scales.append((jnp.where(valid, weight, 0.0), jnp.where(valid, mixture, 0.0)))
-
-        def score_grads(prob, inner, scale):
-            weighted = prob.astype(f32) * scale[0]
-            score_grad = (weighted * (inner.astype(f32) - scale[1])).astype(bf16)
-            return weighted.astype(bf16), score_grad
-
-        query_grad = None
-        unit_grad = None
-        value_grad = None
-        for group in range(per_device + 1):
+        return scales
+
+    def score_grads(prob, inner, scale):
+        weighted = prob.astype(f32) * scale[0]
+        score_grad = (weighted * (inner.astype(f32) - scale[1])).astype(bf16)
+        return weighted.astype(bf16), score_grad
+
+    scales = [scales_of(r) for r in range(rounds)]
+    carried = [None] * rounds
+    for group in range(per_device + 1):
+        for r in range(rounds):
             if group < per_device:
-                queries = rows_ref[r, group][:, :size]
-                cot = rows_ref[r, group][:, 2 * size :]
+                queries = rows_ref[r, group, :, :size]
+                cot = rows_ref[r, group, :, 2 * size :]
             else:
-                queries = ahead_ref[r][:, :size]
-                cot = ahead_ref[r][:, size:]
+                queries = ahead_ref[r, :, :size]
+                cot = ahead_ref[r, :, size:]
             if group == 0:
                 probs = [first_prob_ref[r, :cap, :], first_prob_ref[r, cap:, :]]
                 inners = [first_inner_ref[r, :cap, :], first_inner_ref[r, cap:, :]]
@@ -616,24 +616,27 @@
             else:
                 fill = fill_row(fill_ref, r, per_device, rounds)
                 score = scored(units_ref[r, per_device - 1], queries, fill, False)
-                probs = [jnp.exp(score - ahead_log)]
-                inners = [dot_nt(rows_ref[r, per_device - 1][:, size : 2 * size], cot)]
-            weighted, score_grad = score_grads(probs[0], inners[0], scales[group])
+                probs = [jnp.exp(score - ahead_sums(r, 0))]
+                inners = [dot_nt(rows_ref[r, per_device - 1, :, size : 2 * size], cot)]
+            scale = scales[r][group]
+            weighted, score_grad = score_grads(probs[0], inners[0], scale)
             if group > 0:
+                query_grad, unit_grad, value_grad = carried[r]
                 unit_grad = unit_grad + dot_nn(score_grad, queries)
                 value_grad = value_grad + dot_nn(weighted, cot)
-                key_part = key_grad(rows_ref[r, group - 1][:, :size], unit_grad)
+                key_part = key_grad(rows_ref[r, group - 1, :, :size], unit_grad)
                 span = slice((group - 1) * cap, group * cap)
-                grads_ref[span, :size] = (query_grad + key_part).astype(bf16)
-                grads_ref[span, size:] = value_grad.astype(bf16)
+                grads_ref[r, span, :size] = (query_grad + key_part).astype(bf16)
+                grads_ref[r, span, size:] = value_grad.astype(bf16)
             if group < per_device:
                 unit_before = behind_unit_ref[r] if group == 0 else units_ref[r, group - 1]
                 query_grad = dot_tn(score_grad, unit_before)
-                weighted, score_grad = score_grads(probs[1], inners[1], scales[group])
+                weighted, score_grad = score_grads(probs[1], inners[1], scale)
                 query_grad = query_grad + dot_tn(score_grad, units_ref[r, group])
                 unit_grad = dot_nn(score_grad, queries)
-                value_grad = dot_nn(weighted, cot)
-        packed = dot_nn(spread_t_ref[r], grads_ref[...]).astype(bf16)
+                carried[r] = (query_grad, unit_grad, dot_nn(weighted, cot))
+    for r in range(rounds):
+        packed = dot_nn(spread_t_ref[r], grads_ref[r]).astype(bf16)
         send_ref[:, r * bound : (r + 1) * bound, :] = packed.reshape(devices, bound, 2 * size)
 
 
@@ -752,7 +755,7 @@
             inner,
             spread_t,
         ],
-        [((slots, 2 * size), bf16)],
+        [((rounds, slots, 2 * size), bf16)],
     )
     home = exchange(grads_send.reshape(devices * span, 2 * size))
     return call(

time: 103 us -> 103 us (level)
  no operation moved by 1% of the time
where the time goes in v4:
time: 103 us; the launch traced here: 102 us
  blocking collectives  38.8 us (38%)
  waiting for transfers between devices  26.1 us (25%)
  Pallas kernels  23.6 us (23%)
  starting transfers between devices  13.2 us (13%)
    all_to_all x2, blocking collectives, exchange(): return lax.all_to_all(array, 'seq', split_axis=0, concat_axis=0, tiled=True)  38.8 us
    pallas_call x7, Pallas kernels, call(): pl.pallas_call(kernel, out_shape=tuple((pltpu.HBM(shape, dtype) if at in...  23.6 us
    all_to_all x1, waiting for transfers between devices, exchange(): return lax.all_to_all(array, 'seq', split_axis=0, concat_axis=0, tiled=True)  23.3 us
    all_to_all x1, starting transfers between devices, exchange(): return lax.all_to_all(array, 'seq', split_axis=0, concat_axis=0, tiled=True)  8.32 us
    ppermute x2, starting transfers between devices, shifted(): lax.ppermute(array, 'seq', [(order[i], order[(i + by) % devices]) for i i...  4.83 us
    ppermute x2, waiting for transfers between devices, shifted(): lax.ppermute(array, 'seq', [(order[i], order[(i + by) % devices]) for i i...  2.76 us
  transfers between devices with their start and end apart: 3, of which 3 were waited for; matrix products, arithmetic and copies ran while one was open for 0% of the time, Pallas kernels for 14%

profile of v4, /device:TPU:0, one launch (start us, length us, event | category | flops | bytes accessed | tf_op | source)
XLA Modules:
  0.0 102.3 jit_solution(16374898174868985569)
XLA Ops:
  0.6 3.5 %shard_map.68 = (bf16[2048,384]{1,0:T(8,128)(2,1)}, s32[3,32,256]{2,1,0:T(8,128)S(1)}) custom-call(s32[2,48]{1,0:T(2,128)} %bitcast.15, s32[96,256]{1,0:T(8,128)} %bitcast.14, bf16[512,128]{1,0:T(8,128)(2,1)} %bitcast.11, bf16[512,128]{1,0:T(8,128)(2,1)} %bitcast.12, bf16[512,128]{1,0:T(8,128)(2,1)} %bitcast.13), custom_call_target="tpu_custom_call" | custom-call | tf_op jit(solution)/shard_map/pallas_call | solution.py:81
  4.1 8.3 %all-to-all-start = ((bf16[16,128,384]{2,1,0:T(8,128)(2,1)}), bf16[16,128,384]{2,1,0:T(8,128)(2,1)S(1)}, u32[]{:S(2)}, u32[]{:S(2)}) async-start(bf16[16,128,384]{2,1,0:T(8,128)(2,1)} %bitcast.10), calls=%async_computation | async-start | bytes 3145728 | tf_op jit(solution)/shard_map/all_to_all | solution.py:651
  12.5 10.9 %shard_map.69 = (f32[6,256]{1,0:T(8,128)S(1)}, f32[10,256]{1,0:T(8,128)S(1)}, bf16[2,1024,768]{2,1,0:T(8,128)(2,1)}, bf16[2,128,1024]{2,1,0:T(8,128)(2,1)}, f32[...) custom-call(s32[3,32,256]{2,1,0:T(8,128)S(1)} %get-tuple-element.28.tokens_ref), custom_call_target="tpu_custom_call" | custom-call | tf_op jit(solution)/shard_map/pallas_call | solution.py:81
  23.4 23.3 %all-to-all-done.got_ref = bf16[16,128,384]{2,1,0:T(8,128)(2,1)S(1)} async-done(((bf16[16,128,384]{2,1,0:T(8,128)(2,1)}), bf16[16,128,384]{2,1,0:T(8,128)(2,1)S(1)}, u32[]{:S(2)}, u32[]{:S(2)}) %all-to-all-start) | async-done | bytes 1572896 | tf_op jit(solution)/shard_map/all_to_all | solution.py:651
  46.7 0.8 shard_map.70
  47.4 4.8 %collective-permute-start = (bf16[2,256,256]{2,1,0:T(8,128)(2,1)S(1)}, bf16[2,256,256]{2,1,0:T(8,128)(2,1)S(1)}, u32[]{:S(2)}, u32[]{:S(2)}) collective-permute-start(bf16[2,256,256]{2,1,0:T(8,128)(2,1)S(1)} %get-tuple-element.33.last_ref), channel_id=1, source_target_pairs={{0,8},{8,16},{16,24},{24,26},{26,18},{18,10},{10,2},{2,6},{6,14},{... | collective-permute-start | bytes 786440 | tf_op jit(solution)/shard_map/ppermute | solution.py:657
  52.3 0.0 collective-permute-start.1
  52.3 0.0 copy-start
  52.3 2.8 %shard_map.71 = (bf16[2,3,256,384]{3,2,1,0:T(8,128)(2,1)S(1)}, bf16[2,3,256,128]{3,2,1,0:T(8,128)(2,1)S(1)}, bf16[2,2,512,256]{3,2,1,0:T(8,128)(2,1)S(1)}, bf16[...) custom-call(f32[10,256]{1,0:T(8,128)S(1)} %get-tuple-element.30.fill, ...), custom_call_target="tpu_custom_call" | custom-call | tf_op jit(solution)/shard_map/pallas_call | solution.py:81
  55.1 0.0 copy-start.2
  55.1 1.0 %collective-permute-done.behind_ref = bf16[2,256,256]{2,1,0:T(8,128)(2,1)S(1)} collective-permute-done((bf16[2,256,256]{2,1,0:T(8,128)(2,1)S(1)}, bf16[2,256,256]{2,1,0:T(8,128)(2,1)S(1)}, u32[]{:S(2)}, u32[]{:S(2)}) %collective-permute-start) | collective-permute-done | bytes 262176 | tf_op jit(solution)/shard_map/ppermute | solution.py:657
  56.1 0.8 shard_map.72
  56.9 1.7 %collective-permute-done.1.ahead_ref = bf16[2,256,256]{2,1,0:T(8,128)(2,1)S(1)} collective-permute-done((bf16[2,256,256]{2,1,0:T(8,128)(2,1)S(1)}, bf16[2,256,256]{2,1,0:T(8,128)(2,1)S(1)}, u32[]{:S(2)}, u32[]{:S(2)}) %collective-permute-start.1) | collective-permute-done | bytes 262176 | tf_op jit(solution)/shard_map/ppermute | solution.py:657
  58.6 12.4 %all_to_all.22.everyone_ref = f32[16,24,128]{2,1,0:T(8,128)S(1)} all-to-all(f32[16,24,128]{2,1,0:T(8,128)S(1)} %get-tuple-element.40), channel_id=1, replica_groups=mesh['seq'=16,'head'=2] {'seq'}, dimensions={0} | all-to-all | bytes 393216 | tf_op jit(solution)/shard_map/all_to_all | solution.py:651
  71.0 0.0 copy-done
  71.0 0.0 copy-done.2
  71.0 3.4 %shard_map.73 = bf16[16,128,256]{2,1,0:T(8,128)(2,1)S(1)} custom-call(f32[10,256]{1,0:T(8,128)S(1)} %get-tuple-element.30.fill_ref, f32[16,24,128]{2,1,0:T(8,128)S(1)} %all_to_all.22.everyone_ref, bf16[2,128,1024]{2,1,0:T(8,128)(2,1)S(1)} %copy-done.2, f32[8,256]{1,0:T(8,128)S(1)} %get-tuple-element.42.low_ref, f32[12,256]{1,0:T(8,128)S(1)} %get-tuple-element.43.sums_ref, ...), custom_call_target="tpu_custom_call" | custom-call | tf_op jit(solution)/shard_map/pallas_call | solution.py:81
  74.5 0.0 copy-start.1
  74.5 26.4 %all_to_all.23 = bf16[16,128,256]{2,1,0:T(8,128)(2,1)S(1)} all-to-all(bf16[16,128,256]{2,1,0:T(8,128)(2,1)S(1)} %shard_map.73), channel_id=1, replica_groups=mesh['seq'=16,'head'=2] {'seq'}, dimensions={0} | all-to-all | bytes 2097152 | tf_op jit(solution)/shard_map/all_to_all | solution.py:651
  100.9 0.0 copy-done.1
  100.9 1.4 %shard_map.74 = (bf16[512,128]{1,0:T(8,128)(2,1)}, bf16[512,128]{1,0:T(8,128)(2,1)}) custom-call(bf16[512,2048]{1,0:T(8,128)(2,1)S(1)} %copy-done.1, bf16[2048,256]{1,0:T(8,128)(2,1)S(1)} %bitcast.9), custom_call_target="tpu_custom_call" | custom-call | tf_op jit(solution)/shard_map/pallas_call | solution.py:81
Async XLA Ops:
  4.1 42.5 %all-to-all-start = ((bf16[16,128,384]{2,1,0:T(8,128)(2,1)}), bf16[16,128,384]{2,1,0:T(8,128)(2,1)S(1)}, u32[]{:S(2)}, u32[]{:S(2)}) async-start(bf16[16,128,384]{2,1,0:T(8,128)(2,1)} %bitcast.10), calls=%async_computation | async-start | bytes 3145728 | tf_op jit(solution)/shard_map/all_to_all | solution.py:651
  47.4 8.7 %collective-permute-start = (bf16[2,256,256]{2,1,0:T(8,128)(2,1)S(1)}, bf16[2,256,256]{2,1,0:T(8,128)(2,1)S(1)}, u32[]{:S(2)}, u32[]{:S(2)}) collective-permute-start(bf16[2,256,256]{2,1,0:T(8,128)(2,1)S(1)} %get-tuple-element.33.last_ref), channel_id=1, source_target_pairs={{0,8},{8,16},{16,24},{24,26},{26,18},{18,10},{10,2},{2,6},{6,14},{... | collective-permute-start | bytes 786440 | tf_op jit(solution)/shard_map/ppermute | solution.py:657
  52.3 6.4 %collective-permute-start.1 = (bf16[2,256,256]{2,1,0:T(8,128)(2,1)S(1)}, bf16[2,256,256]{2,1,0:T(8,128)(2,1)S(1)}, u32[]{:S(2)}, u32[]{:S(2)}) collective-permute-start(bf16[2,256,256]{2,1,0:T(8,128)(2,1)S(1)} %get-tuple-element.34.first_ref), channel_id=1, source_target_pairs={{0,4},{8,0},{16,8},{24,16},{26,24},{18,26},{10,18},{2,10},{6,2},{1... | collective-permute-start | bytes 786440 | tf_op jit(solution)/shard_map/ppermute | solution.py:657
  52.3 18.8 %copy-start = (bf16[2,1024,768]{2,1,0:T(8,128)(2,1)S(1)}, bf16[2,1024,768]{2,1,0:T(8,128)(2,1)}, u32[]{:S(2)}) copy-start(bf16[2,1024,768]{2,1,0:T(8,128)(2,1)} %get-tuple-element.51.spread_t_ref) | copy-start | bytes 9437188
  55.1 15.9 %copy-start.2 = (bf16[2,128,1024]{2,1,0:T(8,128)(2,1)S(1)}, bf16[2,128,1024]{2,1,0:T(8,128)(2,1)}, u32[]{:S(2)}) copy-start(bf16[2,128,1024]{2,1,0:T(8,128)(2,1)} %get-tuple-element.41.partner_ref) | copy-start | bytes 1572868
  74.5 26.4 %copy-start.1 = (bf16[512,2048]{1,0:T(8,128)(2,1)S(1)}, bf16[512,2048]{1,0:T(8,128)(2,1)}, u32[]{:S(2)}) copy-start(bf16[512,2048]{1,0:T(8,128)(2,1)} %get-tuple-element.29.home_ref) | copy-start | bytes 6291460

commit v5 on v4

--- a/solution.py
+++ b/solution.py
@@ -68,7 +68,17 @@
     return one_hot(iota((size, size), 0) < iota((size, size), 1))
 
 
-def call(kernel, out_shapes, operands, scratch=(), remote=0, semaphores=0, far=(), direct=()):
+def call(
+    kernel,
+    out_shapes,
+    operands,
+    scratch=(),
+    remote=0,
+    semaphores=0,
+    far=(),
+    direct=(),
+    cost=0,
+):
     count = len(operands)
     held = sum(array.size * array.dtype.itemsize for array in operands[: count - remote])
     for shape, dtype in list(out_shapes) + list(scratch):
@@ -91,6 +101,7 @@
         ),
         scratch_shapes=[pltpu.VMEM(shape, dtype) for shape, dtype in scratch]
         + [pltpu.SemaphoreType.DMA((semaphores,))] * min(semaphores, 1),
+        cost_estimate=pl.CostEstimate(flops=cost, transcendentals=0, bytes_accessed=0),
         compiler_params=pltpu.CompilerParams(vmem_limit_bytes=held + 12 * 1024 * 1024),
     )(*operands)
 
@@ -112,9 +123,9 @@
     return jnp.where(float_iota(listed.shape, 1) < limit, listed, -1)
 
 
-def rank_slots(rounds, devices, token_count, tokens_ref, key_ref, value_ref):
+def rank_slots(rounds, devices, token_count, source, tokens_ref, key_ref, value_ref):
     per_device, _, cap = key_ref.shape
-    start = lax.axis_index("seq") * token_count
+    start = source * token_count
     before = earlier(cap)
     carry = jnp.zeros((rounds * devices, 1), f32)
     for group in range(per_device):
@@ -176,16 +187,25 @@
         copy.wait()
     for group in range(tokens_ref.shape[0]):
         tokens_ref[group] = slot_tokens(members_ref, counts_ref, devices, group)
-    rank_slots(rounds, devices, token_count, tokens_ref, key_ref, value_ref)
+    me = lax.axis_index("seq")
+    rank_slots(rounds, devices, token_count, me, tokens_ref, key_ref, value_ref)
+    half = devices // 2
+    first = me // half * half
     parts = 4
-    step = devices // parts
+    step = half // parts
     sends = []
     for part in range(parts):
         picks = [
             pick_rows(
-                rounds, devices, bound, block_of(device, devices), token_count, key_ref, value_ref
+                rounds,
+                devices,
+                bound,
+                block_of(first + at, devices),
+                token_count,
+                key_ref,
+                value_ref,
             )
-            for device in range(part * step, (part + 1) * step)
+            for at in range(part * step, (part + 1) * step)
         ]
         if part == 0:
             for copy in copies[halves + 1 :]:
@@ -201,31 +221,45 @@
         copy.wait()
 
 
-def index_kernel(
-    rounds,
-    devices,
-    bound,
-    token_count,
-    tokens_ref,
-    place_ref,
-    fill_ref,
-    spread_t_ref,
-    partner_ref,
-    low_ref,
-    home_ref,
-    table_ref,
-    pick_ref,
-    key_ref,
-    value_ref,
-):
+def far_pick_kernel(rounds, devices, bound, token_count, tokens_ref, pick_ref, key_ref, value_ref):
+    me = lax.axis_index("seq")
+    half = devices // 2
+    first = me // half * half
+    source = lax.rem(me + half, devices)
+    rank_slots(rounds, devices, token_count, source, tokens_ref, key_ref, value_ref)
+    size = rounds * bound
+    for at in range(half):
+        block = block_of(first + jnp.bitwise_xor(me - first, at), devices)
+        pick_ref[at * size : (at + 1) * size, :] = pick_rows(
+            rounds, devices, bound, block, token_count, key_ref, value_ref
+        )
+
+
+def far_pack_kernel(pick_ref, q_ref, v_ref, g_ref, *send_refs):
+    rows = jnp.concatenate([q_ref[...], v_ref[...], g_ref[...]], axis=1)
+    span = send_refs[0].shape[0]
+    parts = 4
+    count = len(send_refs) // parts
+    for part in range(parts):
+        first = part * count
+        packed = dot_nn(pick_ref[pl.ds(first * span, count * span), :], rows).astype(bf16)
+        for at in range(count):
+            send_refs[first + at][...] = packed[at * span : (at + 1) * span]
+
+
+def place_kernel(rounds, devices, bound, token_count, tokens_ref, place_ref, home_place_ref, fill_ref):
     per_device, _, cap = tokens_ref.shape
-    me = block_of(lax.axis_index("seq"), devices)
-    after = lax.rem(me + 1, devices)
-    buffer_rows = devices * bound
+    seat = lax.axis_index("seq")
+    me = block_of(seat, devices)
+    half = devices // 2
     before = earlier(cap)
-    source_start = iota((devices, cap), 0) * token_count
-    source_place = float_iota((devices, cap), 0) * bound + 1.0
-    place_column = float_iota((buffer_rows, cap), 0)
+    source = iota((devices, cap), 0)
+    source_start = source * token_count
+    home_place = source.astype(f32) * bound + 1.0
+    first = seat // half * half
+    near = (source >= first) & (source < first + half)
+    crossed = half + jnp.bitwise_xor(source % half, seat - first)
+    source_place = jnp.where(near, source - first, crossed).astype(f32) * bound + 1.0
     for r in range(rounds):
         carry = jnp.zeros((devices, 1), f32)
         for group in range(per_device):
@@ -233,13 +267,11 @@
             owned = (tokens >= source_start) & (tokens < source_start + token_count)
             rank = dot_nn(one_hot(owned), before) + carry
             carry = carry + jnp.sum(jnp.where(owned, 1.0, 0.0), axis=1, keepdims=True)
-            place = (
-                jnp.sum(jnp.where(owned, rank + source_place, 0.0), axis=0, keepdims=True) - 1.0
-            )
-            span = pl.ds(group * cap, cap)
-            spread_t_ref[r, :, span] = one_hot(place == place_column)
-            place_ref[pl.ds(r * per_device + group, 1), :] = place
-
+            for target, base in ((place_ref, source_place), (home_place_ref, home_place)):
+                place = jnp.sum(jnp.where(owned, rank + base, 0.0), axis=0, keepdims=True) - 1.0
+                row = r * per_device + group
+                target[row : row + 1, :] = place
+    after = lax.rem(me + 1, devices)
     behind = lax.rem(me + devices - 1, devices)
     for r in range(rounds):
         for at in range(per_device + 2):
@@ -250,6 +282,20 @@
             row = r * (per_device + 2) + at
             fill_ref[row : row + 1, :] = jnp.broadcast_to(fill, (1, cap))
 
+
+def index_kernel(
+    rounds,
+    devices,
+    bound,
+    token_count,
+    tokens_ref,
+    partner_ref,
+    low_ref,
+    table_ref,
+):
+    per_device, _, cap = tokens_ref.shape
+    me = block_of(lax.axis_index("seq"), devices)
+    after = lax.rem(me + 1, devices)
     high_count = devices * token_count // lane
     high_start = iota((high_count, cap), 0) * lane
     low_index = iota((lane, cap), 0)
@@ -308,7 +354,29 @@
             partner_ref[r, :, span] = one_hot(row == row_column)
             low_ref[pl.ds(r * (per_device + 1) + group, 1), :] = position - half * lane
 
-    rank_slots(rounds, devices, token_count, tokens_ref, key_ref, value_ref)
+
+def return_index_kernel(
+    rounds,
+    devices,
+    bound,
+    token_count,
+    tokens_ref,
+    home_place_ref,
+    spread_t_ref,
+    home_ref,
+    pick_ref,
+    key_ref,
+    value_ref,
+):
+    per_device, _, cap = tokens_ref.shape
+    place_column = float_iota((devices * bound, cap), 0)
+    for r in range(rounds):
+        for group in range(per_device):
+            row = r * per_device + group
+            place = home_place_ref[row : row + 1, :]
+            spread_t_ref[r, :, pl.ds(group * cap, cap)] = one_hot(place == place_column)
+    seat = lax.axis_index("seq")
+    rank_slots(rounds, devices, token_count, seat, tokens_ref, key_ref, value_ref)
 
     def pick_device(device, carried):
         at = pl.multiple_of(device * rounds * bound, rounds * bound)
@@ -331,17 +399,21 @@
     return short_hot(place_ref[row : row + 1, :], (buffer_rows, cap), 0)
 
 
-def received_rows(got_ref, r, rounds):
-    devices, span, width = got_ref.shape
+def received_rows(near_ref, far_refs, r, rounds):
+    half, span, width = near_ref.shape
     bound = span // rounds
-    return got_ref[:, r * bound : (r + 1) * bound, :].reshape(devices * bound, width)
-
-
-def ends_kernel(rounds, got_ref, place_ref, last_ref, first_ref):
-    size = got_ref.shape[2] // 3
+    rows = slice(r * bound, (r + 1) * bound)
+    parts = [near_ref[:, rows, :].reshape(half * bound, width)]
+    parts += [far_ref[rows, :] for far_ref in far_refs]
+    return jnp.concatenate(parts, axis=0)
+
+
+def ends_kernel(rounds, near_ref, place_ref, *refs):
+    far_refs, (last_ref, first_ref) = refs[:-2], refs[-2:]
+    size = near_ref.shape[2] // 3
     per_device = place_ref.shape[0] // rounds
     for r in range(rounds):
-        received = received_rows(got_ref, r, rounds)
+        received = received_rows(near_ref, far_refs, r, rounds)
         spread = spread_of(place_ref, r, per_device - 1, rounds, received.shape[0])
         last_ref[r] = dot_tn(spread, received[:, : 2 * size]).astype(bf16)
         spread = spread_of(place_ref, r, 0, rounds, received.shape[0])
@@ -383,29 +455,26 @@
     dots = jnp.sum(probs[0] * inners[0], axis=0, keepdims=True) + jnp.sum(
         probs[1] * inners[1], axis=0, keepdims=True
     )
-    return highest + jnp.log(total), dots, [prob.astype(bf16) for prob in probs]
+    centred = [(inner - dots).astype(bf16) for inner in inners]
+    return highest + jnp.log(total), dots, [prob.astype(bf16) for prob in probs], centred
 
 
 def forward_inner_kernel(
     rounds,
     fill_ref,
-    got_ref,
+    near_ref,
     place_ref,
     last_ref,
     first_ref,
-    rows_ref,
-    units_ref,
-    prob_ref,
-    inner_ref,
-    first_score_ref,
-    first_inner_ref,
-    sums_ref,
+    *refs,
 ):
+    far_refs, refs = refs[:-7], refs[-7:]
+    rows_ref, units_ref, prob_ref, inner_ref, first_score_ref, first_inner_ref, sums_ref = refs
     cap = prob_ref.shape[3]
     per_device = rows_ref.shape[1]
     size = rows_ref.shape[3] // 3
     for r in range(rounds):
-        received = received_rows(got_ref, r, rounds)
+        received = received_rows(near_ref, far_refs, r, rounds)
         for group in range(per_device):
             spread = spread_of(place_ref, r, group, rounds, received.shape[0])
             if group == 0:
@@ -440,11 +509,11 @@
                 units[group - 1], queries, fill_row(fill_ref, r, group, rounds), False
             )
             inners = [inner_before, inner_now]
-            log_total, dots, probs = normalised([score_before, score_now], inners)
+            log_total, dots, probs, centred = normalised([score_before, score_now], inners)
             for side in range(2):
                 span = slice(side * cap, (side + 1) * cap)
                 prob_ref[r, group - 1, span, :] = probs[side]
-                inner_ref[r, group - 1, span, :] = inners[side].astype(bf16)
+                inner_ref[r, group - 1, span, :] = centred[side]
             row = r * per_device + group
             sums_ref[row : row + 1, :] = log_total
             row = (rounds + r) * per_device + group
@@ -478,11 +547,11 @@
         cot = rows_ref[r, 0, :, 2 * size :]
         score_before = scored(behind_unit, queries, fill_row(fill_ref, r, 0, rounds), False)
         inners = [dot_nt(behind_ref[r, :, size:], cot), inner_now_ref[r]]
-        log_total, dots, probs = normalised([score_before, score_ref[r]], inners)
+        log_total, dots, probs, centred = normalised([score_before, score_ref[r]], inners)
         for side in range(2):
             span = slice(side * cap, (side + 1) * cap)
             prob_ref[r, span, :] = probs[side]
-            inner_ref[r, span, :] = inners[side].astype(bf16)
+            inner_ref[r, span, :] = centred[side]
         row = r * per_device
         sums_ref[row : row + 1, :] = log_total
         row = (rounds + r) * per_device
@@ -587,16 +656,24 @@
                 own_dot = ahead_sums(r, 1)
             weight = 1.0 / (1.0 + jnp.exp(other_log - own_log))
             other_weight = 1.0 / (1.0 + jnp.exp(own_log - other_log))
-            mixture = weight * own_dot + other_weight * other_dot
+            shift = other_weight * (own_dot - other_dot)
             valid = slot < fill_row(fill_ref, r, group + 1, rounds)
-            scales.append((jnp.where(valid, weight, 0.0), jnp.where(valid, mixture, 0.0)))
+            scales.append((jnp.where(valid, weight, 0.0), jnp.where(valid, shift, 0.0)))
         return scales
 
     def score_grads(prob, inner, scale):
         weighted = prob.astype(f32) * scale[0]
-        score_grad = (weighted * (inner.astype(f32) - scale[1])).astype(bf16)
+        score_grad = (weighted * (inner.astype(f32) + scale[1])).astype(bf16)
         return weighted.astype(bf16), score_grad
 
+    aheads = []
+    for r in range(rounds):
+        queries = ahead_ref[r, :, :size]
+        cot = ahead_ref[r, :, size:]
+        fill = fill_row(fill_ref, r, per_device, rounds)
+        score = scored(units_ref[r, per_device - 1], queries, fill, False)
+        inner = dot_nt(rows_ref[r, per_device - 1, :, size : 2 * size], cot)
+        aheads.append(([jnp.exp(score - ahead_sums(r, 0))], [inner - ahead_sums(r, 1)]))
     scales = [scales_of(r) for r in range(rounds)]
     carried = [None] * rounds
     for group in range(per_device + 1):
@@ -614,10 +691,7 @@
                 probs = [prob_ref[r, group - 1, :cap, :], prob_ref[r, group - 1, cap:, :]]
                 inners = [inner_ref[r, group - 1, :cap, :], inner_ref[r, group - 1, cap:, :]]
             else:
-                fill = fill_row(fill_ref, r, per_device, rounds)
-                score = scored(units_ref[r, per_device - 1], queries, fill, False)
-                probs = [jnp.exp(score - ahead_sums(r, 0))]
-                inners = [dot_nt(rows_ref[r, per_device - 1, :, size : 2 * size], cot)]
+                probs, inners = aheads[r]
             scale = scales[r][group]
             weighted, score_grad = score_grads(probs[0], inners[0], scale)
             if group > 0:
@@ -647,6 +721,26 @@
     value_ref[...] = total[:, size:].astype(bf16)
 
 
+def exchange_in_half(array):
+    devices = lax.axis_size("seq")
+    half = devices // 2
+    halves = [list(range(half)), list(range(half, devices))]
+    return lax.all_to_all(
+        array, "seq", split_axis=0, concat_axis=0, tiled=True, axis_index_groups=halves
+    )
+
+
+def crossed(array, by):
+    devices = lax.axis_size("seq")
+    return lax.ppermute(array, "seq", [(i, i ^ by) for i in range(devices)])
+
+
+def mirrored(array):
+    devices = lax.axis_size("seq")
+    half = devices // 2
+    return lax.ppermute(array, "seq", [(i, (i + half) % devices) for i in range(devices)])
+
+
 def exchange(array):
     return lax.all_to_all(array, "seq", split_axis=0, concat_axis=0, tiled=True)
 
@@ -670,11 +764,13 @@
     listed = members.reshape(rounds * groups, cap)
     keys = [((per_device, rounds * devices, cap), f32)] * 2
     pick = ((devices * span, token_count), bf16)
-    send, tokens = call(
+    half = devices // 2
+    far_rows = [mirrored(rows) for rows in (qk, values, cot)]
+    near_send, tokens = call(
         functools.partial(pack_kernel, rounds, devices, bound),
-        [((devices * span, 3 * size), bf16), (keys[0][0], jnp.int32)],
+        [((half * span, 3 * size), bf16), (keys[0][0], jnp.int32)],
         [counts, listed, qk, values, cot],
-        [((devices * span, 3 * size), bf16)]
+        [((half * span, 3 * size), bf16)]
         + keys
         + [
             (counts.shape, jnp.int32),
@@ -686,25 +782,54 @@
         far=(0,),
         direct=(0,),
     )
-    got = exchange(send).reshape(devices, span, 3 * size)
-    place, fill, spread_t, partner, low, home_pick = call(
+    near = exchange_in_half(near_send).reshape(half, span, 3 * size)
+    (far_pick,) = call(
+        functools.partial(far_pick_kernel, rounds, devices, bound, token_count),
+        [((half * span, token_count), bf16)],
+        [tokens],
+        keys,
+    )
+    place, home_place, fill = call(
+        functools.partial(place_kernel, rounds, devices, bound, token_count),
+        [
+            ((rounds * per_device, cap), f32),
+            ((rounds * per_device, cap), f32),
+            ((rounds * (per_device + 2), cap), f32),
+        ],
+        [tokens],
+    )
+    partner, low = call(
         functools.partial(index_kernel, rounds, devices, bound, token_count),
         [
-            ((rounds * per_device, cap), f32),
-            ((rounds * (per_device + 2), cap), f32),
-            ((rounds, buffer_rows, slots), bf16),
             ((rounds, devices * table_kept(slots // lane), slots + cap), bf16),
             ((rounds * (per_device + 1), cap), f32),
-            ((token_count, devices * span), bf16),
         ],
         [tokens],
-        [((rounds, 2 * devices * token_count // lane, lane), bf16), pick] + keys,
-        far=(2, 3, 5),
-    )
+        [((rounds, 2 * devices * token_count // lane, lane), bf16)],
+        far=(0,),
+    )
+    far_send = call(
+        far_pack_kernel,
+        [((span, 3 * size), bf16)] * half,
+        [far_pick] + far_rows,
+        cost=50_000_000_000,
+    )
+    far_send, partner, tokens, home_place = lax.optimization_barrier(
+        (far_send, partner, tokens, home_place)
+    )
+    far = [far_send[0]] + [crossed(far_send[by], by) for by in range(1, half)]
+    spread_t, home_pick = call(
+        functools.partial(return_index_kernel, rounds, devices, bound, token_count),
+        [((rounds, buffer_rows, slots), bf16), ((token_count, devices * span), bf16)],
+        [tokens, home_place],
+        [pick] + keys,
+        far=(0, 1),
+    )
+    far, spread_t, home_pick = lax.optimization_barrier((far, spread_t, home_pick))
     last, first = call(
         functools.partial(ends_kernel, rounds),
         [((rounds, cap, 2 * size), bf16)] * 2,
-        [got, place],
+        [near, place] + far,
     )
     behind = shifted(last, 1)
     ahead = shifted(first, -1)
@@ -720,7 +845,7 @@
             (square, f32),
             ((sum_rows, cap), f32),
         ],
-        [fill, got, place, last, first],
+        [fill, near, place, last, first] + far,
     )
     behind_unit, first_prob, first_inner, sums, sums_send = call(
         functools.partial(forward_first_kernel, rounds, devices),

time: 103 us -> 95 us (0.922)
  waiting for transfers between devices: 26.1 us -> 7.17 us
  starting transfers between devices: 13.2 us -> 23.4 us
    all_to_all x1, waiting for transfers between devices: 23.3 us -> 0.01 us  [exchange_in_half(): lax.all_to_all(array, 'seq', split_axis=0, concat_axis=0, tiled=True, axi...]
    ppermute x0 -> x10, starting transfers between devices: none -> 16.6 us  [the longest x7 9.54 us: crossed(): return lax.ppermute(array, 'seq', [(i, i ^ by) for i in range(devices)])]
    ppermute x0 -> x10, waiting for transfers between devices: none -> 4.03 us  [the longest x7 4.02 us: crossed(): return lax.ppermute(array, 'seq', [(i, i ^ by) for i in range(devices)])]
    all_to_all x1, starting transfers between devices: 8.32 us -> 4.75 us  [exchange_in_half(): lax.all_to_all(array, 'seq', split_axis=0, concat_axis=0, tiled=True, axi...]
    ppermute x2, starting transfers between devices: 4.83 us -> 2.07 us  [shifted(): lax.ppermute(array, 'seq', [(order[i], order[(i + by) % devices]) for i i...]
    pallas_call x7 -> x11, Pallas kernels: 23.6 us -> 24.5 us  [call(): pl.pallas_call(kernel, out_shape=tuple((pltpu.HBM(shape, dtype) if at in...]
  transfers between devices with their start and end apart: 3 -> 13, of which waited for: 3 -> 4; matrix products, arithmetic and copies ran while one was open for 0% -> 0% of each run, Pallas kernels for 14% -> 20%
where the time goes in v5:
time: 95 us; the launch traced here: 94.7 us
  blocking collectives  38.8 us (41%)
  Pallas kernels  24.5 us (26%)
  starting transfers between devices  23.4 us (25%)
  waiting for transfers between devices  7.17 us (8%)
    all_to_all x2, blocking collectives, exchange(): return lax.all_to_all(array, 'seq', split_axis=0, concat_axis=0, tiled=True)  38.8 us
    pallas_call x11, Pallas kernels, call(): pl.pallas_call(kernel, out_shape=tuple((pltpu.HBM(shape, dtype) if at in...  24.5 us
    ppermute x7, starting transfers between devices, crossed(): return lax.ppermute(array, 'seq', [(i, i ^ by) for i in range(devices)])  9.54 us
    ppermute x3, starting transfers between devices, mirrored(): lax.ppermute(array, 'seq', [(i, (i + half) % devices) for i in range(devi...  7.03 us
    all_to_all x1, starting transfers between devices, exchange_in_half(): lax.all_to_all(array, 'seq', split_axis=0, concat_axis=0, tiled=True, axi...  4.75 us
    ppermute x7, waiting for transfers between devices, crossed(): return lax.ppermute(array, 'seq', [(i, i ^ by) for i in range(devices)])  4.02 us
    ppermute x2, waiting for transfers between devices, shifted(): lax.ppermute(array, 'seq', [(order[i], order[(i + by) % devices]) for i i...  3.14 us
    ppermute x2, starting transfers between devices, shifted(): lax.ppermute(array, 'seq', [(order[i], order[(i + by) % devices]) for i i...  2.07 us
  transfers between devices with their start and end apart: 13, of which 4 were waited for; matrix products, arithmetic and copies ran while one was open for 0% of the time, Pallas kernels for 20%

profile of v5, /device:TPU:0, one launch (start us, length us, event | category | flops | bytes accessed | tf_op | source)
XLA Modules:
  0.0 94.7 jit_solution(5031339492282258105)
XLA Ops:
  0.6 4.1 %collective-permute-start = (bf16[512,128]{1,0:T(8,128)(2,1)}, bf16[512,128]{1,0:T(8,128)(2,1)S(1)}, u32[]{:S(2)}, u32[]{:S(2)}) collective-permute-start(bf16[512,128]{1,0:T(8,128)(2,1)} %bitcast.11), channel_id=1, source_target_pairs={{0,16},{2,18},{4,20},{6,22},{8,24},{10,26},{12,28},{14,30},{16,0},... | collective-permute-start | bytes 393224 | tf_op jit(solution)/shard_map/ppermute | solution.py:741
  4.7 0.1 collective-permute-start.1
  4.8 2.8 %collective-permute-start.2 = (bf16[512,128]{1,0:T(8,128)(2,1)}, bf16[512,128]{1,0:T(8,128)(2,1)S(1)}, u32[]{:S(2)}, u32[]{:S(2)}) collective-permute-start(bf16[512,128]{1,0:T(8,128)(2,1)} %bitcast.15), channel_id=1, source_target_pairs={{0,16},{2,18},{4,20},{6,22},{8,24},{10,26},{12,28},{14,30},{16,0},... | collective-permute-start | bytes 393224 | tf_op jit(solution)/shard_map/ppermute | solution.py:741
  7.7 2.8 %shard_map.68 = (bf16[1024,384]{1,0:T(8,128)(2,1)}, s32[3,32,256]{2,1,0:T(8,128)S(1)}) custom-call(s32[2,48]{1,0:T(2,128)} %bitcast.18, s32[96,256]{1,0:T(8,128)} %bitcast.17, bf16[512,128]{1,0:T(8,128)(2,1)} %bitcast.12, bf16[512,128]{1,0:T(8,128)(2,1)} %bitcast.14, bf16[512,128]{1,0:T(8,128)(2,1)} %bitcast.16), custom_call_target="tpu_custom_call" | custom-call | tf_op jit(solution)/shard_map/pallas_call | solution.py:91
  10.5 4.8 %all-to-all-start = ((bf16[8,128,384]{2,1,0:T(8,128)(2,1)}), bf16[8,128,384]{2,1,0:T(8,128)(2,1)S(1)}, u32[]{:S(2)}, u32[]{:S(2)}) async-start(bf16[8,128,384]{2,1,0:T(8,128)(2,1)} %bitcast.10), calls=%async_computation | async-start | bytes 1572864 | tf_op jit(solution)/shard_map/all_to_all | solution.py:728
  15.2 0.7 shard_map.69.pick_ref
  15.9 0.2 shard_map.72
  16.1 6.5 %shard_map.71 = (bf16[2,128,1024]{2,1,0:T(8,128)(2,1)}, f32[8,256]{1,0:T(8,128)S(1)}) custom-call(s32[3,32,256]{2,1,0:T(8,128)S(1)} %get-tuple-element.77.tokens_ref), custom_call_target="tpu_custom_call" | custom-call | tf_op jit(solution)/shard_map/pallas_call | solution.py:91
  22.7 0.0 collective-permute-done.q_ref
  22.7 0.0 collective-permute-done.1.v_ref
  22.7 0.0 collective-permute-done.2.g_ref
  22.7 0.7 shard_map.70
  23.4 2.1 %collective-permute-start.3 = (bf16[128,384]{1,0:T(8,128)(2,1)S(1)}, bf16[128,384]{1,0:T(8,128)(2,1)S(1)}, u32[]{:S(2)}, u32[]{:S(2)}) collective-permute-start(bf16[128,384]{1,0:T(8,128)(2,1)S(1)} %get-tuple-element.70), channel_id=1, source_target_pairs={{0,2},{2,0},{4,6},{6,4},{8,10},{10,8},{12,14},{14,12},{16,18},{18,... | collective-permute-start | bytes 294920 | tf_op jit(solution)/shard_map/ppermute | solution.py:735
  25.5 1.5 %collective-permute-start.4 = (bf16[128,384]{1,0:T(8,128)(2,1)S(1)}, bf16[128,384]{1,0:T(8,128)(2,1)S(1)}, u32[]{:S(2)}, u32[]{:S(2)}) collective-permute-start(bf16[128,384]{1,0:T(8,128)(2,1)S(1)} %get-tuple-element.71), channel_id=1, source_target_pairs={{0,4},{2,6},{4,0},{6,2},{8,12},{10,14},{12,8},{14,10},{16,20},{18,... | collective-permute-start | bytes 294920 | tf_op jit(solution)/shard_map/ppermute | solution.py:735
  26.9 0.1 collective-permute-start.5
  27.0 2.0 %collective-permute-start.6 = (bf16[128,384]{1,0:T(8,128)(2,1)S(1)}, bf16[128,384]{1,0:T(8,128)(2,1)S(1)}, u32[]{:S(2)}, u32[]{:S(2)}) collective-permute-start(bf16[128,384]{1,0:T(8,128)(2,1)S(1)} %get-tuple-element.73), channel_id=1, source_target_pairs={{0,8},{2,10},{4,12},{6,14},{8,0},{10,2},{12,4},{14,6},{16,24},{18,... | collective-permute-start | bytes 294920 | tf_op jit(solution)/shard_map/ppermute | solution.py:735
  29.0 1.5 %collective-permute-start.7 = (bf16[128,384]{1,0:T(8,128)(2,1)S(1)}, bf16[128,384]{1,0:T(8,128)(2,1)S(1)}, u32[]{:S(2)}, u32[]{:S(2)}) collective-permute-start(bf16[128,384]{1,0:T(8,128)(2,1)S(1)} %get-tuple-element.74), channel_id=1, source_target_pairs={{0,10},{2,8},{4,14},{6,12},{8,2},{10,0},{12,6},{14,4},{16,26},{18,... | collective-permute-start | bytes 294920 | tf_op jit(solution)/shard_map/ppermute | solution.py:735
  30.4 0.5 collective-permute-done.3.refs_1_
  30.9 1.9 %collective-permute-start.8 = (bf16[128,384]{1,0:T(8,128)(2,1)S(1)}, bf16[128,384]{1,0:T(8,128)(2,1)S(1)}, u32[]{:S(2)}, u32[]{:S(2)}) collective-permute-start(bf16[128,384]{1,0:T(8,128)(2,1)S(1)} %get-tuple-element.75), channel_id=1, source_target_pairs={{0,12},{2,14},{4,8},{6,10},{8,4},{10,6},{12,0},{14,2},{16,28},{18,... | collective-permute-start | bytes 294920 | tf_op jit(solution)/shard_map/ppermute | solution.py:735
  32.8 1.2 %collective-permute-done.4.refs_2_ = bf16[128,384]{1,0:T(8,128)(2,1)S(1)} collective-permute-done((bf16[128,384]{1,0:T(8,128)(2,1)S(1)}, bf16[128,384]{1,0:T(8,128)(2,1)S(1)}, u32[]{:S(2)}, u32[]{:S(2)}) %collective-permute-start.4) | collective-permute-done | bytes 98336 | tf_op jit(solution)/shard_map/ppermute | solution.py:735
  34.0 0.6 collective-permute-start.9
  34.7 4.4 %shard_map.73 = (bf16[2,1024,768]{2,1,0:T(8,128)(2,1)}, bf16[512,2048]{1,0:T(8,128)(2,1)}) custom-call(s32[3,32,256]{2,1,0:T(8,128)S(1)} %get-tuple-element.77.tokens_ref, f32[6,256]{1,0:T(8,128)S(1)} %get-tuple-element.78.home_place_ref), custom_call_target="tpu_custom_call" | custom-call | tf_op jit(solution)/shard_map/pallas_call | solution.py:91
  39.0 0.0 collective-permute-done.5.refs_3_
  39.0 0.0 collective-permute-done.6.refs_4_
  39.0 0.0 collective-permute-done.7.refs_5_
  39.0 0.0 collective-permute-done.8.refs_6_
  39.1 2.3 %collective-permute-done.9.refs_7_ = bf16[128,384]{1,0:T(8,128)(2,1)S(1)} collective-permute-done((bf16[128,384]{1,0:T(8,128)(2,1)S(1)}, bf16[128,384]{1,0:T(8,128)(2,1)S(1)}, u32[]{:S(2)}, u32[]{:S(2)}) %collective-permute-start.9) | collective-permute-done | bytes 98336 | tf_op jit(solution)/shard_map/ppermute | solution.py:735
  41.3 0.0 all-to-all-done.near_ref
  41.3 0.8 shard_map.74
  42.1 0.1 collective-permute-start.10
  42.2 2.0 %collective-permute-start.11 = (bf16[2,256,256]{2,1,0:T(8,128)(2,1)S(1)}, bf16[2,256,256]{2,1,0:T(8,128)(2,1)S(1)}, u32[]{:S(2)}, u32[]{:S(2)}) collective-permute-start(bf16[2,256,256]{2,1,0:T(8,128)(2,1)S(1)} %get-tuple-element.94.first_ref), channel_id=1, source_target_pairs={{0,4},{8,0},{16,8},{24,16},{26,24},{18,26},{10,18},{2,10},{6,2},{1... | collective-permute-start | bytes 786440 | tf_op jit(solution)/shard_map/ppermute | solution.py:751
  44.2 0.0 copy-start
  44.2 0.0 copy-start.2
  44.2 2.9 %shard_map.75 = (bf16[2,3,256,384]{3,2,1,0:T(8,128)(2,1)S(1)}, bf16[2,3,256,128]{3,2,1,0:T(8,128)(2,1)S(1)}, bf16[2,2,512,256]{3,2,1,0:T(8,128)(2,1)S(1)}, bf16[...) custom-call(f32[10,256]{1,0:T(8,128)S(1)} %get-tuple-element.82.fill, ...), custom_call_target="tpu_custom_call" | custom-call | tf_op jit(solution)/shard_map/pallas_call | solution.py:91
  47.1 3.1 %collective-permute-done.10.behind_ref = bf16[2,256,256]{2,1,0:T(8,128)(2,1)S(1)} collective-permute-done((bf16[2,256,256]{2,1,0:T(8,128)(2,1)S(1)}, bf16[2,256,256]{2,1,0:T(8,128)(2,1)S(1)}, u32[]{:S(2)}, u32[]{:S(2)}) %collective-permute-start.10) | collective-permute-done | bytes 262176 | tf_op jit(solution)/shard_map/ppermute | solution.py:751
  50.3 0.8 shard_map.76
  51.0 0.0 collective-permute-done.11.ahead_ref
  51.0 11.7 %all_to_all.22.everyone_ref = f32[16,24,128]{2,1,0:T(8,128)S(1)} all-to-all(f32[16,24,128]{2,1,0:T(8,128)S(1)} %get-tuple-element.100), channel_id=1, replica_groups=mesh['seq'=16,'head'=2] {'seq'}, dimensions={0} | all-to-all | bytes 393216 | tf_op jit(solution)/shard_map/all_to_all | solution.py:745
  62.8 0.0 copy-done
  62.8 0.0 copy-done.2
  62.8 3.4 %shard_map.77 = bf16[16,128,256]{2,1,0:T(8,128)(2,1)S(1)} custom-call(f32[10,256]{1,0:T(8,128)S(1)} %get-tuple-element.82.fill_ref, f32[16,24,128]{2,1,0:T(8,128)S(1)} %all_to_all.22.everyone_ref, bf16[2,128,1024]{2,1,0:T(8,128)(2,1)S(1)} %copy-done.2, f32[8,256]{1,0:T(8,128)S(1)} %get-tuple-element.102.low_ref, f32[12,256]{1,0:T(8,128)S(1)} %get-tuple-element.103.sums_ref, ...), custom_call_target="tpu_custom_call" | custom-call | tf_op jit(solution)/shard_map/pallas_call | solution.py:91
  66.2 0.0 copy-start.1
  66.2 27.1 %all_to_all.23 = bf16[16,128,256]{2,1,0:T(8,128)(2,1)S(1)} all-to-all(bf16[16,128,256]{2,1,0:T(8,128)(2,1)S(1)} %shard_map.77), channel_id=1, replica_groups=mesh['seq'=16,'head'=2] {'seq'}, dimensions={0} | all-to-all | bytes 2097152 | tf_op jit(solution)/shard_map/all_to_all | solution.py:745
  93.3 0.0 copy-done.1
  93.3 1.4 %shard_map.78 = (bf16[512,128]{1,0:T(8,128)(2,1)}, bf16[512,128]{1,0:T(8,128)(2,1)}) custom-call(bf16[512,2048]{1,0:T(8,128)(2,1)S(1)} %copy-done.1, bf16[2048,256]{1,0:T(8,128)(2,1)S(1)} %bitcast.9), custom_call_target="tpu_custom_call" | custom-call | tf_op jit(solution)/shard_map/pallas_call | solution.py:91
Async XLA Ops:
  0.6 22.0 %collective-permute-start = (bf16[512,128]{1,0:T(8,128)(2,1)}, bf16[512,128]{1,0:T(8,128)(2,1)S(1)}, u32[]{:S(2)}, u32[]{:S(2)}) collective-permute-start(bf16[512,128]{1,0:T(8,128)(2,1)} %bitcast.11), channel_id=1, source_target_pairs={{0,16},{2,18},{4,20},{6,22},{8,24},{10,26},{12,28},{14,30},{16,0},... | collective-permute-start | bytes 393224 | tf_op jit(solution)/shard_map/ppermute | solution.py:741
  4.7 17.9 %collective-permute-start.1 = (bf16[512,128]{1,0:T(8,128)(2,1)}, bf16[512,128]{1,0:T(8,128)(2,1)S(1)}, u32[]{:S(2)}, u32[]{:S(2)}) collective-permute-start(bf16[512,128]{1,0:T(8,128)(2,1)} %bitcast.13), channel_id=1, source_target_pairs={{0,16},{2,18},{4,20},{6,22},{8,24},{10,26},{12,28},{14,30},{16,0},... | collective-permute-start | bytes 393224 | tf_op jit(solution)/shard_map/ppermute | solution.py:741
  4.8 17.9 %collective-permute-start.2 = (bf16[512,128]{1,0:T(8,128)(2,1)}, bf16[512,128]{1,0:T(8,128)(2,1)S(1)}, u32[]{:S(2)}, u32[]{:S(2)}) collective-permute-start(bf16[512,128]{1,0:T(8,128)(2,1)} %bitcast.15), channel_id=1, source_target_pairs={{0,16},{2,18},{4,20},{6,22},{8,24},{10,26},{12,28},{14,30},{16,0},... | collective-permute-start | bytes 393224 | tf_op jit(solution)/shard_map/ppermute | solution.py:741
  10.5 30.9 %all-to-all-start = ((bf16[8,128,384]{2,1,0:T(8,128)(2,1)}), bf16[8,128,384]{2,1,0:T(8,128)(2,1)S(1)}, u32[]{:S(2)}, u32[]{:S(2)}) async-start(bf16[8,128,384]{2,1,0:T(8,128)(2,1)} %bitcast.10), calls=%async_computation | async-start | bytes 1572864 | tf_op jit(solution)/shard_map/all_to_all | solution.py:728
  23.4 7.5 %collective-permute-start.3 = (bf16[128,384]{1,0:T(8,128)(2,1)S(1)}, bf16[128,384]{1,0:T(8,128)(2,1)S(1)}, u32[]{:S(2)}, u32[]{:S(2)}) collective-permute-start(bf16[128,384]{1,0:T(8,128)(2,1)S(1)} %get-tuple-element.70), channel_id=1, source_target_pairs={{0,2},{2,0},{4,6},{6,4},{8,10},{10,8},{12,14},{14,12},{16,18},{18,... | collective-permute-start | bytes 294920 | tf_op jit(solution)/shard_map/ppermute | solution.py:735
  25.5 8.6 %collective-permute-start.4 = (bf16[128,384]{1,0:T(8,128)(2,1)S(1)}, bf16[128,384]{1,0:T(8,128)(2,1)S(1)}, u32[]{:S(2)}, u32[]{:S(2)}) collective-permute-start(bf16[128,384]{1,0:T(8,128)(2,1)S(1)} %get-tuple-element.71), channel_id=1, source_target_pairs={{0,4},{2,6},{4,0},{6,2},{8,12},{10,14},{12,8},{14,10},{16,20},{18,... | collective-permute-start | bytes 294920 | tf_op jit(solution)/shard_map/ppermute | solution.py:735
  26.9 12.1 %collective-permute-start.5 = (bf16[128,384]{1,0:T(8,128)(2,1)S(1)}, bf16[128,384]{1,0:T(8,128)(2,1)S(1)}, u32[]{:S(2)}, u32[]{:S(2)}) collective-permute-start(bf16[128,384]{1,0:T(8,128)(2,1)S(1)} %get-tuple-element.72), channel_id=1, source_target_pairs={{0,6},{2,4},{4,2},{6,0},{8,14},{10,12},{12,10},{14,8},{16,22},{18,... | collective-permute-start | bytes 294920 | tf_op jit(solution)/shard_map/ppermute | solution.py:735
  27.0 12.0 %collective-permute-start.6 = (bf16[128,384]{1,0:T(8,128)(2,1)S(1)}, bf16[128,384]{1,0:T(8,128)(2,1)S(1)}, u32[]{:S(2)}, u32[]{:S(2)}) collective-permute-start(bf16[128,384]{1,0:T(8,128)(2,1)S(1)} %get-tuple-element.73), channel_id=1, source_target_pairs={{0,8},{2,10},{4,12},{6,14},{8,0},{10,2},{12,4},{14,6},{16,24},{18,... | collective-permute-start | bytes 294920 | tf_op jit(solution)/shard_map/ppermute | solution.py:735
  29.0 10.1 %collective-permute-start.7 = (bf16[128,384]{1,0:T(8,128)(2,1)S(1)}, bf16[128,384]{1,0:T(8,128)(2,1)S(1)}, u32[]{:S(2)}, u32[]{:S(2)}) collective-permute-start(bf16[128,384]{1,0:T(8,128)(2,1)S(1)} %get-tuple-element.74), channel_id=1, source_target_pairs={{0,10},{2,8},{4,14},{6,12},{8,2},{10,0},{12,6},{14,4},{16,26},{18,... | collective-permute-start | bytes 294920 | tf_op jit(solution)/shard_map/ppermute | solution.py:735
  30.9 8.1 %collective-permute-start.8 = (bf16[128,384]{1,0:T(8,128)(2,1)S(1)}, bf16[128,384]{1,0:T(8,128)(2,1)S(1)}, u32[]{:S(2)}, u32[]{:S(2)}) collective-permute-start(bf16[128,384]{1,0:T(8,128)(2,1)S(1)} %get-tuple-element.75), channel_id=1, source_target_pairs={{0,12},{2,14},{4,8},{6,10},{8,4},{10,6},{12,0},{14,2},{16,28},{18,... | collective-permute-start | bytes 294920 | tf_op jit(solution)/shard_map/ppermute | solution.py:735
  34.0 7.3 %collective-permute-start.9 = (bf16[128,384]{1,0:T(8,128)(2,1)S(1)}, bf16[128,384]{1,0:T(8,128)(2,1)S(1)}, u32[]{:S(2)}, u32[]{:S(2)}) collective-permute-start(bf16[128,384]{1,0:T(8,128)(2,1)S(1)} %get-tuple-element.76), channel_id=1, source_target_pairs={{0,14},{2,12},{4,10},{6,8},{8,6},{10,4},{12,2},{14,0},{16,30},{18,... | collective-permute-start | bytes 294920 | tf_op jit(solution)/shard_map/ppermute | solution.py:735
  42.1 8.1 %collective-permute-start.10 = (bf16[2,256,256]{2,1,0:T(8,128)(2,1)S(1)}, bf16[2,256,256]{2,1,0:T(8,128)(2,1)S(1)}, u32[]{:S(2)}, u32[]{:S(2)}) collective-permute-start(bf16[2,256,256]{2,1,0:T(8,128)(2,1)S(1)} %get-tuple-element.93.last_ref), channel_id=1, source_target_pairs={{0,8},{8,16},{16,24},{24,26},{26,18},{18,10},{10,2},{2,6},{6,14},{... | collective-permute-start | bytes 786440 | tf_op jit(solution)/shard_map/ppermute | solution.py:751
  42.2 8.9 %collective-permute-start.11 = (bf16[2,256,256]{2,1,0:T(8,128)(2,1)S(1)}, bf16[2,256,256]{2,1,0:T(8,128)(2,1)S(1)}, u32[]{:S(2)}, u32[]{:S(2)}) collective-permute-start(bf16[2,256,256]{2,1,0:T(8,128)(2,1)S(1)} %get-tuple-element.94.first_ref), channel_id=1, source_target_pairs={{0,4},{8,0},{16,8},{24,16},{26,24},{18,26},{10,18},{2,10},{6,2},{1... | collective-permute-start | bytes 786440 | tf_op jit(solution)/shard_map/ppermute | solution.py:751
  44.2 18.6 %copy-start = (bf16[2,1024,768]{2,1,0:T(8,128)(2,1)S(1)}, bf16[2,1024,768]{2,1,0:T(8,128)(2,1)}, u32[]{:S(2)}) copy-start(bf16[2,1024,768]{2,1,0:T(8,128)(2,1)} %get-tuple-element.111.spread_t_ref) | copy-start | bytes 9437188
  44.2 18.6 %copy-start.2 = (bf16[2,128,1024]{2,1,0:T(8,128)(2,1)S(1)}, bf16[2,128,1024]{2,1,0:T(8,128)(2,1)}, u32[]{:S(2)}) copy-start(bf16[2,128,1024]{2,1,0:T(8,128)(2,1)} %get-tuple-element.101.partner_ref) | copy-start | bytes 1572868
  66.2 27.1 %copy-start.1 = (bf16[512,2048]{1,0:T(8,128)(2,1)S(1)}, bf16[512,2048]{1,0:T(8,128)(2,1)}, u32[]{:S(2)}) copy-start(bf16[512,2048]{1,0:T(8,128)(2,1)} %get-tuple-element.81.home_ref) | copy-start | bytes 6291460

commit v6 on v5

--- a/solution.py
+++ b/solution.py
@@ -153,15 +153,25 @@
     return jnp.concatenate(picks, axis=0)
 
 
+def join_kernel(q_hbm, v_hbm, g_hbm, joined_ref, sems):
+    size = q_hbm.shape[1]
+    copies = []
+    for at, source in enumerate((q_hbm, v_hbm, g_hbm)):
+        target = joined_ref.at[:, pl.ds(at * size, size)]
+        copies.append(pltpu.make_async_copy(source, target, sems.at[at]))
+    for copy in copies:
+        copy.start()
+    for copy in copies:
+        copy.wait()
+
+
 def pack_kernel(
     rounds,
     devices,
     bound,
+    joined_ref,
     counts_hbm,
     members_hbm,
-    q_hbm,
-    v_hbm,
-    g_hbm,
     send_hbm,
     tokens_ref,
     packed_ref,
@@ -169,21 +179,17 @@
     value_ref,
     counts_ref,
     members_ref,
-    rows_ref,
     sems,
 ):
-    token_count, size = q_hbm.shape
+    token_count = joined_ref.shape[0]
     halves = members_ref.shape[0]
-    copies = [pltpu.make_async_copy(counts_hbm, counts_ref, sems.at[halves + 3])]
+    copies = [pltpu.make_async_copy(counts_hbm, counts_ref, sems.at[halves])]
     for half in range(halves):
         source = members_hbm.at[:, pl.ds(half * lane, lane)]
         copies.append(pltpu.make_async_copy(source, members_ref.at[half], sems.at[half]))
-    for at, source in enumerate((q_hbm, v_hbm, g_hbm)):
-        target = rows_ref.at[:, pl.ds(at * size, size)]
-        copies.append(pltpu.make_async_copy(source, target, sems.at[halves + at]))
     for copy in copies:
         copy.start()
-    for copy in copies[: halves + 1]:
+    for copy in copies:
         copy.wait()
     for group in range(tokens_ref.shape[0]):
         tokens_ref[group] = slot_tokens(members_ref, counts_ref, devices, group)
@@ -207,13 +213,10 @@
             )
             for at in range(part * step, (part + 1) * step)
         ]
-        if part == 0:
-            for copy in copies[halves + 1 :]:
-                copy.wait()
         span = pl.ds(part * step * rounds * bound, step * rounds * bound)
-        packed_ref[span, :] = dot_nn(jnp.concatenate(picks, axis=0), rows_ref[...]).astype(bf16)
+        packed_ref[span, :] = dot_nn(jnp.concatenate(picks, axis=0), joined_ref[...]).astype(bf16)
         copy = pltpu.make_async_copy(
-            packed_ref.at[span, :], send_hbm.at[span, :], sems.at[halves + 4 + part]
+            packed_ref.at[span, :], send_hbm.at[span, :], sems.at[halves + 1 + part]
         )
         copy.start()
         sends.append(copy)
@@ -235,8 +238,8 @@
         )
 
 
-def far_pack_kernel(pick_ref, q_ref, v_ref, g_ref, *send_refs):
-    rows = jnp.concatenate([q_ref[...], v_ref[...], g_ref[...]], axis=1)
+def far_pack_kernel(pick_ref, rows_ref, *send_refs):
+    rows = rows_ref[...]
     span = send_refs[0].shape[0]
     parts = 4
     count = len(send_refs) // parts
@@ -378,14 +381,11 @@
     seat = lax.axis_index("seq")
     rank_slots(rounds, devices, token_count, seat, tokens_ref, key_ref, value_ref)
 
-    def pick_device(device, carried):
-        at = pl.multiple_of(device * rounds * bound, rounds * bound)
-        pick_ref[pl.ds(at, rounds * bound), :] = pick_rows(
+    size = rounds * bound
+    for device in range(devices):
+        pick_ref[device * size : (device + 1) * size, :] = pick_rows(
             rounds, devices, bound, block_of(device, devices), token_count, key_ref, value_ref
         )
-        return carried
-
-    lax.fori_loop(0, devices, pick_device, 0, unroll=2)
     home_ref[...] = jnp.transpose(pick_ref[...])
 
 
@@ -765,20 +765,26 @@
     keys = [((per_device, rounds * devices, cap), f32)] * 2
     pick = ((devices * span, token_count), bf16)
     half = devices // 2
-    far_rows = [mirrored(rows) for rows in (qk, values, cot)]
+    (joined,) = call(
+        join_kernel,
+        [((token_count, 3 * size), bf16)],
+        [qk, values, cot],
+        remote=3,
+        semaphores=3,
+    )
+    far_rows = mirrored(joined)
     near_send, tokens = call(
         functools.partial(pack_kernel, rounds, devices, bound),
         [((half * span, 3 * size), bf16), (keys[0][0], jnp.int32)],
-        [counts, listed, qk, values, cot],
+        [joined, counts, listed],
         [((half * span, 3 * size), bf16)]
         + keys
         + [
             (counts.shape, jnp.int32),
             ((cap // lane, rounds * groups, lane), jnp.int32),
-            ((token_count, 3 * size), bf16),
         ],
-        remote=5,
-        semaphores=cap // lane + 8,
+        remote=2,
+        semaphores=cap // lane + 5,
         far=(0,),
         direct=(0,),
     )
@@ -811,7 +817,7 @@
     far_send = call(
         far_pack_kernel,
         [((span, 3 * size), bf16)] * half,
-        [far_pick] + far_rows,
+        [far_pick, far_rows],
         cost=50_000_000_000,
     )
     far_send, partner, tokens, home_place = lax.optimization_barrier(

time: 95 us -> 93.2 us (0.981)
  starting transfers between devices: 23.4 us -> 19.1 us
  waiting for transfers between devices: 7.17 us -> 10.3 us
  blocking collectives: 38.8 us -> 37.6 us
    ppermute x3 -> x1, starting transfers between devices: 7.03 us -> 4.1 us  [mirrored(): lax.ppermute(array, 'seq', [(i, (i + half) % devices) for i in range(devi...]
    ppermute x3 -> x1, waiting for transfers between devices: 0.01 us -> 2.64 us  [mirrored(): lax.ppermute(array, 'seq', [(i, (i + half) % devices) for i in range(devi...]
    ppermute x7, starting transfers between devices: 9.54 us -> 8.16 us  [crossed(): return lax.ppermute(array, 'seq', [(i, i ^ by) for i in range(devices)])]
    all_to_all x2, blocking collectives: 38.8 us -> 37.6 us  [exchange(): return lax.all_to_all(array, 'seq', split_axis=0, concat_axis=0, tiled=True)]
    ppermute x7, waiting for transfers between devices: 4.02 us -> 5.19 us  [crossed(): return lax.ppermute(array, 'seq', [(i, i ^ by) for i in range(devices)])]
    pallas_call x11 -> x12, Pallas kernels: 24.5 us -> 25.1 us  [call(): pl.pallas_call(kernel, out_shape=tuple((pltpu.HBM(shape, dtype) if at in...]
  transfers between devices with their start and end apart: 13 -> 11, of which waited for: 4 -> 6; matrix products, arithmetic and copies ran while one was open for 0% -> 0% of each run, Pallas kernels for 20% -> 20%
where the time goes in v6:
time: 93.2 us; the launch traced here: 92.8 us
  blocking collectives  37.6 us (40%)
  Pallas kernels  25.1 us (27%)
  starting transfers between devices  19.1 us (20%)
  waiting for transfers between devices  10.3 us (11%)
    all_to_all x2, blocking collectives, exchange(): return lax.all_to_all(array, 'seq', split_axis=0, concat_axis=0, tiled=True)  37.6 us
    pallas_call x12, Pallas kernels, call(): pl.pallas_call(kernel, out_shape=tuple((pltpu.HBM(shape, dtype) if at in...  25.1 us
    ppermute x7, starting transfers between devices, crossed(): return lax.ppermute(array, 'seq', [(i, i ^ by) for i in range(devices)])  8.16 us
    ppermute x7, waiting for transfers between devices, crossed(): return lax.ppermute(array, 'seq', [(i, i ^ by) for i in range(devices)])  5.19 us
    all_to_all x1, starting transfers between devices, exchange_in_half(): lax.all_to_all(array, 'seq', split_axis=0, concat_axis=0, tiled=True, axi...  4.75 us
    ppermute x1, starting transfers between devices, mirrored(): lax.ppermute(array, 'seq', [(i, (i + half) % devices) for i in range(devi...  4.1 us
    ppermute x1, waiting for transfers between devices, mirrored(): lax.ppermute(array, 'seq', [(i, (i + half) % devices) for i in range(devi...  2.64 us
    ppermute x2, waiting for transfers between devices, shifted(): lax.ppermute(array, 'seq', [(order[i], order[(i + by) % devices]) for i i...  2.48 us
  transfers between devices with their start and end apart: 11, of which 6 were waited for; matrix products, arithmetic and copies ran while one was open for 0% of the time, Pallas kernels for 20%

profile of v6, /device:TPU:0, one launch (start us, length us, event | category | flops | bytes accessed | tf_op | source)
XLA Modules:
  0.0 92.8 jit_solution(13268835121926483426)
XLA Ops:
  0.6 1.1 %shard_map.68.joined_ref = bf16[512,384]{1,0:T(8,128)(2,1)S(1)} custom-call(bf16[512,128]{1,0:T(8,128)(2,1)} %bitcast.11, bf16[512,128]{1,0:T(8,128)(2,1)} %bitcast.12, bf16[512,128]{1,0:T(8,128)(2,1)} %bitcast.13), custom_call_target="tpu_custom_call" | custom-call | tf_op jit(solution)/shard_map/pallas_call | solution.py:91
  1.7 4.1 %collective-permute-start = (bf16[512,384]{1,0:T(8,128)(2,1)S(1)}, bf16[512,384]{1,0:T(8,128)(2,1)S(1)}, u32[]{:S(2)}, u32[]{:S(2)}) collective-permute-start(bf16[512,384]{1,0:T(8,128)(2,1)S(1)} %shard_map.68.joined_ref), channel_id=1, source_target_pairs={{0,16},{2,18},{4,20},{6,22},{8,24},{10,26},{12,28},{14,30},{16,0},... | collective-permute-start | bytes 1179656 | tf_op jit(solution)/shard_map/ppermute | solution.py:741
  5.8 2.8 %shard_map.69 = (bf16[1024,384]{1,0:T(8,128)(2,1)}, s32[3,32,256]{2,1,0:T(8,128)S(1)}) custom-call(bf16[512,384]{1,0:T(8,128)(2,1)S(1)} %shard_map.68.joined_ref, s32[2,48]{1,0:T(2,128)} %bitcast.15, s32[96,256]{1,0:T(8,128)} %bitcast.14), custom_call_target="tpu_custom_call" | custom-call | tf_op jit(solution)/shard_map/pallas_call | solution.py:91
  8.6 4.7 %all-to-all-start = ((bf16[8,128,384]{2,1,0:T(8,128)(2,1)}), bf16[8,128,384]{2,1,0:T(8,128)(2,1)S(1)}, u32[]{:S(2)}, u32[]{:S(2)}) async-start(bf16[8,128,384]{2,1,0:T(8,128)(2,1)} %bitcast.10), calls=%async_computation | async-start | bytes 1572864 | tf_op jit(solution)/shard_map/all_to_all | solution.py:728
  13.4 0.7 shard_map.70.pick_ref
  14.0 0.2 shard_map.73
  14.3 6.5 %shard_map.72 = (bf16[2,128,1024]{2,1,0:T(8,128)(2,1)}, f32[8,256]{1,0:T(8,128)S(1)}) custom-call(s32[3,32,256]{2,1,0:T(8,128)S(1)} %get-tuple-element.77.tokens_ref), custom_call_target="tpu_custom_call" | custom-call | tf_op jit(solution)/shard_map/pallas_call | solution.py:91
  20.8 2.6 %collective-permute-done.rows_ref = bf16[512,384]{1,0:T(8,128)(2,1)S(1)} collective-permute-done((bf16[512,384]{1,0:T(8,128)(2,1)S(1)}, bf16[512,384]{1,0:T(8,128)(2,1)S(1)}, u32[]{:S(2)}, u32[]{:S(2)}) %collective-permute-start) | collective-permute-done | bytes 393248 | tf_op jit(solution)/shard_map/ppermute | solution.py:741
  23.4 0.7 shard_map.71
  24.1 1.6 %collective-permute-start.1 = (bf16[128,384]{1,0:T(8,128)(2,1)S(1)}, bf16[128,384]{1,0:T(8,128)(2,1)S(1)}, u32[]{:S(2)}, u32[]{:S(2)}) collective-permute-start(bf16[128,384]{1,0:T(8,128)(2,1)S(1)} %get-tuple-element.70), channel_id=1, source_target_pairs={{0,2},{2,0},{4,6},{6,4},{8,10},{10,8},{12,14},{14,12},{16,18},{18,... | collective-permute-start | bytes 294920 | tf_op jit(solution)/shard_map/ppermute | solution.py:735
  25.8 1.5 %collective-permute-start.2 = (bf16[128,384]{1,0:T(8,128)(2,1)S(1)}, bf16[128,384]{1,0:T(8,128)(2,1)S(1)}, u32[]{:S(2)}, u32[]{:S(2)}) collective-permute-start(bf16[128,384]{1,0:T(8,128)(2,1)S(1)} %get-tuple-element.71), channel_id=1, source_target_pairs={{0,4},{2,6},{4,0},{6,2},{8,12},{10,14},{12,8},{14,10},{16,20},{18,... | collective-permute-start | bytes 294920 | tf_op jit(solution)/shard_map/ppermute | solution.py:735
  27.3 0.4 collective-permute-start.3
  27.7 0.7 collective-permute-start.4
  28.4 2.3 %collective-permute-start.5 = (bf16[128,384]{1,0:T(8,128)(2,1)S(1)}, bf16[128,384]{1,0:T(8,128)(2,1)S(1)}, u32[]{:S(2)}, u32[]{:S(2)}) collective-permute-start(bf16[128,384]{1,0:T(8,128)(2,1)S(1)} %get-tuple-element.74), channel_id=1, source_target_pairs={{0,10},{2,8},{4,14},{6,12},{8,2},{10,0},{12,6},{14,4},{16,26},{18,... | collective-permute-start | bytes 294920 | tf_op jit(solution)/shard_map/ppermute | solution.py:735
  30.7 0.7 collective-permute-done.1.refs_1_
  31.4 0.9 collective-permute-start.6
  32.3 1.9 %collective-permute-done.2.refs_2_ = bf16[128,384]{1,0:T(8,128)(2,1)S(1)} collective-permute-done((bf16[128,384]{1,0:T(8,128)(2,1)S(1)}, bf16[128,384]{1,0:T(8,128)(2,1)S(1)}, u32[]{:S(2)}, u32[]{:S(2)}) %collective-permute-start.2) | collective-permute-done | bytes 98336 | tf_op jit(solution)/shard_map/ppermute | solution.py:735
  34.2 0.7 collective-permute-start.7
  34.9 3.9 %shard_map.74 = (bf16[2,1024,768]{2,1,0:T(8,128)(2,1)}, bf16[512,2048]{1,0:T(8,128)(2,1)}) custom-call(s32[3,32,256]{2,1,0:T(8,128)S(1)} %get-tuple-element.77.tokens_ref, f32[6,256]{1,0:T(8,128)S(1)} %get-tuple-element.78.home_place_ref), custom_call_target="tpu_custom_call" | custom-call | tf_op jit(solution)/shard_map/pallas_call | solution.py:91
  38.8 0.0 collective-permute-done.3.refs_3_
  38.8 0.0 collective-permute-done.4.refs_4_
  38.8 0.0 collective-permute-done.5.refs_5_
  38.8 0.5 collective-permute-done.6.refs_6_
  39.3 2.1 %collective-permute-done.7.refs_7_ = bf16[128,384]{1,0:T(8,128)(2,1)S(1)} collective-permute-done((bf16[128,384]{1,0:T(8,128)(2,1)S(1)}, bf16[128,384]{1,0:T(8,128)(2,1)S(1)}, u32[]{:S(2)}, u32[]{:S(2)}) %collective-permute-start.7) | collective-permute-done | bytes 98336 | tf_op jit(solution)/shard_map/ppermute | solution.py:735
  41.4 0.0 all-to-all-done.near_ref
  41.4 0.8 shard_map.75
  42.2 0.1 collective-permute-start.8
  42.2 2.0 %collective-permute-start.9 = (bf16[2,256,256]{2,1,0:T(8,128)(2,1)S(1)}, bf16[2,256,256]{2,1,0:T(8,128)(2,1)S(1)}, u32[]{:S(2)}, u32[]{:S(2)}) collective-permute-start(bf16[2,256,256]{2,1,0:T(8,128)(2,1)S(1)} %get-tuple-element.94.first_ref), channel_id=1, source_target_pairs={{0,4},{8,0},{16,8},{24,16},{26,24},{18,26},{10,18},{2,10},{6,2},{1... | collective-permute-start | bytes 786440 | tf_op jit(solution)/shard_map/ppermute | solution.py:751
  44.2 0.0 copy-start
  44.2 0.0 copy-start.2
  44.2 2.9 %shard_map.76 = (bf16[2,3,256,384]{3,2,1,0:T(8,128)(2,1)S(1)}, bf16[2,3,256,128]{3,2,1,0:T(8,128)(2,1)S(1)}, bf16[2,2,512,256]{3,2,1,0:T(8,128)(2,1)S(1)}, bf16[...) custom-call(f32[10,256]{1,0:T(8,128)S(1)} %get-tuple-element.82.fill, ...), custom_call_target="tpu_custom_call" | custom-call | tf_op jit(solution)/shard_map/pallas_call | solution.py:91
  47.2 2.5 %collective-permute-done.8.behind_ref = bf16[2,256,256]{2,1,0:T(8,128)(2,1)S(1)} collective-permute-done((bf16[2,256,256]{2,1,0:T(8,128)(2,1)S(1)}, bf16[2,256,256]{2,1,0:T(8,128)(2,1)S(1)}, u32[]{:S(2)}, u32[]{:S(2)}) %collective-permute-start.8) | collective-permute-done | bytes 262176 | tf_op jit(solution)/shard_map/ppermute | solution.py:751
  49.7 0.8 shard_map.77
  50.4 0.0 collective-permute-done.9.ahead_ref
  50.4 11.1 %all_to_all.22.everyone_ref = f32[16,24,128]{2,1,0:T(8,128)S(1)} all-to-all(f32[16,24,128]{2,1,0:T(8,128)S(1)} %get-tuple-element.100), channel_id=1, replica_groups=mesh['seq'=16,'head'=2] {'seq'}, dimensions={0} | all-to-all | bytes 393216 | tf_op jit(solution)/shard_map/all_to_all | solution.py:745
  61.6 0.0 copy-done
  61.6 0.0 copy-done.2
  61.6 3.4 %shard_map.78 = bf16[16,128,256]{2,1,0:T(8,128)(2,1)S(1)} custom-call(f32[10,256]{1,0:T(8,128)S(1)} %get-tuple-element.82.fill_ref, f32[16,24,128]{2,1,0:T(8,128)S(1)} %all_to_all.22.everyone_ref, bf16[2,128,1024]{2,1,0:T(8,128)(2,1)S(1)} %copy-done.2, f32[8,256]{1,0:T(8,128)S(1)} %get-tuple-element.102.low_ref, f32[12,256]{1,0:T(8,128)S(1)} %get-tuple-element.103.sums_ref, ...), custom_call_target="tpu_custom_call" | custom-call | tf_op jit(solution)/shard_map/pallas_call | solution.py:91
  65.0 0.0 copy-start.1
  65.0 26.4 %all_to_all.23 = bf16[16,128,256]{2,1,0:T(8,128)(2,1)S(1)} all-to-all(bf16[16,128,256]{2,1,0:T(8,128)(2,1)S(1)} %shard_map.78), channel_id=1, replica_groups=mesh['seq'=16,'head'=2] {'seq'}, dimensions={0} | all-to-all | bytes 2097152 | tf_op jit(solution)/shard_map/all_to_all | solution.py:745
  91.4 0.0 copy-done.1
  91.4 1.4 %shard_map.79 = (bf16[512,128]{1,0:T(8,128)(2,1)}, bf16[512,128]{1,0:T(8,128)(2,1)}) custom-call(bf16[512,2048]{1,0:T(8,128)(2,1)S(1)} %copy-done.1, bf16[2048,256]{1,0:T(8,128)(2,1)S(1)} %bitcast.9), custom_call_target="tpu_custom_call" | custom-call | tf_op jit(solution)/shard_map/pallas_call | solution.py:91
Async XLA Ops:
  1.7 21.7 %collective-permute-start = (bf16[512,384]{1,0:T(8,128)(2,1)S(1)}, bf16[512,384]{1,0:T(8,128)(2,1)S(1)}, u32[]{:S(2)}, u32[]{:S(2)}) collective-permute-start(bf16[512,384]{1,0:T(8,128)(2,1)S(1)} %shard_map.68.joined_ref), channel_id=1, source_target_pairs={{0,16},{2,18},{4,20},{6,22},{8,24},{10,26},{12,28},{14,30},{16,0},... | collective-permute-start | bytes 1179656 | tf_op jit(solution)/shard_map/ppermute | solution.py:741
  8.6 32.8 %all-to-all-start = ((bf16[8,128,384]{2,1,0:T(8,128)(2,1)}), bf16[8,128,384]{2,1,0:T(8,128)(2,1)S(1)}, u32[]{:S(2)}, u32[]{:S(2)}) async-start(bf16[8,128,384]{2,1,0:T(8,128)(2,1)} %bitcast.10), calls=%async_computation | async-start | bytes 1572864 | tf_op jit(solution)/shard_map/all_to_all | solution.py:728
  24.1 7.3 %collective-permute-start.1 = (bf16[128,384]{1,0:T(8,128)(2,1)S(1)}, bf16[128,384]{1,0:T(8,128)(2,1)S(1)}, u32[]{:S(2)}, u32[]{:S(2)}) collective-permute-start(bf16[128,384]{1,0:T(8,128)(2,1)S(1)} %get-tuple-element.70), channel_id=1, source_target_pairs={{0,2},{2,0},{4,6},{6,4},{8,10},{10,8},{12,14},{14,12},{16,18},{18,... | collective-permute-start | bytes 294920 | tf_op jit(solution)/shard_map/ppermute | solution.py:735
  25.8 8.4 %collective-permute-start.2 = (bf16[128,384]{1,0:T(8,128)(2,1)S(1)}, bf16[128,384]{1,0:T(8,128)(2,1)S(1)}, u32[]{:S(2)}, u32[]{:S(2)}) collective-permute-start(bf16[128,384]{1,0:T(8,128)(2,1)S(1)} %get-tuple-element.71), channel_id=1, source_target_pairs={{0,4},{2,6},{4,0},{6,2},{8,12},{10,14},{12,8},{14,10},{16,20},{18,... | collective-permute-start | bytes 294920 | tf_op jit(solution)/shard_map/ppermute | solution.py:735
  27.3 11.5 %collective-permute-start.3 = (bf16[128,384]{1,0:T(8,128)(2,1)S(1)}, bf16[128,384]{1,0:T(8,128)(2,1)S(1)}, u32[]{:S(2)}, u32[]{:S(2)}) collective-permute-start(bf16[128,384]{1,0:T(8,128)(2,1)S(1)} %get-tuple-element.72), channel_id=1, source_target_pairs={{0,6},{2,4},{4,2},{6,0},{8,14},{10,12},{12,10},{14,8},{16,22},{18,... | collective-permute-start | bytes 294920 | tf_op jit(solution)/shard_map/ppermute | solution.py:735
  27.7 11.1 %collective-permute-start.4 = (bf16[128,384]{1,0:T(8,128)(2,1)S(1)}, bf16[128,384]{1,0:T(8,128)(2,1)S(1)}, u32[]{:S(2)}, u32[]{:S(2)}) collective-permute-start(bf16[128,384]{1,0:T(8,128)(2,1)S(1)} %get-tuple-element.73), channel_id=1, source_target_pairs={{0,8},{2,10},{4,12},{6,14},{8,0},{10,2},{12,4},{14,6},{16,24},{18,... | collective-permute-start | bytes 294920 | tf_op jit(solution)/shard_map/ppermute | solution.py:735
  28.4 10.4 %collective-permute-start.5 = (bf16[128,384]{1,0:T(8,128)(2,1)S(1)}, bf16[128,384]{1,0:T(8,128)(2,1)S(1)}, u32[]{:S(2)}, u32[]{:S(2)}) collective-permute-start(bf16[128,384]{1,0:T(8,128)(2,1)S(1)} %get-tuple-element.74), channel_id=1, source_target_pairs={{0,10},{2,8},{4,14},{6,12},{8,2},{10,0},{12,6},{14,4},{16,26},{18,... | collective-permute-start | bytes 294920 | tf_op jit(solution)/shard_map/ppermute | solution.py:735
  31.4 7.9 %collective-permute-start.6 = (bf16[128,384]{1,0:T(8,128)(2,1)S(1)}, bf16[128,384]{1,0:T(8,128)(2,1)S(1)}, u32[]{:S(2)}, u32[]{:S(2)}) collective-permute-start(bf16[128,384]{1,0:T(8,128)(2,1)S(1)} %get-tuple-element.75), channel_id=1, source_target_pairs={{0,12},{2,14},{4,8},{6,10},{8,4},{10,6},{12,0},{14,2},{16,28},{18,... | collective-permute-start | bytes 294920 | tf_op jit(solution)/shard_map/ppermute | solution.py:735
  34.2 7.2 %collective-permute-start.7 = (bf16[128,384]{1,0:T(8,128)(2,1)S(1)}, bf16[128,384]{1,0:T(8,128)(2,1)S(1)}, u32[]{:S(2)}, u32[]{:S(2)}) collective-permute-start(bf16[128,384]{1,0:T(8,128)(2,1)S(1)} %get-tuple-element.76), channel_id=1, source_target_pairs={{0,14},{2,12},{4,10},{6,8},{8,6},{10,4},{12,2},{14,0},{16,30},{18,... | collective-permute-start | bytes 294920 | tf_op jit(solution)/shard_map/ppermute | solution.py:735
  42.2 7.5 %collective-permute-start.8 = (bf16[2,256,256]{2,1,0:T(8,128)(2,1)S(1)}, bf16[2,256,256]{2,1,0:T(8,128)(2,1)S(1)}, u32[]{:S(2)}, u32[]{:S(2)}) collective-permute-start(bf16[2,256,256]{2,1,0:T(8,128)(2,1)S(1)} %get-tuple-element.93.last_ref), channel_id=1, source_target_pairs={{0,8},{8,16},{16,24},{24,26},{26,18},{18,10},{10,2},{2,6},{6,14},{... | collective-permute-start | bytes 786440 | tf_op jit(solution)/shard_map/ppermute | solution.py:751
  42.2 8.2 %collective-permute-start.9 = (bf16[2,256,256]{2,1,0:T(8,128)(2,1)S(1)}, bf16[2,256,256]{2,1,0:T(8,128)(2,1)S(1)}, u32[]{:S(2)}, u32[]{:S(2)}) collective-permute-start(bf16[2,256,256]{2,1,0:T(8,128)(2,1)S(1)} %get-tuple-element.94.first_ref), channel_id=1, source_target_pairs={{0,4},{8,0},{16,8},{24,16},{26,24},{18,26},{10,18},{2,10},{6,2},{1... | collective-permute-start | bytes 786440 | tf_op jit(solution)/shard_map/ppermute | solution.py:751
  44.2 17.3 %copy-start = (bf16[2,1024,768]{2,1,0:T(8,128)(2,1)S(1)}, bf16[2,1024,768]{2,1,0:T(8,128)(2,1)}, u32[]{:S(2)}) copy-start(bf16[2,1024,768]{2,1,0:T(8,128)(2,1)} %get-tuple-element.111.spread_t_ref) | copy-start | bytes 9437188
  44.2 17.3 %copy-start.2 = (bf16[2,128,1024]{2,1,0:T(8,128)(2,1)S(1)}, bf16[2,128,1024]{2,1,0:T(8,128)(2,1)}, u32[]{:S(2)}) copy-start(bf16[2,128,1024]{2,1,0:T(8,128)(2,1)} %get-tuple-element.101.partner_ref) | copy-start | bytes 1572868
  65.0 26.4 %copy-start.1 = (bf16[512,2048]{1,0:T(8,128)(2,1)S(1)}, bf16[512,2048]{1,0:T(8,128)(2,1)}, u32[]{:S(2)}) copy-start(bf16[512,2048]{1,0:T(8,128)(2,1)} %get-tuple-element.81.home_ref) | copy-start | bytes 6291460

commit v7 on v6

--- a/solution.py
+++ b/solution.py
@@ -232,7 +232,7 @@
     rank_slots(rounds, devices, token_count, source, tokens_ref, key_ref, value_ref)
     size = rounds * bound
     for at in range(half):
-        block = block_of(first + jnp.bitwise_xor(me - first, at), devices)
+        block = block_of(first + jnp.bitwise_xor(me - first, -at % half), devices)
         pick_ref[at * size : (at + 1) * size, :] = pick_rows(
             rounds, devices, bound, block, token_count, key_ref, value_ref
         )
@@ -261,7 +261,8 @@
     home_place = source.astype(f32) * bound + 1.0
     first = seat // half * half
     near = (source >= first) & (source < first + half)
-    crossed = half + jnp.bitwise_xor(source % half, seat - first)
+    bits = jnp.bitwise_xor(source % half, seat - first)
+    crossed = half + jnp.where(bits > 0, half - bits, 0)
     source_place = jnp.where(near, source - first, crossed).astype(f32) * bound + 1.0
     for r in range(rounds):
         carry = jnp.zeros((devices, 1), f32)
@@ -823,7 +824,7 @@
     far_send, partner, tokens, home_place = lax.optimization_barrier(
         (far_send, partner, tokens, home_place)
     )
-    far = [far_send[0]] + [crossed(far_send[by], by) for by in range(1, half)]
+    far = [far_send[0]] + [crossed(far_send[at], half - at) for at in range(1, half)]
     spread_t, home_pick = call(
         functools.partial(return_index_kernel, rounds, devices, bound, token_count),
         [((rounds, buffer_rows, slots), bf16), ((token_count, devices * span), bf16)],

time: 93.2 us -> 92.4 us (level)
  starting transfers between devices: 19.1 us -> 21 us
  blocking collectives: 37.6 us -> 36.1 us
  waiting for transfers between devices: 10.3 us -> 9.06 us
    ppermute x7, starting transfers between devices: 8.16 us -> 10.1 us  [crossed(): return lax.ppermute(array, 'seq', [(i, i ^ by) for i in range(devices)])]
    all_to_all x2, blocking collectives: 37.6 us -> 36.1 us  [exchange(): return lax.all_to_all(array, 'seq', split_axis=0, concat_axis=0, tiled=True)]
    ppermute x2, waiting for transfers between devices: 2.48 us -> 1.42 us  [shifted(): lax.ppermute(array, 'seq', [(order[i], order[(i + by) % devices]) for i i...]
  transfers between devices with their start and end apart: 11 -> 11, of which waited for: 6 -> 4; matrix products, arithmetic and copies ran while one was open for 0% -> 0% of each run, Pallas kernels for 20% -> 20%
where the time goes in v7:
time: 92.4 us; the launch traced here: 92.1 us
  blocking collectives  36.1 us (39%)
  Pallas kernels  25.1 us (27%)
  starting transfers between devices  21 us (23%)
  waiting for transfers between devices  9.06 us (10%)
    all_to_all x2, blocking collectives, exchange(): return lax.all_to_all(array, 'seq', split_axis=0, concat_axis=0, tiled=True)  36.1 us
    pallas_call x12, Pallas kernels, call(): pl.pallas_call(kernel, out_shape=tuple((pltpu.HBM(shape, dtype) if at in...  25.1 us
    ppermute x7, starting transfers between devices, crossed(): return lax.ppermute(array, 'seq', [(i, i ^ by) for i in range(devices)])  10.1 us
    ppermute x7, waiting for transfers between devices, crossed(): return lax.ppermute(array, 'seq', [(i, i ^ by) for i in range(devices)])  5 us
    all_to_all x1, starting transfers between devices, exchange_in_half(): lax.all_to_all(array, 'seq', split_axis=0, concat_axis=0, tiled=True, axi...  4.75 us
    ppermute x1, starting transfers between devices, mirrored(): lax.ppermute(array, 'seq', [(i, (i + half) % devices) for i in range(devi...  4.1 us
    ppermute x1, waiting for transfers between devices, mirrored(): lax.ppermute(array, 'seq', [(i, (i + half) % devices) for i in range(devi...  2.64 us
    ppermute x2, starting transfers between devices, shifted(): lax.ppermute(array, 'seq', [(order[i], order[(i + by) % devices]) for i i...  2.07 us
  transfers between devices with their start and end apart: 11, of which 4 were waited for; matrix products, arithmetic and copies ran while one was open for 0% of the time, Pallas kernels for 20%

profile of v7, /device:TPU:0, one launch (start us, length us, event | category | flops | bytes accessed | tf_op | source)
XLA Modules:
  0.0 92.1 jit_solution(4396353704199220697)
XLA Ops:
  0.6 1.1 %shard_map.68.joined_ref = bf16[512,384]{1,0:T(8,128)(2,1)S(1)} custom-call(bf16[512,128]{1,0:T(8,128)(2,1)} %bitcast.11, bf16[512,128]{1,0:T(8,128)(2,1)} %bitcast.12, bf16[512,128]{1,0:T(8,128)(2,1)} %bitcast.13), custom_call_target="tpu_custom_call" | custom-call | tf_op jit(solution)/shard_map/pallas_call | solution.py:91
  1.7 4.1 %collective-permute-start = (bf16[512,384]{1,0:T(8,128)(2,1)S(1)}, bf16[512,384]{1,0:T(8,128)(2,1)S(1)}, u32[]{:S(2)}, u32[]{:S(2)}) collective-permute-start(bf16[512,384]{1,0:T(8,128)(2,1)S(1)} %shard_map.68.joined_ref), channel_id=1, source_target_pairs={{0,16},{2,18},{4,20},{6,22},{8,24},{10,26},{12,28},{14,30},{16,0},... | collective-permute-start | bytes 1179656 | tf_op jit(solution)/shard_map/ppermute | solution.py:742
  5.8 2.8 %shard_map.69 = (bf16[1024,384]{1,0:T(8,128)(2,1)}, s32[3,32,256]{2,1,0:T(8,128)S(1)}) custom-call(bf16[512,384]{1,0:T(8,128)(2,1)S(1)} %shard_map.68.joined_ref, s32[2,48]{1,0:T(2,128)} %bitcast.15, s32[96,256]{1,0:T(8,128)} %bitcast.14), custom_call_target="tpu_custom_call" | custom-call | tf_op jit(solution)/shard_map/pallas_call | solution.py:91
  8.6 4.7 %all-to-all-start = ((bf16[8,128,384]{2,1,0:T(8,128)(2,1)}), bf16[8,128,384]{2,1,0:T(8,128)(2,1)S(1)}, u32[]{:S(2)}, u32[]{:S(2)}) async-start(bf16[8,128,384]{2,1,0:T(8,128)(2,1)} %bitcast.10), calls=%async_computation | async-start | bytes 1572864 | tf_op jit(solution)/shard_map/all_to_all | solution.py:729
  13.4 0.7 shard_map.70.pick_ref
  14.0 0.2 shard_map.73
  14.3 6.5 %shard_map.72 = (bf16[2,128,1024]{2,1,0:T(8,128)(2,1)}, f32[8,256]{1,0:T(8,128)S(1)}) custom-call(s32[3,32,256]{2,1,0:T(8,128)S(1)} %get-tuple-element.77.tokens_ref), custom_call_target="tpu_custom_call" | custom-call | tf_op jit(solution)/shard_map/pallas_call | solution.py:91
  20.8 2.6 %collective-permute-done.rows_ref = bf16[512,384]{1,0:T(8,128)(2,1)S(1)} collective-permute-done((bf16[512,384]{1,0:T(8,128)(2,1)S(1)}, bf16[512,384]{1,0:T(8,128)(2,1)S(1)}, u32[]{:S(2)}, u32[]{:S(2)}) %collective-permute-start) | collective-permute-done | bytes 393248 | tf_op jit(solution)/shard_map/ppermute | solution.py:742
  23.4 0.7 shard_map.71
  24.1 2.6 %collective-permute-start.1 = (bf16[128,384]{1,0:T(8,128)(2,1)S(1)}, bf16[128,384]{1,0:T(8,128)(2,1)S(1)}, u32[]{:S(2)}, u32[]{:S(2)}) collective-permute-start(bf16[128,384]{1,0:T(8,128)(2,1)S(1)} %get-tuple-element.70), channel_id=1, source_target_pairs={{0,14},{2,12},{4,10},{6,8},{8,6},{10,4},{12,2},{14,0},{16,30},{18,... | collective-permute-start | bytes 294920 | tf_op jit(solution)/shard_map/ppermute | solution.py:736
  26.8 1.4 %collective-permute-start.2 = (bf16[128,384]{1,0:T(8,128)(2,1)S(1)}, bf16[128,384]{1,0:T(8,128)(2,1)S(1)}, u32[]{:S(2)}, u32[]{:S(2)}) collective-permute-start(bf16[128,384]{1,0:T(8,128)(2,1)S(1)} %get-tuple-element.71), channel_id=1, source_target_pairs={{0,12},{2,14},{4,8},{6,10},{8,4},{10,6},{12,0},{14,2},{16,28},{18,... | collective-permute-start | bytes 294920 | tf_op jit(solution)/shard_map/ppermute | solution.py:736
  28.1 0.6 collective-permute-start.3
  28.7 1.4 %collective-permute-start.4 = (bf16[128,384]{1,0:T(8,128)(2,1)S(1)}, bf16[128,384]{1,0:T(8,128)(2,1)S(1)}, u32[]{:S(2)}, u32[]{:S(2)}) collective-permute-start(bf16[128,384]{1,0:T(8,128)(2,1)S(1)} %get-tuple-element.73), channel_id=1, source_target_pairs={{0,8},{2,10},{4,12},{6,14},{8,0},{10,2},{12,4},{14,6},{16,24},{18,... | collective-permute-start | bytes 294920 | tf_op jit(solution)/shard_map/ppermute | solution.py:736
  30.1 2.5 %collective-permute-start.5 = (bf16[128,384]{1,0:T(8,128)(2,1)S(1)}, bf16[128,384]{1,0:T(8,128)(2,1)S(1)}, u32[]{:S(2)}, u32[]{:S(2)}) collective-permute-start(bf16[128,384]{1,0:T(8,128)(2,1)S(1)} %get-tuple-element.74), channel_id=1, source_target_pairs={{0,6},{2,4},{4,2},{6,0},{8,14},{10,12},{12,10},{14,8},{16,22},{18,... | collective-permute-start | bytes 294920 | tf_op jit(solution)/shard_map/ppermute | solution.py:736
  32.6 4.3 %collective-permute-done.1.refs_1_ = bf16[128,384]{1,0:T(8,128)(2,1)S(1)} collective-permute-done((bf16[128,384]{1,0:T(8,128)(2,1)S(1)}, bf16[128,384]{1,0:T(8,128)(2,1)S(1)}, u32[]{:S(2)}, u32[]{:S(2)}) %collective-permute-start.1) | collective-permute-done | bytes 98336 | tf_op jit(solution)/shard_map/ppermute | solution.py:736
  36.9 0.6 collective-permute-start.6
  37.5 0.6 collective-permute-done.2.refs_2_
  38.1 1.1 %collective-permute-start.7 = (bf16[128,384]{1,0:T(8,128)(2,1)S(1)}, bf16[128,384]{1,0:T(8,128)(2,1)S(1)}, u32[]{:S(2)}, u32[]{:S(2)}) collective-permute-start(bf16[128,384]{1,0:T(8,128)(2,1)S(1)} %get-tuple-element.76), channel_id=1, source_target_pairs={{0,2},{2,0},{4,6},{6,4},{8,10},{10,8},{12,14},{14,12},{16,18},{18,... | collective-permute-start | bytes 294920 | tf_op jit(solution)/shard_map/ppermute | solution.py:736
  39.2 3.9 %shard_map.74 = (bf16[2,1024,768]{2,1,0:T(8,128)(2,1)}, bf16[512,2048]{1,0:T(8,128)(2,1)}) custom-call(s32[3,32,256]{2,1,0:T(8,128)S(1)} %get-tuple-element.77.tokens_ref, f32[6,256]{1,0:T(8,128)S(1)} %get-tuple-element.78.home_place_ref), custom_call_target="tpu_custom_call" | custom-call | tf_op jit(solution)/shard_map/pallas_call | solution.py:91
  43.1 0.0 collective-permute-done.3.refs_3_
  43.1 0.0 collective-permute-done.4.refs_4_
  43.1 0.0 collective-permute-done.5.refs_5_
  43.1 0.0 collective-permute-done.6.refs_6_
  43.1 0.0 collective-permute-done.7.refs_7_
  43.1 0.0 all-to-all-done.near_ref
  43.1 0.8 shard_map.75
  43.9 0.1 collective-permute-start.8
  44.0 2.0 %collective-permute-start.9 = (bf16[2,256,256]{2,1,0:T(8,128)(2,1)S(1)}, bf16[2,256,256]{2,1,0:T(8,128)(2,1)S(1)}, u32[]{:S(2)}, u32[]{:S(2)}) collective-permute-start(bf16[2,256,256]{2,1,0:T(8,128)(2,1)S(1)} %get-tuple-element.94.first_ref), channel_id=1, source_target_pairs={{0,4},{8,0},{16,8},{24,16},{26,24},{18,26},{10,18},{2,10},{6,2},{1... | collective-permute-start | bytes 786440 | tf_op jit(solution)/shard_map/ppermute | solution.py:752
  46.0 0.0 copy-start
  46.0 0.0 copy-start.2
  46.0 2.9 %shard_map.76 = (bf16[2,3,256,384]{3,2,1,0:T(8,128)(2,1)S(1)}, bf16[2,3,256,128]{3,2,1,0:T(8,128)(2,1)S(1)}, bf16[2,2,512,256]{3,2,1,0:T(8,128)(2,1)S(1)}, bf16[...) custom-call(f32[10,256]{1,0:T(8,128)S(1)} %get-tuple-element.82.fill, ...), custom_call_target="tpu_custom_call" | custom-call | tf_op jit(solution)/shard_map/pallas_call | solution.py:91
  48.9 1.4 %collective-permute-done.8.behind_ref = bf16[2,256,256]{2,1,0:T(8,128)(2,1)S(1)} collective-permute-done((bf16[2,256,256]{2,1,0:T(8,128)(2,1)S(1)}, bf16[2,256,256]{2,1,0:T(8,128)(2,1)S(1)}, u32[]{:S(2)}, u32[]{:S(2)}) %collective-permute-start.8) | collective-permute-done | bytes 262176 | tf_op jit(solution)/shard_map/ppermute | solution.py:752
  50.3 0.8 shard_map.77
  51.1 0.0 collective-permute-done.9.ahead_ref
  51.1 11.7 %all_to_all.22.everyone_ref = f32[16,24,128]{2,1,0:T(8,128)S(1)} all-to-all(f32[16,24,128]{2,1,0:T(8,128)S(1)} %get-tuple-element.100), channel_id=1, replica_groups=mesh['seq'=16,'head'=2] {'seq'}, dimensions={0} | all-to-all | bytes 393216 | tf_op jit(solution)/shard_map/all_to_all | solution.py:746
  62.8 0.0 copy-done
  62.8 0.0 copy-done.2
  62.8 3.4 %shard_map.78 = bf16[16,128,256]{2,1,0:T(8,128)(2,1)S(1)} custom-call(f32[10,256]{1,0:T(8,128)S(1)} %get-tuple-element.82.fill_ref, f32[16,24,128]{2,1,0:T(8,128)S(1)} %all_to_all.22.everyone_ref, bf16[2,128,1024]{2,1,0:T(8,128)(2,1)S(1)} %copy-done.2, f32[8,256]{1,0:T(8,128)S(1)} %get-tuple-element.102.low_ref, f32[12,256]{1,0:T(8,128)S(1)} %get-tuple-element.103.sums_ref, ...), custom_call_target="tpu_custom_call" | custom-call | tf_op jit(solution)/shard_map/pallas_call | solution.py:91
  66.2 0.0 copy-start.1
  66.2 24.5 %all_to_all.23 = bf16[16,128,256]{2,1,0:T(8,128)(2,1)S(1)} all-to-all(bf16[16,128,256]{2,1,0:T(8,128)(2,1)S(1)} %shard_map.78), channel_id=1, replica_groups=mesh['seq'=16,'head'=2] {'seq'}, dimensions={0} | all-to-all | bytes 2097152 | tf_op jit(solution)/shard_map/all_to_all | solution.py:746
  90.7 0.0 copy-done.1
  90.7 1.4 %shard_map.79 = (bf16[512,128]{1,0:T(8,128)(2,1)}, bf16[512,128]{1,0:T(8,128)(2,1)}) custom-call(bf16[512,2048]{1,0:T(8,128)(2,1)S(1)} %copy-done.1, bf16[2048,256]{1,0:T(8,128)(2,1)S(1)} %bitcast.9), custom_call_target="tpu_custom_call" | custom-call | tf_op jit(solution)/shard_map/pallas_call | solution.py:91
Async XLA Ops:
  1.7 21.7 %collective-permute-start = (bf16[512,384]{1,0:T(8,128)(2,1)S(1)}, bf16[512,384]{1,0:T(8,128)(2,1)S(1)}, u32[]{:S(2)}, u32[]{:S(2)}) collective-permute-start(bf16[512,384]{1,0:T(8,128)(2,1)S(1)} %shard_map.68.joined_ref), channel_id=1, source_target_pairs={{0,16},{2,18},{4,20},{6,22},{8,24},{10,26},{12,28},{14,30},{16,0},... | collective-permute-start | bytes 1179656 | tf_op jit(solution)/shard_map/ppermute | solution.py:742
  8.6 34.5 %all-to-all-start = ((bf16[8,128,384]{2,1,0:T(8,128)(2,1)}), bf16[8,128,384]{2,1,0:T(8,128)(2,1)S(1)}, u32[]{:S(2)}, u32[]{:S(2)}) async-start(bf16[8,128,384]{2,1,0:T(8,128)(2,1)} %bitcast.10), calls=%async_computation | async-start | bytes 1572864 | tf_op jit(solution)/shard_map/all_to_all | solution.py:729
  24.1 12.8 %collective-permute-start.1 = (bf16[128,384]{1,0:T(8,128)(2,1)S(1)}, bf16[128,384]{1,0:T(8,128)(2,1)S(1)}, u32[]{:S(2)}, u32[]{:S(2)}) collective-permute-start(bf16[128,384]{1,0:T(8,128)(2,1)S(1)} %get-tuple-element.70), channel_id=1, source_target_pairs={{0,14},{2,12},{4,10},{6,8},{8,6},{10,4},{12,2},{14,0},{16,30},{18,... | collective-permute-start | bytes 294920 | tf_op jit(solution)/shard_map/ppermute | solution.py:736
  26.8 11.4 %collective-permute-start.2 = (bf16[128,384]{1,0:T(8,128)(2,1)S(1)}, bf16[128,384]{1,0:T(8,128)(2,1)S(1)}, u32[]{:S(2)}, u32[]{:S(2)}) collective-permute-start(bf16[128,384]{1,0:T(8,128)(2,1)S(1)} %get-tuple-element.71), channel_id=1, source_target_pairs={{0,12},{2,14},{4,8},{6,10},{8,4},{10,6},{12,0},{14,2},{16,28},{18,... | collective-permute-start | bytes 294920 | tf_op jit(solution)/shard_map/ppermute | solution.py:736
  28.1 15.0 %collective-permute-start.3 = (bf16[128,384]{1,0:T(8,128)(2,1)S(1)}, bf16[128,384]{1,0:T(8,128)(2,1)S(1)}, u32[]{:S(2)}, u32[]{:S(2)}) collective-permute-start(bf16[128,384]{1,0:T(8,128)(2,1)S(1)} %get-tuple-element.72), channel_id=1, source_target_pairs={{0,10},{2,8},{4,14},{6,12},{8,2},{10,0},{12,6},{14,4},{16,26},{18,... | collective-permute-start | bytes 294920 | tf_op jit(solution)/shard_map/ppermute | solution.py:736
  28.7 14.4 %collective-permute-start.4 = (bf16[128,384]{1,0:T(8,128)(2,1)S(1)}, bf16[128,384]{1,0:T(8,128)(2,1)S(1)}, u32[]{:S(2)}, u32[]{:S(2)}) collective-permute-start(bf16[128,384]{1,0:T(8,128)(2,1)S(1)} %get-tuple-element.73), channel_id=1, source_target_pairs={{0,8},{2,10},{4,12},{6,14},{8,0},{10,2},{12,4},{14,6},{16,24},{18,... | collective-permute-start | bytes 294920 | tf_op jit(solution)/shard_map/ppermute | solution.py:736
  30.1 13.0 %collective-permute-start.5 = (bf16[128,384]{1,0:T(8,128)(2,1)S(1)}, bf16[128,384]{1,0:T(8,128)(2,1)S(1)}, u32[]{:S(2)}, u32[]{:S(2)}) collective-permute-start(bf16[128,384]{1,0:T(8,128)(2,1)S(1)} %get-tuple-element.74), channel_id=1, source_target_pairs={{0,6},{2,4},{4,2},{6,0},{8,14},{10,12},{12,10},{14,8},{16,22},{18,... | collective-permute-start | bytes 294920 | tf_op jit(solution)/shard_map/ppermute | solution.py:736
  36.9 6.2 %collective-permute-start.6 = (bf16[128,384]{1,0:T(8,128)(2,1)S(1)}, bf16[128,384]{1,0:T(8,128)(2,1)S(1)}, u32[]{:S(2)}, u32[]{:S(2)}) collective-permute-start(bf16[128,384]{1,0:T(8,128)(2,1)S(1)} %get-tuple-element.75), channel_id=1, source_target_pairs={{0,4},{2,6},{4,0},{6,2},{8,12},{10,14},{12,8},{14,10},{16,20},{18,... | collective-permute-start | bytes 294920 | tf_op jit(solution)/shard_map/ppermute | solution.py:736
  38.1 5.0 %collective-permute-start.7 = (bf16[128,384]{1,0:T(8,128)(2,1)S(1)}, bf16[128,384]{1,0:T(8,128)(2,1)S(1)}, u32[]{:S(2)}, u32[]{:S(2)}) collective-permute-start(bf16[128,384]{1,0:T(8,128)(2,1)S(1)} %get-tuple-element.76), channel_id=1, source_target_pairs={{0,2},{2,0},{4,6},{6,4},{8,10},{10,8},{12,14},{14,12},{16,18},{18,... | collective-permute-start | bytes 294920 | tf_op jit(solution)/shard_map/ppermute | solution.py:736
  43.9 6.4 %collective-permute-start.8 = (bf16[2,256,256]{2,1,0:T(8,128)(2,1)S(1)}, bf16[2,256,256]{2,1,0:T(8,128)(2,1)S(1)}, u32[]{:S(2)}, u32[]{:S(2)}) collective-permute-start(bf16[2,256,256]{2,1,0:T(8,128)(2,1)S(1)} %get-tuple-element.93.last_ref), channel_id=1, source_target_pairs={{0,8},{8,16},{16,24},{24,26},{26,18},{18,10},{10,2},{2,6},{6,14},{... | collective-permute-start | bytes 786440 | tf_op jit(solution)/shard_map/ppermute | solution.py:752
  44.0 7.1 %collective-permute-start.9 = (bf16[2,256,256]{2,1,0:T(8,128)(2,1)S(1)}, bf16[2,256,256]{2,1,0:T(8,128)(2,1)S(1)}, u32[]{:S(2)}, u32[]{:S(2)}) collective-permute-start(bf16[2,256,256]{2,1,0:T(8,128)(2,1)S(1)} %get-tuple-element.94.first_ref), channel_id=1, source_target_pairs={{0,4},{8,0},{16,8},{24,16},{26,24},{18,26},{10,18},{2,10},{6,2},{1... | collective-permute-start | bytes 786440 | tf_op jit(solution)/shard_map/ppermute | solution.py:752
  46.0 16.8 %copy-start = (bf16[2,1024,768]{2,1,0:T(8,128)(2,1)S(1)}, bf16[2,1024,768]{2,1,0:T(8,128)(2,1)}, u32[]{:S(2)}) copy-start(bf16[2,1024,768]{2,1,0:T(8,128)(2,1)} %get-tuple-element.111.spread_t_ref) | copy-start | bytes 9437188
  46.0 16.8 %copy-start.2 = (bf16[2,128,1024]{2,1,0:T(8,128)(2,1)S(1)}, bf16[2,128,1024]{2,1,0:T(8,128)(2,1)}, u32[]{:S(2)}) copy-start(bf16[2,128,1024]{2,1,0:T(8,128)(2,1)} %get-tuple-element.101.partner_ref) | copy-start | bytes 1572868
  66.2 24.5 %copy-start.1 = (bf16[512,2048]{1,0:T(8,128)(2,1)S(1)}, bf16[512,2048]{1,0:T(8,128)(2,1)}, u32[]{:S(2)}) copy-start(bf16[512,2048]{1,0:T(8,128)(2,1)} %get-tuple-element.81.home_ref) | copy-start | bytes 6291460

commit v8 on v7

--- a/solution.py
+++ b/solution.py
@@ -186,7 +186,8 @@
     copies = [pltpu.make_async_copy(counts_hbm, counts_ref, sems.at[halves])]
     for half in range(halves):
         source = members_hbm.at[:, pl.ds(half * lane, lane)]
-        copies.append(pltpu.make_async_copy(source, members_ref.at[half], sems.at[half]))
+        target = members_ref.at[half, pl.ds(0, members_hbm.shape[0])]
+        copies.append(pltpu.make_async_copy(source, target, sems.at[half]))
     for copy in copies:
         copy.start()
     for copy in copies:
@@ -782,7 +783,7 @@
         + keys
         + [
             (counts.shape, jnp.int32),
-            ((cap // lane, rounds * groups, lane), jnp.int32),
+            ((cap // lane, rounds * groups + 8 * per_device, lane), jnp.int32),
         ],
         remote=2,
         semaphores=cap // lane + 5,

time: 92.4 us -> 92.4 us (level)
  no operation moved by 1% of the time
where the time goes in v8:
time: 92.4 us; the launch traced here: 92.1 us
  blocking collectives  36.1 us (39%)
  Pallas kernels  25.1 us (27%)
  starting transfers between devices  21 us (23%)
  waiting for transfers between devices  9.06 us (10%)
    all_to_all x2, blocking collectives, exchange(): return lax.all_to_all(array, 'seq', split_axis=0, concat_axis=0, tiled=True)  36.1 us
    pallas_call x12, Pallas kernels, call(): pl.pallas_call(kernel, out_shape=tuple((pltpu.HBM(shape, dtype) if at in...  25.1 us
    ppermute x7, starting transfers between devices, crossed(): return lax.ppermute(array, 'seq', [(i, i ^ by) for i in range(devices)])  10.1 us
    ppermute x7, waiting for transfers between devices, crossed(): return lax.ppermute(array, 'seq', [(i, i ^ by) for i in range(devices)])  5 us
    all_to_all x1, starting transfers between devices, exchange_in_half(): lax.all_to_all(array, 'seq', split_axis=0, concat_axis=0, tiled=True, axi...  4.75 us
    ppermute x1, starting transfers between devices, mirrored(): lax.ppermute(array, 'seq', [(i, (i + half) % devices) for i in range(devi...  4.1 us
    ppermute x1, waiting for transfers between devices, mirrored(): lax.ppermute(array, 'seq', [(i, (i + half) % devices) for i in range(devi...  2.64 us
    ppermute x2, starting transfers between devices, shifted(): lax.ppermute(array, 'seq', [(order[i], order[(i + by) % devices]) for i i...  2.07 us
  transfers between devices with their start and end apart: 11, of which 4 were waited for; matrix products, arithmetic and copies ran while one was open for 0% of the time, Pallas kernels for 20%

profile of v8, /device:TPU:0, one launch (start us, length us, event | category | flops | bytes accessed | tf_op | source)
XLA Modules:
  0.0 92.1 jit_solution(12723851572872549948)
XLA Ops:
  0.6 1.1 %shard_map.68.joined_ref = bf16[512,384]{1,0:T(8,128)(2,1)S(1)} custom-call(bf16[512,128]{1,0:T(8,128)(2,1)} %bitcast.11, bf16[512,128]{1,0:T(8,128)(2,1)} %bitcast.12, bf16[512,128]{1,0:T(8,128)(2,1)} %bitcast.13), custom_call_target="tpu_custom_call" | custom-call | tf_op jit(solution)/shard_map/pallas_call | solution.py:91
  1.7 4.1 %collective-permute-start = (bf16[512,384]{1,0:T(8,128)(2,1)S(1)}, bf16[512,384]{1,0:T(8,128)(2,1)S(1)}, u32[]{:S(2)}, u32[]{:S(2)}) collective-permute-start(bf16[512,384]{1,0:T(8,128)(2,1)S(1)} %shard_map.68.joined_ref), channel_id=1, source_target_pairs={{0,16},{2,18},{4,20},{6,22},{8,24},{10,26},{12,28},{14,30},{16,0},... | collective-permute-start | bytes 1179656 | tf_op jit(solution)/shard_map/ppermute | solution.py:743
  5.8 2.8 %shard_map.69 = (bf16[1024,384]{1,0:T(8,128)(2,1)}, s32[3,32,256]{2,1,0:T(8,128)S(1)}) custom-call(bf16[512,384]{1,0:T(8,128)(2,1)S(1)} %shard_map.68.joined_ref, s32[2,48]{1,0:T(2,128)} %bitcast.15, s32[96,256]{1,0:T(8,128)} %bitcast.14), custom_call_target="tpu_custom_call" | custom-call | tf_op jit(solution)/shard_map/pallas_call | solution.py:91
  8.6 4.7 %all-to-all-start = ((bf16[8,128,384]{2,1,0:T(8,128)(2,1)}), bf16[8,128,384]{2,1,0:T(8,128)(2,1)S(1)}, u32[]{:S(2)}, u32[]{:S(2)}) async-start(bf16[8,128,384]{2,1,0:T(8,128)(2,1)} %bitcast.10), calls=%async_computation | async-start | bytes 1572864 | tf_op jit(solution)/shard_map/all_to_all | solution.py:730
  13.4 0.7 shard_map.70.pick_ref
  14.0 0.2 shard_map.73
  14.3 6.5 %shard_map.72 = (bf16[2,128,1024]{2,1,0:T(8,128)(2,1)}, f32[8,256]{1,0:T(8,128)S(1)}) custom-call(s32[3,32,256]{2,1,0:T(8,128)S(1)} %get-tuple-element.77.tokens_ref), custom_call_target="tpu_custom_call" | custom-call | tf_op jit(solution)/shard_map/pallas_call | solution.py:91
  20.8 2.6 %collective-permute-done.rows_ref = bf16[512,384]{1,0:T(8,128)(2,1)S(1)} collective-permute-done((bf16[512,384]{1,0:T(8,128)(2,1)S(1)}, bf16[512,384]{1,0:T(8,128)(2,1)S(1)}, u32[]{:S(2)}, u32[]{:S(2)}) %collective-permute-start) | collective-permute-done | bytes 393248 | tf_op jit(solution)/shard_map/ppermute | solution.py:743
  23.4 0.7 shard_map.71
  24.1 2.6 %collective-permute-start.1 = (bf16[128,384]{1,0:T(8,128)(2,1)S(1)}, bf16[128,384]{1,0:T(8,128)(2,1)S(1)}, u32[]{:S(2)}, u32[]{:S(2)}) collective-permute-start(bf16[128,384]{1,0:T(8,128)(2,1)S(1)} %get-tuple-element.70), channel_id=1, source_target_pairs={{0,14},{2,12},{4,10},{6,8},{8,6},{10,4},{12,2},{14,0},{16,30},{18,... | collective-permute-start | bytes 294920 | tf_op jit(solution)/shard_map/ppermute | solution.py:737
  26.8 1.4 %collective-permute-start.2 = (bf16[128,384]{1,0:T(8,128)(2,1)S(1)}, bf16[128,384]{1,0:T(8,128)(2,1)S(1)}, u32[]{:S(2)}, u32[]{:S(2)}) collective-permute-start(bf16[128,384]{1,0:T(8,128)(2,1)S(1)} %get-tuple-element.71), channel_id=1, source_target_pairs={{0,12},{2,14},{4,8},{6,10},{8,4},{10,6},{12,0},{14,2},{16,28},{18,... | collective-permute-start | bytes 294920 | tf_op jit(solution)/shard_map/ppermute | solution.py:737
  28.1 0.6 collective-permute-start.3
  28.7 1.4 %collective-permute-start.4 = (bf16[128,384]{1,0:T(8,128)(2,1)S(1)}, bf16[128,384]{1,0:T(8,128)(2,1)S(1)}, u32[]{:S(2)}, u32[]{:S(2)}) collective-permute-start(bf16[128,384]{1,0:T(8,128)(2,1)S(1)} %get-tuple-element.73), channel_id=1, source_target_pairs={{0,8},{2,10},{4,12},{6,14},{8,0},{10,2},{12,4},{14,6},{16,24},{18,... | collective-permute-start | bytes 294920 | tf_op jit(solution)/shard_map/ppermute | solution.py:737
  30.1 2.5 %collective-permute-start.5 = (bf16[128,384]{1,0:T(8,128)(2,1)S(1)}, bf16[128,384]{1,0:T(8,128)(2,1)S(1)}, u32[]{:S(2)}, u32[]{:S(2)}) collective-permute-start(bf16[128,384]{1,0:T(8,128)(2,1)S(1)} %get-tuple-element.74), channel_id=1, source_target_pairs={{0,6},{2,4},{4,2},{6,0},{8,14},{10,12},{12,10},{14,8},{16,22},{18,... | collective-permute-start | bytes 294920 | tf_op jit(solution)/shard_map/ppermute | solution.py:737
  32.6 4.3 %collective-permute-done.1.refs_1_ = bf16[128,384]{1,0:T(8,128)(2,1)S(1)} collective-permute-done((bf16[128,384]{1,0:T(8,128)(2,1)S(1)}, bf16[128,384]{1,0:T(8,128)(2,1)S(1)}, u32[]{:S(2)}, u32[]{:S(2)}) %collective-permute-start.1) | collective-permute-done | bytes 98336 | tf_op jit(solution)/shard_map/ppermute | solution.py:737
  36.9 0.6 collective-permute-start.6
  37.5 0.6 collective-permute-done.2.refs_2_
  38.1 1.1 %collective-permute-start.7 = (bf16[128,384]{1,0:T(8,128)(2,1)S(1)}, bf16[128,384]{1,0:T(8,128)(2,1)S(1)}, u32[]{:S(2)}, u32[]{:S(2)}) collective-permute-start(bf16[128,384]{1,0:T(8,128)(2,1)S(1)} %get-tuple-element.76), channel_id=1, source_target_pairs={{0,2},{2,0},{4,6},{6,4},{8,10},{10,8},{12,14},{14,12},{16,18},{18,... | collective-permute-start | bytes 294920 | tf_op jit(solution)/shard_map/ppermute | solution.py:737
  39.2 3.9 %shard_map.74 = (bf16[2,1024,768]{2,1,0:T(8,128)(2,1)}, bf16[512,2048]{1,0:T(8,128)(2,1)}) custom-call(s32[3,32,256]{2,1,0:T(8,128)S(1)} %get-tuple-element.77.tokens_ref, f32[6,256]{1,0:T(8,128)S(1)} %get-tuple-element.78.home_place_ref), custom_call_target="tpu_custom_call" | custom-call | tf_op jit(solution)/shard_map/pallas_call | solution.py:91
  43.1 0.0 collective-permute-done.3.refs_3_
  43.1 0.0 collective-permute-done.4.refs_4_
  43.1 0.0 collective-permute-done.5.refs_5_
  43.1 0.0 collective-permute-done.6.refs_6_
  43.1 0.0 collective-permute-done.7.refs_7_
  43.1 0.0 all-to-all-done.near_ref
  43.1 0.8 shard_map.75
  43.9 0.1 collective-permute-start.8
  44.0 2.0 %collective-permute-start.9 = (bf16[2,256,256]{2,1,0:T(8,128)(2,1)S(1)}, bf16[2,256,256]{2,1,0:T(8,128)(2,1)S(1)}, u32[]{:S(2)}, u32[]{:S(2)}) collective-permute-start(bf16[2,256,256]{2,1,0:T(8,128)(2,1)S(1)} %get-tuple-element.94.first_ref), channel_id=1, source_target_pairs={{0,4},{8,0},{16,8},{24,16},{26,24},{18,26},{10,18},{2,10},{6,2},{1... | collective-permute-start | bytes 786440 | tf_op jit(solution)/shard_map/ppermute | solution.py:753
  46.0 0.0 copy-start
  46.0 0.0 copy-start.2
  46.0 2.9 %shard_map.76 = (bf16[2,3,256,384]{3,2,1,0:T(8,128)(2,1)S(1)}, bf16[2,3,256,128]{3,2,1,0:T(8,128)(2,1)S(1)}, bf16[2,2,512,256]{3,2,1,0:T(8,128)(2,1)S(1)}, bf16[...) custom-call(f32[10,256]{1,0:T(8,128)S(1)} %get-tuple-element.82.fill, ...), custom_call_target="tpu_custom_call" | custom-call | tf_op jit(solution)/shard_map/pallas_call | solution.py:91
  48.9 1.4 %collective-permute-done.8.behind_ref = bf16[2,256,256]{2,1,0:T(8,128)(2,1)S(1)} collective-permute-done((bf16[2,256,256]{2,1,0:T(8,128)(2,1)S(1)}, bf16[2,256,256]{2,1,0:T(8,128)(2,1)S(1)}, u32[]{:S(2)}, u32[]{:S(2)}) %collective-permute-start.8) | collective-permute-done | bytes 262176 | tf_op jit(solution)/shard_map/ppermute | solution.py:753
  50.3 0.8 shard_map.77
  51.1 0.0 collective-permute-done.9.ahead_ref
  51.1 11.7 %all_to_all.22.everyone_ref = f32[16,24,128]{2,1,0:T(8,128)S(1)} all-to-all(f32[16,24,128]{2,1,0:T(8,128)S(1)} %get-tuple-element.100), channel_id=1, replica_groups=mesh['seq'=16,'head'=2] {'seq'}, dimensions={0} | all-to-all | bytes 393216 | tf_op jit(solution)/shard_map/all_to_all | solution.py:747
  62.8 0.0 copy-done
  62.8 0.0 copy-done.2
  62.8 3.4 %shard_map.78 = bf16[16,128,256]{2,1,0:T(8,128)(2,1)S(1)} custom-call(f32[10,256]{1,0:T(8,128)S(1)} %get-tuple-element.82.fill_ref, f32[16,24,128]{2,1,0:T(8,128)S(1)} %all_to_all.22.everyone_ref, bf16[2,128,1024]{2,1,0:T(8,128)(2,1)S(1)} %copy-done.2, f32[8,256]{1,0:T(8,128)S(1)} %get-tuple-element.102.low_ref, f32[12,256]{1,0:T(8,128)S(1)} %get-tuple-element.103.sums_ref, ...), custom_call_target="tpu_custom_call" | custom-call | tf_op jit(solution)/shard_map/pallas_call | solution.py:91
  66.2 0.0 copy-start.1
  66.2 24.5 %all_to_all.23 = bf16[16,128,256]{2,1,0:T(8,128)(2,1)S(1)} all-to-all(bf16[16,128,256]{2,1,0:T(8,128)(2,1)S(1)} %shard_map.78), channel_id=1, replica_groups=mesh['seq'=16,'head'=2] {'seq'}, dimensions={0} | all-to-all | bytes 2097152 | tf_op jit(solution)/shard_map/all_to_all | solution.py:747
  90.7 0.0 copy-done.1
  90.7 1.4 %shard_map.79 = (bf16[512,128]{1,0:T(8,128)(2,1)}, bf16[512,128]{1,0:T(8,128)(2,1)}) custom-call(bf16[512,2048]{1,0:T(8,128)(2,1)S(1)} %copy-done.1, bf16[2048,256]{1,0:T(8,128)(2,1)S(1)} %bitcast.9), custom_call_target="tpu_custom_call" | custom-call | tf_op jit(solution)/shard_map/pallas_call | solution.py:91
Async XLA Ops:
  1.7 21.7 %collective-permute-start = (bf16[512,384]{1,0:T(8,128)(2,1)S(1)}, bf16[512,384]{1,0:T(8,128)(2,1)S(1)}, u32[]{:S(2)}, u32[]{:S(2)}) collective-permute-start(bf16[512,384]{1,0:T(8,128)(2,1)S(1)} %shard_map.68.joined_ref), channel_id=1, source_target_pairs={{0,16},{2,18},{4,20},{6,22},{8,24},{10,26},{12,28},{14,30},{16,0},... | collective-permute-start | bytes 1179656 | tf_op jit(solution)/shard_map/ppermute | solution.py:743
  8.6 34.5 %all-to-all-start = ((bf16[8,128,384]{2,1,0:T(8,128)(2,1)}), bf16[8,128,384]{2,1,0:T(8,128)(2,1)S(1)}, u32[]{:S(2)}, u32[]{:S(2)}) async-start(bf16[8,128,384]{2,1,0:T(8,128)(2,1)} %bitcast.10), calls=%async_computation | async-start | bytes 1572864 | tf_op jit(solution)/shard_map/all_to_all | solution.py:730
  24.1 12.8 %collective-permute-start.1 = (bf16[128,384]{1,0:T(8,128)(2,1)S(1)}, bf16[128,384]{1,0:T(8,128)(2,1)S(1)}, u32[]{:S(2)}, u32[]{:S(2)}) collective-permute-start(bf16[128,384]{1,0:T(8,128)(2,1)S(1)} %get-tuple-element.70), channel_id=1, source_target_pairs={{0,14},{2,12},{4,10},{6,8},{8,6},{10,4},{12,2},{14,0},{16,30},{18,... | collective-permute-start | bytes 294920 | tf_op jit(solution)/shard_map/ppermute | solution.py:737
  26.8 11.4 %collective-permute-start.2 = (bf16[128,384]{1,0:T(8,128)(2,1)S(1)}, bf16[128,384]{1,0:T(8,128)(2,1)S(1)}, u32[]{:S(2)}, u32[]{:S(2)}) collective-permute-start(bf16[128,384]{1,0:T(8,128)(2,1)S(1)} %get-tuple-element.71), channel_id=1, source_target_pairs={{0,12},{2,14},{4,8},{6,10},{8,4},{10,6},{12,0},{14,2},{16,28},{18,... | collective-permute-start | bytes 294920 | tf_op jit(solution)/shard_map/ppermute | solution.py:737
  28.1 15.0 %collective-permute-start.3 = (bf16[128,384]{1,0:T(8,128)(2,1)S(1)}, bf16[128,384]{1,0:T(8,128)(2,1)S(1)}, u32[]{:S(2)}, u32[]{:S(2)}) collective-permute-start(bf16[128,384]{1,0:T(8,128)(2,1)S(1)} %get-tuple-element.72), channel_id=1, source_target_pairs={{0,10},{2,8},{4,14},{6,12},{8,2},{10,0},{12,6},{14,4},{16,26},{18,... | collective-permute-start | bytes 294920 | tf_op jit(solution)/shard_map/ppermute | solution.py:737
  28.7 14.4 %collective-permute-start.4 = (bf16[128,384]{1,0:T(8,128)(2,1)S(1)}, bf16[128,384]{1,0:T(8,128)(2,1)S(1)}, u32[]{:S(2)}, u32[]{:S(2)}) collective-permute-start(bf16[128,384]{1,0:T(8,128)(2,1)S(1)} %get-tuple-element.73), channel_id=1, source_target_pairs={{0,8},{2,10},{4,12},{6,14},{8,0},{10,2},{12,4},{14,6},{16,24},{18,... | collective-permute-start | bytes 294920 | tf_op jit(solution)/shard_map/ppermute | solution.py:737
  30.1 13.0 %collective-permute-start.5 = (bf16[128,384]{1,0:T(8,128)(2,1)S(1)}, bf16[128,384]{1,0:T(8,128)(2,1)S(1)}, u32[]{:S(2)}, u32[]{:S(2)}) collective-permute-start(bf16[128,384]{1,0:T(8,128)(2,1)S(1)} %get-tuple-element.74), channel_id=1, source_target_pairs={{0,6},{2,4},{4,2},{6,0},{8,14},{10,12},{12,10},{14,8},{16,22},{18,... | collective-permute-start | bytes 294920 | tf_op jit(solution)/shard_map/ppermute | solution.py:737
  36.9 6.2 %collective-permute-start.6 = (bf16[128,384]{1,0:T(8,128)(2,1)S(1)}, bf16[128,384]{1,0:T(8,128)(2,1)S(1)}, u32[]{:S(2)}, u32[]{:S(2)}) collective-permute-start(bf16[128,384]{1,0:T(8,128)(2,1)S(1)} %get-tuple-element.75), channel_id=1, source_target_pairs={{0,4},{2,6},{4,0},{6,2},{8,12},{10,14},{12,8},{14,10},{16,20},{18,... | collective-permute-start | bytes 294920 | tf_op jit(solution)/shard_map/ppermute | solution.py:737
  38.1 5.0 %collective-permute-start.7 = (bf16[128,384]{1,0:T(8,128)(2,1)S(1)}, bf16[128,384]{1,0:T(8,128)(2,1)S(1)}, u32[]{:S(2)}, u32[]{:S(2)}) collective-permute-start(bf16[128,384]{1,0:T(8,128)(2,1)S(1)} %get-tuple-element.76), channel_id=1, source_target_pairs={{0,2},{2,0},{4,6},{6,4},{8,10},{10,8},{12,14},{14,12},{16,18},{18,... | collective-permute-start | bytes 294920 | tf_op jit(solution)/shard_map/ppermute | solution.py:737
  43.9 6.4 %collective-permute-start.8 = (bf16[2,256,256]{2,1,0:T(8,128)(2,1)S(1)}, bf16[2,256,256]{2,1,0:T(8,128)(2,1)S(1)}, u32[]{:S(2)}, u32[]{:S(2)}) collective-permute-start(bf16[2,256,256]{2,1,0:T(8,128)(2,1)S(1)} %get-tuple-element.93.last_ref), channel_id=1, source_target_pairs={{0,8},{8,16},{16,24},{24,26},{26,18},{18,10},{10,2},{2,6},{6,14},{... | collective-permute-start | bytes 786440 | tf_op jit(solution)/shard_map/ppermute | solution.py:753
  44.0 7.1 %collective-permute-start.9 = (bf16[2,256,256]{2,1,0:T(8,128)(2,1)S(1)}, bf16[2,256,256]{2,1,0:T(8,128)(2,1)S(1)}, u32[]{:S(2)}, u32[]{:S(2)}) collective-permute-start(bf16[2,256,256]{2,1,0:T(8,128)(2,1)S(1)} %get-tuple-element.94.first_ref), channel_id=1, source_target_pairs={{0,4},{8,0},{16,8},{24,16},{26,24},{18,26},{10,18},{2,10},{6,2},{1... | collective-permute-start | bytes 786440 | tf_op jit(solution)/shard_map/ppermute | solution.py:753
  46.0 16.8 %copy-start = (bf16[2,1024,768]{2,1,0:T(8,128)(2,1)S(1)}, bf16[2,1024,768]{2,1,0:T(8,128)(2,1)}, u32[]{:S(2)}) copy-start(bf16[2,1024,768]{2,1,0:T(8,128)(2,1)} %get-tuple-element.111.spread_t_ref) | copy-start | bytes 9437188
  46.0 16.8 %copy-start.2 = (bf16[2,128,1024]{2,1,0:T(8,128)(2,1)S(1)}, bf16[2,128,1024]{2,1,0:T(8,128)(2,1)}, u32[]{:S(2)}) copy-start(bf16[2,128,1024]{2,1,0:T(8,128)(2,1)} %get-tuple-element.101.partner_ref) | copy-start | bytes 1572868
  66.2 24.5 %copy-start.1 = (bf16[512,2048]{1,0:T(8,128)(2,1)S(1)}, bf16[512,2048]{1,0:T(8,128)(2,1)}, u32[]{:S(2)}) copy-start(bf16[512,2048]{1,0:T(8,128)(2,1)} %get-tuple-element.81.home_ref) | copy-start | bytes 6291460

commit v9 on v8

--- a/solution.py
+++ b/solution.py
@@ -225,6 +225,13 @@
         copy.wait()
 
 
+def bits_at(at, half):
+    plane = half // 2
+    if at == 0:
+        return 0
+    return half - at if at <= plane else at - plane
+
+
 def far_pick_kernel(rounds, devices, bound, token_count, tokens_ref, pick_ref, key_ref, value_ref):
     me = lax.axis_index("seq")
     half = devices // 2
@@ -233,7 +240,7 @@
     rank_slots(rounds, devices, token_count, source, tokens_ref, key_ref, value_ref)
     size = rounds * bound
     for at in range(half):
-        block = block_of(first + jnp.bitwise_xor(me - first, -at % half), devices)
+        block = block_of(first + jnp.bitwise_xor(me - first, bits_at(at, half)), devices)
         pick_ref[at * size : (at + 1) * size, :] = pick_rows(
             rounds, devices, bound, block, token_count, key_ref, value_ref
         )
@@ -263,7 +270,9 @@
     first = seat // half * half
     near = (source >= first) & (source < first + half)
     bits = jnp.bitwise_xor(source % half, seat - first)
-    crossed = half + jnp.where(bits > 0, half - bits, 0)
+    plane = half // 2
+    order = jnp.where(bits < plane, bits + plane, half - bits)
+    crossed = half + jnp.where(bits > 0, order, 0)
     source_place = jnp.where(near, source - first, crossed).astype(f32) * bound + 1.0
     for r in range(rounds):
         carry = jnp.zeros((devices, 1), f32)
@@ -822,10 +831,6 @@
         [far_pick, far_rows],
         cost=50_000_000_000,
     )
-    far_send, partner, tokens, home_place = lax.optimization_barrier(
-        (far_send, partner, tokens, home_place)
-    )
-    far = [far_send[0]] + [crossed(far_send[at], half - at) for at in range(1, half)]
     spread_t, home_pick = call(
         functools.partial(return_index_kernel, rounds, devices, bound, token_count),
         [((rounds, buffer_rows, slots), bf16), ((token_count, devices * span), bf16)],
@@ -833,7 +838,10 @@
         [pick] + keys,
         far=(0, 1),
     )
-    far, spread_t, home_pick = lax.optimization_barrier((far, spread_t, home_pick))
+    far_send, partner, spread_t, home_pick = lax.optimization_barrier(
+        (far_send, partner, spread_t, home_pick)
+    )
+    far = [far_send[0]] + [crossed(far_send[at], bits_at(at, half)) for at in range(1, half)]
     last, first = call(
         functools.partial(ends_kernel, rounds),
         [((rounds, cap, 2 * size), bf16)] * 2,

time: 92.4 us -> 92.1 us (level)
    ppermute x1, waiting for transfers between devices: 2.64 us -> 0.01 us  [mirrored(): lax.ppermute(array, 'seq', [(i, (i + half) % devices) for i in range(devi...]
    ppermute x7, waiting for transfers between devices: 5 us -> 7.27 us  [crossed(): return lax.ppermute(array, 'seq', [(i, i ^ by) for i in range(devices)])]
  transfers between devices with their start and end apart: 11 -> 11, of which waited for: 4 -> 7; matrix products, arithmetic and copies ran while one was open for 0% -> 0% of each run, Pallas kernels for 20% -> 20%
where the time goes in v9:
time: 92.1 us; the launch traced here: 91.8 us
  blocking collectives  36.3 us (39%)
  Pallas kernels  25.1 us (27%)
  starting transfers between devices  20.9 us (23%)
  waiting for transfers between devices  8.69 us (9%)
    all_to_all x2, blocking collectives, exchange(): return lax.all_to_all(array, 'seq', split_axis=0, concat_axis=0, tiled=True)  36.3 us
    pallas_call x12, Pallas kernels, call(): pl.pallas_call(kernel, out_shape=tuple((pltpu.HBM(shape, dtype) if at in...  25.1 us
    ppermute x7, starting transfers between devices, crossed(): return lax.ppermute(array, 'seq', [(i, i ^ by) for i in range(devices)])  10 us
    ppermute x7, waiting for transfers between devices, crossed(): return lax.ppermute(array, 'seq', [(i, i ^ by) for i in range(devices)])  7.27 us
    all_to_all x1, starting transfers between devices, exchange_in_half(): lax.all_to_all(array, 'seq', split_axis=0, concat_axis=0, tiled=True, axi...  4.75 us
    ppermute x1, starting transfers between devices, mirrored(): lax.ppermute(array, 'seq', [(i, (i + half) % devices) for i in range(devi...  4.1 us
    ppermute x2, starting transfers between devices, shifted(): lax.ppermute(array, 'seq', [(order[i], order[(i + by) % devices]) for i i...  2.07 us
  transfers between devices with their start and end apart: 11, of which 7 were waited for; matrix products, arithmetic and copies ran while one was open for 0% of the time, Pallas kernels for 20%

profile of v9, /device:TPU:0, one launch (start us, length us, event | category | flops | bytes accessed | tf_op | source)
XLA Modules:
  0.0 91.8 jit_solution(8186703423142377952)
XLA Ops:
  0.6 1.1 %shard_map.68.joined_ref = bf16[512,384]{1,0:T(8,128)(2,1)S(1)} custom-call(bf16[512,128]{1,0:T(8,128)(2,1)} %bitcast.11, bf16[512,128]{1,0:T(8,128)(2,1)} %bitcast.12, bf16[512,128]{1,0:T(8,128)(2,1)} %bitcast.13), custom_call_target="tpu_custom_call" | custom-call | tf_op jit(solution)/shard_map/pallas_call | solution.py:91
  1.7 4.1 %collective-permute-start = (bf16[512,384]{1,0:T(8,128)(2,1)S(1)}, bf16[512,384]{1,0:T(8,128)(2,1)S(1)}, u32[]{:S(2)}, u32[]{:S(2)}) collective-permute-start(bf16[512,384]{1,0:T(8,128)(2,1)S(1)} %shard_map.68.joined_ref), channel_id=1, source_target_pairs={{0,16},{2,18},{4,20},{6,22},{8,24},{10,26},{12,28},{14,30},{16,0},... | collective-permute-start | bytes 1179656 | tf_op jit(solution)/shard_map/ppermute | solution.py:752
  5.8 2.8 %shard_map.69 = (bf16[1024,384]{1,0:T(8,128)(2,1)}, s32[3,32,256]{2,1,0:T(8,128)S(1)}) custom-call(bf16[512,384]{1,0:T(8,128)(2,1)S(1)} %shard_map.68.joined_ref, s32[2,48]{1,0:T(2,128)} %bitcast.15, s32[96,256]{1,0:T(8,128)} %bitcast.14), custom_call_target="tpu_custom_call" | custom-call | tf_op jit(solution)/shard_map/pallas_call | solution.py:91
  8.6 4.7 %all-to-all-start = ((bf16[8,128,384]{2,1,0:T(8,128)(2,1)}), bf16[8,128,384]{2,1,0:T(8,128)(2,1)S(1)}, u32[]{:S(2)}, u32[]{:S(2)}) async-start(bf16[8,128,384]{2,1,0:T(8,128)(2,1)} %bitcast.10), calls=%async_computation | async-start | bytes 1572864 | tf_op jit(solution)/shard_map/all_to_all | solution.py:739
  13.4 0.2 shard_map.73
  13.6 0.7 shard_map.70.pick_ref
  14.3 6.5 %shard_map.72 = (bf16[2,128,1024]{2,1,0:T(8,128)(2,1)}, f32[8,256]{1,0:T(8,128)S(1)}) custom-call(s32[3,32,256]{2,1,0:T(8,128)S(1)} %get-tuple-element.48.tokens_ref), custom_call_target="tpu_custom_call" | custom-call | tf_op jit(solution)/shard_map/pallas_call | solution.py:91
  20.8 3.9 %shard_map.74 = (bf16[2,1024,768]{2,1,0:T(8,128)(2,1)}, bf16[512,2048]{1,0:T(8,128)(2,1)}) custom-call(s32[3,32,256]{2,1,0:T(8,128)S(1)} %get-tuple-element.48.tokens_ref, f32[6,256]{1,0:T(8,128)S(1)} %get-tuple-element.58.home_place_ref), custom_call_target="tpu_custom_call" | custom-call | tf_op jit(solution)/shard_map/pallas_call | solution.py:91
  24.7 0.0 collective-permute-done.rows_ref
  24.7 0.7 shard_map.71
  25.4 3.9 %collective-permute-start.1 = (bf16[128,384]{1,0:T(8,128)(2,1)S(1)}, bf16[128,384]{1,0:T(8,128)(2,1)S(1)}, u32[]{:S(2)}, u32[]{:S(2)}) collective-permute-start(bf16[128,384]{1,0:T(8,128)(2,1)S(1)} %get-tuple-element.66), channel_id=1, source_target_pairs={{0,14},{2,12},{4,10},{6,8},{8,6},{10,4},{12,2},{14,0},{16,30},{18,... | collective-permute-start | bytes 294920 | tf_op jit(solution)/shard_map/ppermute | solution.py:746
  29.3 0.6 collective-permute-start.2
  29.8 1.5 %collective-permute-start.3 = (bf16[128,384]{1,0:T(8,128)(2,1)S(1)}, bf16[128,384]{1,0:T(8,128)(2,1)S(1)}, u32[]{:S(2)}, u32[]{:S(2)}) collective-permute-start(bf16[128,384]{1,0:T(8,128)(2,1)S(1)} %get-tuple-element.68), channel_id=1, source_target_pairs={{0,10},{2,8},{4,14},{6,12},{8,2},{10,0},{12,6},{14,4},{16,26},{18,... | collective-permute-start | bytes 294920 | tf_op jit(solution)/shard_map/ppermute | solution.py:746
  31.3 0.1 collective-permute-start.4
  31.4 1.9 %collective-permute-start.5 = (bf16[128,384]{1,0:T(8,128)(2,1)S(1)}, bf16[128,384]{1,0:T(8,128)(2,1)S(1)}, u32[]{:S(2)}, u32[]{:S(2)}) collective-permute-start(bf16[128,384]{1,0:T(8,128)(2,1)S(1)} %get-tuple-element.70), channel_id=1, source_target_pairs={{0,2},{2,0},{4,6},{6,4},{8,10},{10,8},{12,14},{14,12},{16,18},{18,... | collective-permute-start | bytes 294920 | tf_op jit(solution)/shard_map/ppermute | solution.py:746
  33.3 3.0 %collective-permute-done.1.refs_1_ = bf16[128,384]{1,0:T(8,128)(2,1)S(1)} collective-permute-done((bf16[128,384]{1,0:T(8,128)(2,1)S(1)}, bf16[128,384]{1,0:T(8,128)(2,1)S(1)}, u32[]{:S(2)}, u32[]{:S(2)}) %collective-permute-start.1) | collective-permute-done | bytes 98336 | tf_op jit(solution)/shard_map/ppermute | solution.py:746
  36.4 0.6 collective-permute-start.6
  37.0 0.2 collective-permute-done.2.refs_2_
  37.1 1.4 %collective-permute-start.7 = (bf16[128,384]{1,0:T(8,128)(2,1)S(1)}, bf16[128,384]{1,0:T(8,128)(2,1)S(1)}, u32[]{:S(2)}, u32[]{:S(2)}) collective-permute-start(bf16[128,384]{1,0:T(8,128)(2,1)S(1)} %get-tuple-element.72), channel_id=1, source_target_pairs={{0,6},{2,4},{4,2},{6,0},{8,14},{10,12},{12,10},{14,8},{16,22},{18,... | collective-permute-start | bytes 294920 | tf_op jit(solution)/shard_map/ppermute | solution.py:746
  38.6 0.6 collective-permute-done.3.refs_3_
  39.2 0.3 collective-permute-done.4.refs_4_
  39.5 0.0 collective-permute-done.5.refs_5_
  39.5 2.1 %collective-permute-done.6.refs_6_ = bf16[128,384]{1,0:T(8,128)(2,1)S(1)} collective-permute-done((bf16[128,384]{1,0:T(8,128)(2,1)S(1)}, bf16[128,384]{1,0:T(8,128)(2,1)S(1)}, u32[]{:S(2)}, u32[]{:S(2)}) %collective-permute-start.6) | collective-permute-done | bytes 98336 | tf_op jit(solution)/shard_map/ppermute | solution.py:746
  41.6 1.0 %collective-permute-done.7.refs_7_ = bf16[128,384]{1,0:T(8,128)(2,1)S(1)} collective-permute-done((bf16[128,384]{1,0:T(8,128)(2,1)S(1)}, bf16[128,384]{1,0:T(8,128)(2,1)S(1)}, u32[]{:S(2)}, u32[]{:S(2)}) %collective-permute-start.7) | collective-permute-done | bytes 98336 | tf_op jit(solution)/shard_map/ppermute | solution.py:746
  42.7 0.0 all-to-all-done.near_ref
  42.7 0.8 shard_map.75
  43.4 0.1 collective-permute-start.8
  43.5 2.0 %collective-permute-start.9 = (bf16[2,256,256]{2,1,0:T(8,128)(2,1)S(1)}, bf16[2,256,256]{2,1,0:T(8,128)(2,1)S(1)}, u32[]{:S(2)}, u32[]{:S(2)}) collective-permute-start(bf16[2,256,256]{2,1,0:T(8,128)(2,1)S(1)} %get-tuple-element.74.first_ref), channel_id=1, source_target_pairs={{0,4},{8,0},{16,8},{24,16},{26,24},{18,26},{10,18},{2,10},{6,2},{1... | collective-permute-start | bytes 786440 | tf_op jit(solution)/shard_map/ppermute | solution.py:762
  45.5 0.0 copy-start
  45.5 0.0 copy-start.2
  45.5 2.9 %shard_map.76 = (bf16[2,3,256,384]{3,2,1,0:T(8,128)(2,1)S(1)}, bf16[2,3,256,128]{3,2,1,0:T(8,128)(2,1)S(1)}, bf16[2,2,512,256]{3,2,1,0:T(8,128)(2,1)S(1)}, bf16[...) custom-call(f32[10,256]{1,0:T(8,128)S(1)} %get-tuple-element.62.fill, ...), custom_call_target="tpu_custom_call" | custom-call | tf_op jit(solution)/shard_map/pallas_call | solution.py:91
  48.4 1.4 %collective-permute-done.8.behind_ref = bf16[2,256,256]{2,1,0:T(8,128)(2,1)S(1)} collective-permute-done((bf16[2,256,256]{2,1,0:T(8,128)(2,1)S(1)}, bf16[2,256,256]{2,1,0:T(8,128)(2,1)S(1)}, u32[]{:S(2)}, u32[]{:S(2)}) %collective-permute-start.8) | collective-permute-done | bytes 262176 | tf_op jit(solution)/shard_map/ppermute | solution.py:762
  49.9 0.8 shard_map.77
  50.7 0.0 collective-permute-done.9.ahead_ref
  50.7 12.6 %all_to_all.22.everyone_ref = f32[16,24,128]{2,1,0:T(8,128)S(1)} all-to-all(f32[16,24,128]{2,1,0:T(8,128)S(1)} %get-tuple-element.80), channel_id=1, replica_groups=mesh['seq'=16,'head'=2] {'seq'}, dimensions={0} | all-to-all | bytes 393216 | tf_op jit(solution)/shard_map/all_to_all | solution.py:756
  63.3 0.0 copy-done
  63.3 0.0 copy-done.2
  63.3 3.4 %shard_map.78 = bf16[16,128,256]{2,1,0:T(8,128)(2,1)S(1)} custom-call(f32[10,256]{1,0:T(8,128)S(1)} %get-tuple-element.62.fill_ref, f32[16,24,128]{2,1,0:T(8,128)S(1)} %all_to_all.22.everyone_ref, bf16[2,128,1024]{2,1,0:T(8,128)(2,1)S(1)} %copy-done.2, f32[8,256]{1,0:T(8,128)S(1)} %get-tuple-element.82.low_ref, f32[12,256]{1,0:T(8,128)S(1)} %get-tuple-element.83.sums_ref, ...), custom_call_target="tpu_custom_call" | custom-call | tf_op jit(solution)/shard_map/pallas_call | solution.py:91
  66.7 0.0 copy-start.1
  66.7 23.7 %all_to_all.23 = bf16[16,128,256]{2,1,0:T(8,128)(2,1)S(1)} all-to-all(bf16[16,128,256]{2,1,0:T(8,128)(2,1)S(1)} %shard_map.78), channel_id=1, replica_groups=mesh['seq'=16,'head'=2] {'seq'}, dimensions={0} | all-to-all | bytes 2097152 | tf_op jit(solution)/shard_map/all_to_all | solution.py:756
  90.4 0.0 copy-done.1
  90.4 1.4 %shard_map.79 = (bf16[512,128]{1,0:T(8,128)(2,1)}, bf16[512,128]{1,0:T(8,128)(2,1)}) custom-call(bf16[512,2048]{1,0:T(8,128)(2,1)S(1)} %copy-done.1, bf16[2048,256]{1,0:T(8,128)(2,1)S(1)} %bitcast.9), custom_call_target="tpu_custom_call" | custom-call | tf_op jit(solution)/shard_map/pallas_call | solution.py:91
Async XLA Ops:
  1.7 23.0 %collective-permute-start = (bf16[512,384]{1,0:T(8,128)(2,1)S(1)}, bf16[512,384]{1,0:T(8,128)(2,1)S(1)}, u32[]{:S(2)}, u32[]{:S(2)}) collective-permute-start(bf16[512,384]{1,0:T(8,128)(2,1)S(1)} %shard_map.68.joined_ref), channel_id=1, source_target_pairs={{0,16},{2,18},{4,20},{6,22},{8,24},{10,26},{12,28},{14,30},{16,0},... | collective-permute-start | bytes 1179656 | tf_op jit(solution)/shard_map/ppermute | solution.py:752
  8.6 34.0 %all-to-all-start = ((bf16[8,128,384]{2,1,0:T(8,128)(2,1)}), bf16[8,128,384]{2,1,0:T(8,128)(2,1)S(1)}, u32[]{:S(2)}, u32[]{:S(2)}) async-start(bf16[8,128,384]{2,1,0:T(8,128)(2,1)} %bitcast.10), calls=%async_computation | async-start | bytes 1572864 | tf_op jit(solution)/shard_map/all_to_all | solution.py:739
  25.4 11.0 %collective-permute-start.1 = (bf16[128,384]{1,0:T(8,128)(2,1)S(1)}, bf16[128,384]{1,0:T(8,128)(2,1)S(1)}, u32[]{:S(2)}, u32[]{:S(2)}) collective-permute-start(bf16[128,384]{1,0:T(8,128)(2,1)S(1)} %get-tuple-element.66), channel_id=1, source_target_pairs={{0,14},{2,12},{4,10},{6,8},{8,6},{10,4},{12,2},{14,0},{16,30},{18,... | collective-permute-start | bytes 294920 | tf_op jit(solution)/shard_map/ppermute | solution.py:746
  29.3 7.9 %collective-permute-start.2 = (bf16[128,384]{1,0:T(8,128)(2,1)S(1)}, bf16[128,384]{1,0:T(8,128)(2,1)S(1)}, u32[]{:S(2)}, u32[]{:S(2)}) collective-permute-start(bf16[128,384]{1,0:T(8,128)(2,1)S(1)} %get-tuple-element.67), channel_id=1, source_target_pairs={{0,12},{2,14},{4,8},{6,10},{8,4},{10,6},{12,0},{14,2},{16,28},{18,... | collective-permute-start | bytes 294920 | tf_op jit(solution)/shard_map/ppermute | solution.py:746
  29.8 9.4 %collective-permute-start.3 = (bf16[128,384]{1,0:T(8,128)(2,1)S(1)}, bf16[128,384]{1,0:T(8,128)(2,1)S(1)}, u32[]{:S(2)}, u32[]{:S(2)}) collective-permute-start(bf16[128,384]{1,0:T(8,128)(2,1)S(1)} %get-tuple-element.68), channel_id=1, source_target_pairs={{0,10},{2,8},{4,14},{6,12},{8,2},{10,0},{12,6},{14,4},{16,26},{18,... | collective-permute-start | bytes 294920 | tf_op jit(solution)/shard_map/ppermute | solution.py:746
  31.3 8.2 %collective-permute-start.4 = (bf16[128,384]{1,0:T(8,128)(2,1)S(1)}, bf16[128,384]{1,0:T(8,128)(2,1)S(1)}, u32[]{:S(2)}, u32[]{:S(2)}) collective-permute-start(bf16[128,384]{1,0:T(8,128)(2,1)S(1)} %get-tuple-element.69), channel_id=1, source_target_pairs={{0,8},{2,10},{4,12},{6,14},{8,0},{10,2},{12,4},{14,6},{16,24},{18,... | collective-permute-start | bytes 294920 | tf_op jit(solution)/shard_map/ppermute | solution.py:746
  31.4 8.2 %collective-permute-start.5 = (bf16[128,384]{1,0:T(8,128)(2,1)S(1)}, bf16[128,384]{1,0:T(8,128)(2,1)S(1)}, u32[]{:S(2)}, u32[]{:S(2)}) collective-permute-start(bf16[128,384]{1,0:T(8,128)(2,1)S(1)} %get-tuple-element.70), channel_id=1, source_target_pairs={{0,2},{2,0},{4,6},{6,4},{8,10},{10,8},{12,14},{14,12},{16,18},{18,... | collective-permute-start | bytes 294920 | tf_op jit(solution)/shard_map/ppermute | solution.py:746
  36.4 5.3 %collective-permute-start.6 = (bf16[128,384]{1,0:T(8,128)(2,1)S(1)}, bf16[128,384]{1,0:T(8,128)(2,1)S(1)}, u32[]{:S(2)}, u32[]{:S(2)}) collective-permute-start(bf16[128,384]{1,0:T(8,128)(2,1)S(1)} %get-tuple-element.71), channel_id=1, source_target_pairs={{0,4},{2,6},{4,0},{6,2},{8,12},{10,14},{12,8},{14,10},{16,20},{18,... | collective-permute-start | bytes 294920 | tf_op jit(solution)/shard_map/ppermute | solution.py:746
  37.1 5.5 %collective-permute-start.7 = (bf16[128,384]{1,0:T(8,128)(2,1)S(1)}, bf16[128,384]{1,0:T(8,128)(2,1)S(1)}, u32[]{:S(2)}, u32[]{:S(2)}) collective-permute-start(bf16[128,384]{1,0:T(8,128)(2,1)S(1)} %get-tuple-element.72), channel_id=1, source_target_pairs={{0,6},{2,4},{4,2},{6,0},{8,14},{10,12},{12,10},{14,8},{16,22},{18,... | collective-permute-start | bytes 294920 | tf_op jit(solution)/shard_map/ppermute | solution.py:746
  43.4 6.4 %collective-permute-start.8 = (bf16[2,256,256]{2,1,0:T(8,128)(2,1)S(1)}, bf16[2,256,256]{2,1,0:T(8,128)(2,1)S(1)}, u32[]{:S(2)}, u32[]{:S(2)}) collective-permute-start(bf16[2,256,256]{2,1,0:T(8,128)(2,1)S(1)} %get-tuple-element.73.last_ref), channel_id=1, source_target_pairs={{0,8},{8,16},{16,24},{24,26},{26,18},{18,10},{10,2},{2,6},{6,14},{... | collective-permute-start | bytes 786440 | tf_op jit(solution)/shard_map/ppermute | solution.py:762
  43.5 7.2 %collective-permute-start.9 = (bf16[2,256,256]{2,1,0:T(8,128)(2,1)S(1)}, bf16[2,256,256]{2,1,0:T(8,128)(2,1)S(1)}, u32[]{:S(2)}, u32[]{:S(2)}) collective-permute-start(bf16[2,256,256]{2,1,0:T(8,128)(2,1)S(1)} %get-tuple-element.74.first_ref), channel_id=1, source_target_pairs={{0,4},{8,0},{16,8},{24,16},{26,24},{18,26},{10,18},{2,10},{6,2},{1... | collective-permute-start | bytes 786440 | tf_op jit(solution)/shard_map/ppermute | solution.py:762
  45.5 17.8 %copy-start = (bf16[2,1024,768]{2,1,0:T(8,128)(2,1)S(1)}, bf16[2,1024,768]{2,1,0:T(8,128)(2,1)}, u32[]{:S(2)}) copy-start(bf16[2,1024,768]{2,1,0:T(8,128)(2,1)} %get-tuple-element.91.spread_t_ref) | copy-start | bytes 9437188
  45.5 17.8 %copy-start.2 = (bf16[2,128,1024]{2,1,0:T(8,128)(2,1)S(1)}, bf16[2,128,1024]{2,1,0:T(8,128)(2,1)}, u32[]{:S(2)}) copy-start(bf16[2,128,1024]{2,1,0:T(8,128)(2,1)} %get-tuple-element.81.partner_ref) | copy-start | bytes 1572868
  66.7 23.7 %copy-start.1 = (bf16[512,2048]{1,0:T(8,128)(2,1)S(1)}, bf16[512,2048]{1,0:T(8,128)(2,1)}, u32[]{:S(2)}) copy-start(bf16[512,2048]{1,0:T(8,128)(2,1)} %get-tuple-element.61.home_ref) | copy-start | bytes 6291460

commit v10 on v9

--- a/solution.py
+++ b/solution.py
@@ -339,7 +339,7 @@
             return total
 
         total = lax.fori_loop(
-            0, devices, one_block, jnp.zeros((2 * high_count, lane), f32), unroll=2
+            0, devices, one_block, jnp.zeros((2 * high_count, lane), f32), unroll=4
         )
         table_ref[r] = total.astype(bf16)
 

time: 92.1 us -> 92.1 us (level)
  waiting for transfers between devices: 8.69 us -> 9.97 us
  Pallas kernels: 25.1 us -> 23.9 us
    ppermute x7, waiting for transfers between devices: 7.27 us -> 8.54 us  [crossed(): return lax.ppermute(array, 'seq', [(i, i ^ by) for i in range(devices)])]
    pallas_call x12, Pallas kernels: 25.1 us -> 23.9 us  [call(): pl.pallas_call(kernel, out_shape=tuple((pltpu.HBM(shape, dtype) if at in...]
  transfers between devices with their start and end apart: 11 -> 11, of which waited for: 7 -> 7; matrix products, arithmetic and copies ran while one was open for 0% -> 0% of each run, Pallas kernels for 20% -> 19%
where the time goes in v10:
time: 92.1 us; the launch traced here: 91.8 us
  blocking collectives  36.3 us (39%)
  Pallas kernels  23.9 us (26%)
  starting transfers between devices  20.9 us (23%)
  waiting for transfers between devices  9.97 us (11%)
    all_to_all x2, blocking collectives, exchange(): return lax.all_to_all(array, 'seq', split_axis=0, concat_axis=0, tiled=True)  36.3 us
    pallas_call x12, Pallas kernels, call(): pl.pallas_call(kernel, out_shape=tuple((pltpu.HBM(shape, dtype) if at in...  23.9 us
    ppermute x7, starting transfers between devices, crossed(): return lax.ppermute(array, 'seq', [(i, i ^ by) for i in range(devices)])  9.95 us
    ppermute x7, waiting for transfers between devices, crossed(): return lax.ppermute(array, 'seq', [(i, i ^ by) for i in range(devices)])  8.54 us
    all_to_all x1, starting transfers between devices, exchange_in_half(): lax.all_to_all(array, 'seq', split_axis=0, concat_axis=0, tiled=True, axi...  4.75 us
    ppermute x1, starting transfers between devices, mirrored(): lax.ppermute(array, 'seq', [(i, (i + half) % devices) for i in range(devi...  4.1 us
    ppermute x2, starting transfers between devices, shifted(): lax.ppermute(array, 'seq', [(order[i], order[(i + by) % devices]) for i i...  2.07 us
  transfers between devices with their start and end apart: 11, of which 7 were waited for; matrix products, arithmetic and copies ran while one was open for 0% of the time, Pallas kernels for 19%

profile of v10, /device:TPU:0, one launch (start us, length us, event | category | flops | bytes accessed | tf_op | source)
XLA Modules:
  0.0 91.8 jit_solution(15130910978727620302)
XLA Ops:
  0.6 1.1 %shard_map.68.joined_ref = bf16[512,384]{1,0:T(8,128)(2,1)S(1)} custom-call(bf16[512,128]{1,0:T(8,128)(2,1)} %bitcast.11, bf16[512,128]{1,0:T(8,128)(2,1)} %bitcast.12, bf16[512,128]{1,0:T(8,128)(2,1)} %bitcast.13), custom_call_target="tpu_custom_call" | custom-call | tf_op jit(solution)/shard_map/pallas_call | solution.py:91
  1.7 4.1 %collective-permute-start = (bf16[512,384]{1,0:T(8,128)(2,1)S(1)}, bf16[512,384]{1,0:T(8,128)(2,1)S(1)}, u32[]{:S(2)}, u32[]{:S(2)}) collective-permute-start(bf16[512,384]{1,0:T(8,128)(2,1)S(1)} %shard_map.68.joined_ref), channel_id=1, source_target_pairs={{0,16},{2,18},{4,20},{6,22},{8,24},{10,26},{12,28},{14,30},{16,0},... | collective-permute-start | bytes 1179656 | tf_op jit(solution)/shard_map/ppermute | solution.py:752
  5.8 2.8 %shard_map.69 = (bf16[1024,384]{1,0:T(8,128)(2,1)}, s32[3,32,256]{2,1,0:T(8,128)S(1)}) custom-call(bf16[512,384]{1,0:T(8,128)(2,1)S(1)} %shard_map.68.joined_ref, s32[2,48]{1,0:T(2,128)} %bitcast.15, s32[96,256]{1,0:T(8,128)} %bitcast.14), custom_call_target="tpu_custom_call" | custom-call | tf_op jit(solution)/shard_map/pallas_call | solution.py:91
  8.6 4.7 %all-to-all-start = ((bf16[8,128,384]{2,1,0:T(8,128)(2,1)}), bf16[8,128,384]{2,1,0:T(8,128)(2,1)S(1)}, u32[]{:S(2)}, u32[]{:S(2)}) async-start(bf16[8,128,384]{2,1,0:T(8,128)(2,1)} %bitcast.10), calls=%async_computation | async-start | bytes 1572864 | tf_op jit(solution)/shard_map/all_to_all | solution.py:739
  13.4 0.2 shard_map.73
  13.6 0.7 shard_map.70.pick_ref
  14.3 5.3 %shard_map.72 = (bf16[2,128,1024]{2,1,0:T(8,128)(2,1)}, f32[8,256]{1,0:T(8,128)S(1)}) custom-call(s32[3,32,256]{2,1,0:T(8,128)S(1)} %get-tuple-element.48.tokens_ref), custom_call_target="tpu_custom_call" | custom-call | tf_op jit(solution)/shard_map/pallas_call | solution.py:91
  19.6 3.9 %shard_map.74 = (bf16[2,1024,768]{2,1,0:T(8,128)(2,1)}, bf16[512,2048]{1,0:T(8,128)(2,1)}) custom-call(s32[3,32,256]{2,1,0:T(8,128)S(1)} %get-tuple-element.48.tokens_ref, f32[6,256]{1,0:T(8,128)S(1)} %get-tuple-element.58.home_place_ref), custom_call_target="tpu_custom_call" | custom-call | tf_op jit(solution)/shard_map/pallas_call | solution.py:91
  23.5 0.0 collective-permute-done.rows_ref
  23.5 0.7 shard_map.71
  24.2 3.9 %collective-permute-start.1 = (bf16[128,384]{1,0:T(8,128)(2,1)S(1)}, bf16[128,384]{1,0:T(8,128)(2,1)S(1)}, u32[]{:S(2)}, u32[]{:S(2)}) collective-permute-start(bf16[128,384]{1,0:T(8,128)(2,1)S(1)} %get-tuple-element.66), channel_id=1, source_target_pairs={{0,14},{2,12},{4,10},{6,8},{8,6},{10,4},{12,2},{14,0},{16,30},{18,... | collective-permute-start | bytes 294920 | tf_op jit(solution)/shard_map/ppermute | solution.py:746
  28.1 0.6 collective-permute-start.2
  28.6 1.5 %collective-permute-start.3 = (bf16[128,384]{1,0:T(8,128)(2,1)S(1)}, bf16[128,384]{1,0:T(8,128)(2,1)S(1)}, u32[]{:S(2)}, u32[]{:S(2)}) collective-permute-start(bf16[128,384]{1,0:T(8,128)(2,1)S(1)} %get-tuple-element.68), channel_id=1, source_target_pairs={{0,10},{2,8},{4,14},{6,12},{8,2},{10,0},{12,6},{14,4},{16,26},{18,... | collective-permute-start | bytes 294920 | tf_op jit(solution)/shard_map/ppermute | solution.py:746
  30.1 0.1 collective-permute-start.4
  30.2 1.9 %collective-permute-start.5 = (bf16[128,384]{1,0:T(8,128)(2,1)S(1)}, bf16[128,384]{1,0:T(8,128)(2,1)S(1)}, u32[]{:S(2)}, u32[]{:S(2)}) collective-permute-start(bf16[128,384]{1,0:T(8,128)(2,1)S(1)} %get-tuple-element.70), channel_id=1, source_target_pairs={{0,2},{2,0},{4,6},{6,4},{8,10},{10,8},{12,14},{14,12},{16,18},{18,... | collective-permute-start | bytes 294920 | tf_op jit(solution)/shard_map/ppermute | solution.py:746
  32.1 4.3 %collective-permute-done.1.refs_1_ = bf16[128,384]{1,0:T(8,128)(2,1)S(1)} collective-permute-done((bf16[128,384]{1,0:T(8,128)(2,1)S(1)}, bf16[128,384]{1,0:T(8,128)(2,1)S(1)}, u32[]{:S(2)}, u32[]{:S(2)}) %collective-permute-start.1) | collective-permute-done | bytes 98336 | tf_op jit(solution)/shard_map/ppermute | solution.py:746
  36.4 0.6 collective-permute-start.6
  36.9 0.2 collective-permute-done.2.refs_2_
  37.1 1.4 %collective-permute-start.7 = (bf16[128,384]{1,0:T(8,128)(2,1)S(1)}, bf16[128,384]{1,0:T(8,128)(2,1)S(1)}, u32[]{:S(2)}, u32[]{:S(2)}) collective-permute-start(bf16[128,384]{1,0:T(8,128)(2,1)S(1)} %get-tuple-element.72), channel_id=1, source_target_pairs={{0,6},{2,4},{4,2},{6,0},{8,14},{10,12},{12,10},{14,8},{16,22},{18,... | collective-permute-start | bytes 294920 | tf_op jit(solution)/shard_map/ppermute | solution.py:746
  38.6 0.6 collective-permute-done.3.refs_3_
  39.2 0.3 collective-permute-done.4.refs_4_
  39.5 0.0 collective-permute-done.5.refs_5_
  39.5 2.1 %collective-permute-done.6.refs_6_ = bf16[128,384]{1,0:T(8,128)(2,1)S(1)} collective-permute-done((bf16[128,384]{1,0:T(8,128)(2,1)S(1)}, bf16[128,384]{1,0:T(8,128)(2,1)S(1)}, u32[]{:S(2)}, u32[]{:S(2)}) %collective-permute-start.6) | collective-permute-done | bytes 98336 | tf_op jit(solution)/shard_map/ppermute | solution.py:746
  41.6 1.1 %collective-permute-done.7.refs_7_ = bf16[128,384]{1,0:T(8,128)(2,1)S(1)} collective-permute-done((bf16[128,384]{1,0:T(8,128)(2,1)S(1)}, bf16[128,384]{1,0:T(8,128)(2,1)S(1)}, u32[]{:S(2)}, u32[]{:S(2)}) %collective-permute-start.7) | collective-permute-done | bytes 98336 | tf_op jit(solution)/shard_map/ppermute | solution.py:746
  42.7 0.0 all-to-all-done.near_ref
  42.7 0.8 shard_map.75
  43.4 0.1 collective-permute-start.8
  43.5 2.0 %collective-permute-start.9 = (bf16[2,256,256]{2,1,0:T(8,128)(2,1)S(1)}, bf16[2,256,256]{2,1,0:T(8,128)(2,1)S(1)}, u32[]{:S(2)}, u32[]{:S(2)}) collective-permute-start(bf16[2,256,256]{2,1,0:T(8,128)(2,1)S(1)} %get-tuple-element.74.first_ref), channel_id=1, source_target_pairs={{0,4},{8,0},{16,8},{24,16},{26,24},{18,26},{10,18},{2,10},{6,2},{1... | collective-permute-start | bytes 786440 | tf_op jit(solution)/shard_map/ppermute | solution.py:762
  45.5 0.0 copy-start
  45.5 0.0 copy-start.2
  45.5 2.9 %shard_map.76 = (bf16[2,3,256,384]{3,2,1,0:T(8,128)(2,1)S(1)}, bf16[2,3,256,128]{3,2,1,0:T(8,128)(2,1)S(1)}, bf16[2,2,512,256]{3,2,1,0:T(8,128)(2,1)S(1)}, bf16[...) custom-call(f32[10,256]{1,0:T(8,128)S(1)} %get-tuple-element.62.fill, ...), custom_call_target="tpu_custom_call" | custom-call | tf_op jit(solution)/shard_map/pallas_call | solution.py:91
  48.5 1.4 %collective-permute-done.8.behind_ref = bf16[2,256,256]{2,1,0:T(8,128)(2,1)S(1)} collective-permute-done((bf16[2,256,256]{2,1,0:T(8,128)(2,1)S(1)}, bf16[2,256,256]{2,1,0:T(8,128)(2,1)S(1)}, u32[]{:S(2)}, u32[]{:S(2)}) %collective-permute-start.8) | collective-permute-done | bytes 262176 | tf_op jit(solution)/shard_map/ppermute | solution.py:762
  49.9 0.8 shard_map.77
  50.7 0.0 collective-permute-done.9.ahead_ref
  50.7 12.6 %all_to_all.22.everyone_ref = f32[16,24,128]{2,1,0:T(8,128)S(1)} all-to-all(f32[16,24,128]{2,1,0:T(8,128)S(1)} %get-tuple-element.80), channel_id=1, replica_groups=mesh['seq'=16,'head'=2] {'seq'}, dimensions={0} | all-to-all | bytes 393216 | tf_op jit(solution)/shard_map/all_to_all | solution.py:756
  63.3 0.0 copy-done
  63.3 0.0 copy-done.2
  63.3 3.4 %shard_map.78 = bf16[16,128,256]{2,1,0:T(8,128)(2,1)S(1)} custom-call(f32[10,256]{1,0:T(8,128)S(1)} %get-tuple-element.62.fill_ref, f32[16,24,128]{2,1,0:T(8,128)S(1)} %all_to_all.22.everyone_ref, bf16[2,128,1024]{2,1,0:T(8,128)(2,1)S(1)} %copy-done.2, f32[8,256]{1,0:T(8,128)S(1)} %get-tuple-element.82.low_ref, f32[12,256]{1,0:T(8,128)S(1)} %get-tuple-element.83.sums_ref, ...), custom_call_target="tpu_custom_call" | custom-call | tf_op jit(solution)/shard_map/pallas_call | solution.py:91
  66.7 0.0 copy-start.1
  66.7 23.7 %all_to_all.23 = bf16[16,128,256]{2,1,0:T(8,128)(2,1)S(1)} all-to-all(bf16[16,128,256]{2,1,0:T(8,128)(2,1)S(1)} %shard_map.78), channel_id=1, replica_groups=mesh['seq'=16,'head'=2] {'seq'}, dimensions={0} | all-to-all | bytes 2097152 | tf_op jit(solution)/shard_map/all_to_all | solution.py:756
  90.4 0.0 copy-done.1
  90.4 1.4 %shard_map.79 = (bf16[512,128]{1,0:T(8,128)(2,1)}, bf16[512,128]{1,0:T(8,128)(2,1)}) custom-call(bf16[512,2048]{1,0:T(8,128)(2,1)S(1)} %copy-done.1, bf16[2048,256]{1,0:T(8,128)(2,1)S(1)} %bitcast.9), custom_call_target="tpu_custom_call" | custom-call | tf_op jit(solution)/shard_map/pallas_call | solution.py:91
Async XLA Ops:
  1.7 21.8 %collective-permute-start = (bf16[512,384]{1,0:T(8,128)(2,1)S(1)}, bf16[512,384]{1,0:T(8,128)(2,1)S(1)}, u32[]{:S(2)}, u32[]{:S(2)}) collective-permute-start(bf16[512,384]{1,0:T(8,128)(2,1)S(1)} %shard_map.68.joined_ref), channel_id=1, source_target_pairs={{0,16},{2,18},{4,20},{6,22},{8,24},{10,26},{12,28},{14,30},{16,0},... | collective-permute-start | bytes 1179656 | tf_op jit(solution)/shard_map/ppermute | solution.py:752
  8.6 34.0 %all-to-all-start = ((bf16[8,128,384]{2,1,0:T(8,128)(2,1)}), bf16[8,128,384]{2,1,0:T(8,128)(2,1)S(1)}, u32[]{:S(2)}, u32[]{:S(2)}) async-start(bf16[8,128,384]{2,1,0:T(8,128)(2,1)} %bitcast.10), calls=%async_computation | async-start | bytes 1572864 | tf_op jit(solution)/shard_map/all_to_all | solution.py:739
  24.2 12.2 %collective-permute-start.1 = (bf16[128,384]{1,0:T(8,128)(2,1)S(1)}, bf16[128,384]{1,0:T(8,128)(2,1)S(1)}, u32[]{:S(2)}, u32[]{:S(2)}) collective-permute-start(bf16[128,384]{1,0:T(8,128)(2,1)S(1)} %get-tuple-element.66), channel_id=1, source_target_pairs={{0,14},{2,12},{4,10},{6,8},{8,6},{10,4},{12,2},{14,0},{16,30},{18,... | collective-permute-start | bytes 294920 | tf_op jit(solution)/shard_map/ppermute | solution.py:746
  28.1 9.1 %collective-permute-start.2 = (bf16[128,384]{1,0:T(8,128)(2,1)S(1)}, bf16[128,384]{1,0:T(8,128)(2,1)S(1)}, u32[]{:S(2)}, u32[]{:S(2)}) collective-permute-start(bf16[128,384]{1,0:T(8,128)(2,1)S(1)} %get-tuple-element.67), channel_id=1, source_target_pairs={{0,12},{2,14},{4,8},{6,10},{8,4},{10,6},{12,0},{14,2},{16,28},{18,... | collective-permute-start | bytes 294920 | tf_op jit(solution)/shard_map/ppermute | solution.py:746
  28.6 10.6 %collective-permute-start.3 = (bf16[128,384]{1,0:T(8,128)(2,1)S(1)}, bf16[128,384]{1,0:T(8,128)(2,1)S(1)}, u32[]{:S(2)}, u32[]{:S(2)}) collective-permute-start(bf16[128,384]{1,0:T(8,128)(2,1)S(1)} %get-tuple-element.68), channel_id=1, source_target_pairs={{0,10},{2,8},{4,14},{6,12},{8,2},{10,0},{12,6},{14,4},{16,26},{18,... | collective-permute-start | bytes 294920 | tf_op jit(solution)/shard_map/ppermute | solution.py:746
  30.1 9.5 %collective-permute-start.4 = (bf16[128,384]{1,0:T(8,128)(2,1)S(1)}, bf16[128,384]{1,0:T(8,128)(2,1)S(1)}, u32[]{:S(2)}, u32[]{:S(2)}) collective-permute-start(bf16[128,384]{1,0:T(8,128)(2,1)S(1)} %get-tuple-element.69), channel_id=1, source_target_pairs={{0,8},{2,10},{4,12},{6,14},{8,0},{10,2},{12,4},{14,6},{16,24},{18,... | collective-permute-start | bytes 294920 | tf_op jit(solution)/shard_map/ppermute | solution.py:746
  30.2 9.4 %collective-permute-start.5 = (bf16[128,384]{1,0:T(8,128)(2,1)S(1)}, bf16[128,384]{1,0:T(8,128)(2,1)S(1)}, u32[]{:S(2)}, u32[]{:S(2)}) collective-permute-start(bf16[128,384]{1,0:T(8,128)(2,1)S(1)} %get-tuple-element.70), channel_id=1, source_target_pairs={{0,2},{2,0},{4,6},{6,4},{8,10},{10,8},{12,14},{14,12},{16,18},{18,... | collective-permute-start | bytes 294920 | tf_op jit(solution)/shard_map/ppermute | solution.py:746
  36.4 5.3 %collective-permute-start.6 = (bf16[128,384]{1,0:T(8,128)(2,1)S(1)}, bf16[128,384]{1,0:T(8,128)(2,1)S(1)}, u32[]{:S(2)}, u32[]{:S(2)}) collective-permute-start(bf16[128,384]{1,0:T(8,128)(2,1)S(1)} %get-tuple-element.71), channel_id=1, source_target_pairs={{0,4},{2,6},{4,0},{6,2},{8,12},{10,14},{12,8},{14,10},{16,20},{18,... | collective-permute-start | bytes 294920 | tf_op jit(solution)/shard_map/ppermute | solution.py:746
  37.1 5.5 %collective-permute-start.7 = (bf16[128,384]{1,0:T(8,128)(2,1)S(1)}, bf16[128,384]{1,0:T(8,128)(2,1)S(1)}, u32[]{:S(2)}, u32[]{:S(2)}) collective-permute-start(bf16[128,384]{1,0:T(8,128)(2,1)S(1)} %get-tuple-element.72), channel_id=1, source_target_pairs={{0,6},{2,4},{4,2},{6,0},{8,14},{10,12},{12,10},{14,8},{16,22},{18,... | collective-permute-start | bytes 294920 | tf_op jit(solution)/shard_map/ppermute | solution.py:746
  43.4 6.4 %collective-permute-start.8 = (bf16[2,256,256]{2,1,0:T(8,128)(2,1)S(1)}, bf16[2,256,256]{2,1,0:T(8,128)(2,1)S(1)}, u32[]{:S(2)}, u32[]{:S(2)}) collective-permute-start(bf16[2,256,256]{2,1,0:T(8,128)(2,1)S(1)} %get-tuple-element.73.last_ref), channel_id=1, source_target_pairs={{0,8},{8,16},{16,24},{24,26},{26,18},{18,10},{10,2},{2,6},{6,14},{... | collective-permute-start | bytes 786440 | tf_op jit(solution)/shard_map/ppermute | solution.py:762
  43.5 7.2 %collective-permute-start.9 = (bf16[2,256,256]{2,1,0:T(8,128)(2,1)S(1)}, bf16[2,256,256]{2,1,0:T(8,128)(2,1)S(1)}, u32[]{:S(2)}, u32[]{:S(2)}) collective-permute-start(bf16[2,256,256]{2,1,0:T(8,128)(2,1)S(1)} %get-tuple-element.74.first_ref), channel_id=1, source_target_pairs={{0,4},{8,0},{16,8},{24,16},{26,24},{18,26},{10,18},{2,10},{6,2},{1... | collective-permute-start | bytes 786440 | tf_op jit(solution)/shard_map/ppermute | solution.py:762
  45.5 17.8 %copy-start = (bf16[2,1024,768]{2,1,0:T(8,128)(2,1)S(1)}, bf16[2,1024,768]{2,1,0:T(8,128)(2,1)}, u32[]{:S(2)}) copy-start(bf16[2,1024,768]{2,1,0:T(8,128)(2,1)} %get-tuple-element.91.spread_t_ref) | copy-start | bytes 9437188
  45.5 17.8 %copy-start.2 = (bf16[2,128,1024]{2,1,0:T(8,128)(2,1)S(1)}, bf16[2,128,1024]{2,1,0:T(8,128)(2,1)}, u32[]{:S(2)}) copy-start(bf16[2,128,1024]{2,1,0:T(8,128)(2,1)} %get-tuple-element.81.partner_ref) | copy-start | bytes 1572868
  66.7 23.7 %copy-start.1 = (bf16[512,2048]{1,0:T(8,128)(2,1)S(1)}, bf16[512,2048]{1,0:T(8,128)(2,1)}, u32[]{:S(2)}) copy-start(bf16[512,2048]{1,0:T(8,128)(2,1)} %get-tuple-element.61.home_ref) | copy-start | bytes 6291460
